TPU v7x, 32 devices: a whole 2x2x4 slice. The times are simulated.
32 devices in a mesh: frame: 2 (over x), brick: 16 (over z, y, core).
Axes of the slice: x: 2, y: 2, z: 4, core: 2. Of those that a mesh axis runs over, the one named last changes fastest.
Arguments:
- intensity: float32 [8, 256, 128], P('frame', 'brick'), may hold values from 0.1 to 10
- correction: float32 [8, 256, 128], P('frame', 'brick'), may hold values from 0.3 to 3
- splitting: bfloat16 [8, 16, 8, 128, 512], P('frame', 'brick'), may hold values from 0 to 0.015625
- block_count: int32 [8, 16], P('frame', 'brick'), may hold values from 1 to 8, 64 in all within a row
- pix_index: int32 [8, 16, 8], P('frame', 'brick'), may hold values from 0 to 255, as said below
- vox_offset: int32 [8, 16, 8], P('frame', 'brick'), may hold values from 0 to 33
Outputs:
- merged: float32 [16, 32, 512], P('brick', 'frame')
- weight: float32 [16, 32, 512], P('brick', 'frame')
Inputs may be any that keep to these rules, and one draw needn't show every extreme that they name: `block_count`: each frame's counts over the bricks sum to 64, and some pair of the frame holds 8. `pix_index`: the 32 slots of one device (its frames, its brick, padded slots included) include at most 4 slots (counted with repeats, over all of the device's frames) whose pixel block lies in the range 16 * c to 16 * c + 15, for every c; on every device some c has exactly 4 such slots.
All inputs are finite; a program needn't handle non-finite values. No bound on the sum of `block_count` on one device may be relied on, other than what follows from the above.
Results may differ from a plain program's by a relative error of at most 0.00049.
Values may be sent and summed in bfloat16 or wider, within the bound.
No kernel may reach another device: no remote copies, remote signals or barrier semaphores. Data moves between devices by JAX's collectives and lax.ppermute only.
A program may use at most 64 MiB of HBM per device.

v0:
```python
import jax
import jax.numpy as jnp
from jax import lax
from jax.sharding import PartitionSpec as P

BLK_DEV = 16


def extended(block, sides, width):
    for axis, dim in sides:
        count = lax.axis_size(axis)
        forward = [(i, i + 1) for i in range(count - 1)]
        backward = [(target, source) for source, target in forward]
        low = lax.ppermute(
            lax.slice_in_dim(block, block.shape[dim] - width, None, axis=dim), axis, forward
        )
        high = lax.ppermute(lax.slice_in_dim(block, 0, width, axis=dim), axis, backward)
        block = jnp.concatenate([low, block, high], axis=dim)
    return block


def on_device(intensity, correction, splitting, block_count, pix_index, vox_offset):
    frames_dev, blocks_per_device, pixel_width = intensity.shape
    max_slots = splitting.shape[2]
    voxels = splitting.shape[4]
    bricks = lax.axis_size("brick")
    groups = lax.axis_size("frame")
    block_rows = BLK_DEV * groups
    slot_count = frames_dev * max_slots
    local_rows = jnp.stack([intensity, correction], axis=2).astype(jnp.bfloat16)
    indices = pix_index.reshape(slot_count)
    frame_slot = jnp.arange(slot_count, dtype=jnp.int32) // max_slots
    gathered = lax.all_gather(local_rows, "brick", axis=1, tiled=True)
    flat_rows = gathered.reshape(frames_dev * blocks_per_device * bricks, 2, pixel_width)
    rows_per_slot = flat_rows[frame_slot * (blocks_per_device * bricks) + indices]
    divided_blocks = splitting.reshape(slot_count, pixel_width, voxels)
    contrib = jnp.einsum(
        "edb,eba->eda", rows_per_slot, divided_blocks, preferred_element_type=jnp.float32
    )
    flat_contrib = contrib.reshape(slot_count, 2 * voxels)
    live_slots = (jnp.arange(max_slots, dtype=jnp.int32)[None, :] < block_count).reshape(slot_count)
    offsets = vox_offset.reshape(slot_count)
    edge_ids = jnp.array([0, block_rows + 1], dtype=jnp.int32)[:, None]
    edge_place = ((offsets[None, :] == edge_ids) & live_slots[None, :]).astype(jnp.float32)
    overhang = jnp.dot(
        edge_place,
        flat_contrib,
        precision=lax.Precision.HIGHEST,
        preferred_element_type=jnp.float32,
    ).reshape(2, 2, voxels)
    neighbours = extended(overhang, (("brick", 0),), 1)
    lower_add = neighbours[0]
    upper_increment = neighbours[3]
    row_ids = jnp.arange(1, block_rows + 1, dtype=jnp.int32)[:, None]
    placement = ((offsets[None, :] == row_ids) & live_slots[None, :]).astype(jnp.float32)
    interior = jnp.dot(
        placement, flat_contrib, precision=lax.Precision.HIGHEST, preferred_element_type=jnp.float32
    )
    interior = interior.reshape(block_rows, 2, voxels)
    interior = interior.at[0].add(lower_add).at[block_rows - 1].add(upper_increment)
    reduced = lax.psum_scatter(interior, "frame", scatter_dimension=0, tiled=True)
    weight = reduced[:, 1]
    merged = reduced[:, 0] / jnp.maximum(weight, 1.0)
    return (merged[None], weight[None])


def solution(mesh):
    placed = (
        P("frame", "brick", None),
        P("frame", "brick", None),
        P("frame", "brick", None, None, None),
        P("frame", "brick"),
        P("frame", "brick", None),
        P("frame", "brick", None),
    )
    return jax.shard_map(
        on_device,
        mesh=mesh,
        in_specs=placed,
        out_specs=(P("brick", "frame", None), P("brick", "frame", None)),
        check_vma=False,
    )
```

profile of v0, /device:TPU:0, one launch (start us, length us, event | category | flops | bytes accessed | tf_op | source)
XLA Modules:
  0.0 63.6 jit_solution(8194101526361641025)
XLA Ops:
  7.2 0.0 copy-start.1
  7.2 0.0 copy-start.2
  7.2 0.0 reduce-scatter.2.cloned.1.call-start
  7.2 0.8 %convert_bitcast_fusion = (bf16[4,16,1,128]{3,1,0,2:T(8,128)(2,1)S(1)}, bf16[4,16,1,128]{3,1,0,2:T(8,128)(2,1)S(1)}) fusion(f32[4,16,128]{2,1,0:T(8,128)} %param.12, f32[4,16,128]{2,1,0:T(8,128)} %param.11), kind=kLoop, calls=%fused_computation.8 | loop fusion | flops 16384 | bytes 98304 | tf_op jit(solution)/shard_map/stack | solution.py:30
  8.0 24.6 %all_gather.3 = bf16[4,256,2,128]{3,1,0,2:T(8,128)(2,1)S(1)} all-gather(bf16[4,16,2,128]{3,1,0,2:T(8,128)(2,1)S(1)} %pad_maximum_fusion), channel_id=1, replica_groups=mesh['frame'=2,'brick'=16] {'brick'}, dimensions={1}, use_global_device_ids=true | all-gather | bytes 557056 | tf_op jit(solution)/shard_map/all_gather | solution.py:33
  32.6 0.5 copy.9
  33.2 0.5 broadcast.132
  33.7 1.3 %reduce.10 = s32[4,8]{1,0:T(4,128)S(1)} reduce(s32[4,1,8]{2,1,0:T(1,128)} %param.15, s32[]{:T(128)} %broadcast.132), dimensions={1}, to_apply=%param.15.reduce_sub_computation.3 | reduce | bytes 260 | tf_op args[4]
  35.0 0.1 reshape.176
  35.1 0.6 gather_fusion
  35.7 2.8 %fusion.20 = f32[32,2,512]{2,1,0:T(2,128)S(1)} fusion(bf16[32,2,128]{2,1,0:T(2,128)(2,1)S(1)} %gather_fusion, bf16[32,128,512]{2,1,0:T(8,128)(2,1)} %bitcast.35), kind=kOutput, calls=%fused_computation.38 | convolution fusion | flops 8388608 | bytes 4341760 | tf_op jit(solution)/shard_map/edb,eba->eda/dot_general | solution.py:37
  38.6 0.0 copy-done.1
  38.6 0.7 %reduce.11 = s32[4,8]{1,0:T(4,128)S(1)} reduce(s32[4,1,8]{2,1,0:T(1,128)S(1)} %copy-done.1, s32[]{:T(128)} %broadcast.132), dimensions={1}, to_apply=%param.16.reduce_sub_computation.3 | reduce | bytes 260 | tf_op args[5]
  39.3 0.1 eq.28
  39.4 0.0 copy-done.2
  39.4 0.1 iota_compare_fusion
  39.4 0.1 lt.37
  39.5 0.2 fusion.10
  39.8 2.3 %collective-permute-start = (f32[1,2,512]{2,0,1:T(1,128)S(1)}, f32[1,2,512]{2,0,1:T(1,128)S(1)}, u32[]{:S(2)}, u32[]{:S(2)}) collective-permute-start(f32[1,2,512]{2,0,1:T(1,128)S(1)} %bitcast.41), channel_id=1, source_target_pairs={{0,1},{1,2},{2,3},{3,4},{4,5},{5,6},{6,7},{7,8},{8,9},{9,10},{10,1... | collective-permute-start | bytes 12296 | tf_op jit(solution)/shard_map/ppermute | solution.py:14
  42.0 1.3 %collective-permute-start.1 = (f32[1,2,512]{2,0,1:T(1,128)S(1)}, f32[1,2,512]{2,0,1:T(1,128)S(1)}, u32[]{:S(2)}, u32[]{:S(2)}) collective-permute-start(f32[1,2,512]{2,0,1:T(1,128)S(1)} %bitcast.40), channel_id=1, source_target_pairs={{1,0},{2,1},{3,2},{4,3},{5,4},{6,5},{7,6},{8,7},{9,8},{10,9},{11,1... | collective-permute-start | bytes 12296 | tf_op jit(solution)/shard_map/ppermute | solution.py:17
  43.3 0.3 fusion
  43.6 0.0 collective-permute-done
  43.6 0.1 scatter-add.6
  43.7 1.4 %collective-permute-done.1 = f32[1,2,512]{2,0,1:T(1,128)S(1)} collective-permute-done((f32[1,2,512]{2,0,1:T(1,128)S(1)}, f32[1,2,512]{2,0,1:T(1,128)S(1)}, u32[]{:S(2)}, u32[]{:S(2)}) %collective-permute-start.1) | collective-permute-done | bytes 4128 | tf_op jit(solution)/shard_map/ppermute | solution.py:17
  45.1 0.1 scatter-add.9
  45.2 0.0 copy-start
  45.2 0.6 copy-done
  45.8 0.0 reduce-scatter.2.cloned.1.call-update
  45.8 9.5 %reduce-scatter.2.cloned.1.call-done = f32[16,2,512]{2,0,1:T(8,128)} async-done(((f32[32,2,512]{2,0,1:T(8,128)}), f32[16,2,512]{2,0,1:T(8,128)}) %reduce-scatter.2.cloned.1.call-update) | async-done | bytes 65552 | tf_op jit(solution)/shard_map/reduce_scatter | solution.py:61
  55.3 1.4 %fusion.3 = (f32[1,16,512]{2,1,0:T(8,128)}, f32[1,16,512]{2,1,0:T(8,128)}) fusion(f32[16,2,512]{2,0,1:T(8,128)} %reduce-scatter.2.cloned.1.call-done), kind=kLoop, calls=%fused_computation.6 | loop fusion | flops 16384 | bytes 131072 | tf_op jit(solution)/shard_map/div | solution.py:63
  (9 shorter events, 0.1 us)
Async XLA Ops:
  7.2 31.4 %copy-start.1 = (s32[4,1,8]{2,1,0:T(1,128)S(1)}, s32[4,1,8]{2,1,0:T(1,128)}, u32[]{:S(2)}) copy-start(s32[4,1,8]{2,1,0:T(1,128)} %param.16) | copy-start | bytes 388
  7.2 32.2 %copy-start.2 = (s32[4,1]{0,1:T(1,128)S(1)}, s32[4,1]{0,1:T(1,128)}, u32[]{:S(2)}) copy-start(s32[4,1]{0,1:T(1,128)} %param.14) | copy-start | bytes 52
  7.2 48.2 %reduce-scatter.2.cloned.1.call-start = ((), (), s32[]{:S(2)}) async-start(), calls=%async_computation.1 | async-start | bytes 196608 | tf_op jit(solution)/shard_map/reduce_scatter | solution.py:61
  39.8 3.8 %collective-permute-start = (f32[1,2,512]{2,0,1:T(1,128)S(1)}, f32[1,2,512]{2,0,1:T(1,128)S(1)}, u32[]{:S(2)}, u32[]{:S(2)}) collective-permute-start(f32[1,2,512]{2,0,1:T(1,128)S(1)} %bitcast.41), channel_id=1, source_target_pairs={{0,1},{1,2},{2,3},{3,4},{4,5},{5,6},{6,7},{7,8},{8,9},{9,10},{10,1... | collective-permute-start | bytes 12296 | tf_op jit(solution)/shard_map/ppermute | solution.py:14
  42.0 3.1 %collective-permute-start.1 = (f32[1,2,512]{2,0,1:T(1,128)S(1)}, f32[1,2,512]{2,0,1:T(1,128)S(1)}, u32[]{:S(2)}, u32[]{:S(2)}) collective-permute-start(f32[1,2,512]{2,0,1:T(1,128)S(1)} %bitcast.40), channel_id=1, source_target_pairs={{1,0},{2,1},{3,2},{4,3},{5,4},{6,5},{7,6},{8,7},{9,8},{10,9},{11,1... | collective-permute-start | bytes 12296 | tf_op jit(solution)/shard_map/ppermute | solution.py:17
  45.2 0.6 copy-start
Sparse Core Ops, SparseCore 0:
  45.9 9.3 reduce-scatter.1
where the time goes:
time: 64 us; the launch traced here: 63.6 us
  blocking collectives  24.6 us (38%)
  between operations  14.2 us (22%)
  waiting for transfers between devices  10.9 us (17%)
  other arithmetic  4.32 us (7%)
  starting transfers between devices  3.58 us (6%)
  matrix products  3.29 us (5%)
  local copies, waits for them, and re-layouts  2.73 us (4%)
    all_gather x1, blocking collectives, on_device(): gathered = lax.all_gather(local_rows, 'brick', axis=1, tiled=True)  24.6 us
    reduce_scatter x1, waiting for transfers between devices, on_device(): lax.psum_scatter(interior, 'frame', scatter_dimension=0, tiled=True)  9.51 us
    dot_general x1, matrix products, on_device(): jnp.einsum('edb,eba->eda', rows_per_slot, divided_blocks, preferred_eleme...  2.83 us
    ppermute x1, starting transfers between devices, extended(): lax.ppermute(lax.slice_in_dim(block, block.shape[dim] - width, None, axis...  2.25 us
    unnamed x2, other arithmetic  2.01 us
    div x1, other arithmetic, on_device(): merged = reduced[:, 0] / jnp.maximum(weight, 1.0)  1.4 us
    ppermute x1, waiting for transfers between devices, extended(): lax.ppermute(lax.slice_in_dim(block, 0, width, axis=dim), axis, backward)  1.39 us
    ppermute x1, starting transfers between devices, extended(): lax.ppermute(lax.slice_in_dim(block, 0, width, axis=dim), axis, backward)  1.29 us
  transfers between devices with their start and end apart: 3, of which 2 were waited for; matrix products, arithmetic and copies ran while one was open for 1% of the time, Pallas kernels for 0%

commit v1 on v0

v1 whole, which is shorter than its diff:
```python
import functools

import jax
import jax.numpy as jnp
from jax import lax
from jax.experimental import pallas as pl
from jax.experimental.pallas import tpu as pltpu
from jax.sharding import PartitionSpec as P

BLK_DEV = 16
CHANNELS = 2
BLOCK_ROWS = CHANNELS * BLK_DEV + 8


def stages_of(bricks):
    if bricks == 16:
        return ((8,), (6, 2, 4), (1,))
    rounds, distance = [], bricks // 2
    while distance:
        rounds.append((distance,))
        distance //= 2
    return tuple(rounds)


def gather_rows(rows, bricks):
    held, distances = rows[None], [0]
    for exchange in stages_of(bricks):
        arrived = {
            step: lax.ppermute(held, "brick", [(i, i ^ step) for i in range(bricks)]) for step in exchange
        }
        order = sorted(arrived)
        held = jnp.concatenate([held] + [arrived[step] for step in order], axis=0)
        distances = distances + [d ^ step for step in order for d in distances]
    return held, distances


def place_of(distance, distances):
    place, bit = jnp.zeros_like(distance), 1
    while bit < len(distances):
        place = place + jnp.where((distance & bit) != 0, distances.index(bit), 0)
        bit *= 2
    return place


def split_kernel(frames, slots, groups, held_ref, meta_ref, split_ref, *refs):
    outs, placed_ref = refs[:groups], refs[groups]
    bricks, per_brick, pixels = held_ref.shape
    per_frame = per_brick // frames
    reach = bricks * per_frame
    pair = CHANNELS * slots
    sub = lax.broadcasted_iota(jnp.int32, (BLK_DEV, pixels), 0)
    lane = lax.broadcasted_iota(jnp.int32, (pair, pixels), 1)
    zero = jnp.zeros((BLK_DEV, pixels), jnp.float32)
    for frame in range(frames):
        target = meta_ref[pl.ds(frame * pair, pair), :]
        chosen = jnp.concatenate(
            [(target == lane + start).astype(jnp.float32) for start in range(0, reach, pixels)], axis=1
        ).astype(jnp.bfloat16)
        own = held_ref[:, pl.ds(frame * per_frame, per_frame), :].reshape(reach, pixels)
        picked = jnp.dot(chosen, own, preferred_element_type=jnp.float32)
        goal = meta_ref[pl.ds((frames + frame) * pair, pair), :]
        for slot in range(slots):
            first, second = CHANNELS * slot, CHANNELS * slot + 1
            value_0 = jnp.broadcast_to(picked[first : first + 1], sub.shape)
            value_1 = jnp.broadcast_to(picked[second : second + 1], sub.shape)
            goal_0 = jnp.broadcast_to(goal[first : first + 1], sub.shape)
            goal_1 = jnp.broadcast_to(goal[second : second + 1], sub.shape)
            parts = []
            for block in range(groups):
                base = block * BLOCK_ROWS
                parts.append(jnp.where(sub + base == goal_0, value_0, zero))
                parts.append(jnp.where(sub + (base + BLK_DEV) == goal_1, value_1, zero))
                edge = sub[:8] + (base + 2 * BLK_DEV)
                parts.append(
                    jnp.where(
                        edge == goal_0[:8], value_0[:8], jnp.where(edge == goal_1[:8], value_1[:8], zero[:8])
                    )
                )
            place = (frame * slots + slot) * pixels
            placed_ref[:, pl.ds(place, pixels)] = jnp.concatenate(parts, axis=0).astype(jnp.bfloat16)
    total = jnp.dot(placed_ref[...], split_ref[...], preferred_element_type=jnp.float32)
    for block in range(groups):
        outs[block][...] = total[block * BLOCK_ROWS : (block + 1) * BLOCK_ROWS]


def on_device(intensity, correction, splitting, block_count, pix_index, vox_offset):
    frames_dev, blocks_per_device, pixel_width = intensity.shape
    max_slots = splitting.shape[2]
    voxels = splitting.shape[4]
    bricks = lax.axis_size("brick")
    groups = lax.axis_size("frame")
    brick, group = lax.axis_index("brick"), lax.axis_index("frame")
    top = groups - 1
    block_rows = BLK_DEV * groups
    slot_count = frames_dev * max_slots

    local_rows = jnp.stack([intensity, correction], axis=2).astype(jnp.bfloat16)
    local_rows = local_rows.reshape(frames_dev * blocks_per_device * CHANNELS, pixel_width)
    held, distances = gather_rows(local_rows, bricks)

    channel = jnp.arange(CHANNELS, dtype=jnp.int32)
    indices = pix_index.reshape(slot_count)
    place = place_of((indices // blocks_per_device) ^ brick, distances)
    target = (place * blocks_per_device + indices % blocks_per_device)[:, None] * CHANNELS + channel
    offsets = vox_offset.reshape(slot_count)
    live = (jnp.arange(max_slots, dtype=jnp.int32)[None, :] < block_count).reshape(slot_count)
    low, high = offsets == 0, offsets == block_rows + 1
    live = live & ~(low & (brick == 0)) & ~(high & (brick == bricks - 1))
    owner = jnp.where(low, top, jnp.where(high, 0, (offsets - 1) // BLK_DEV))
    base = ((owner - group + groups) % groups) * BLOCK_ROWS
    inside = (offsets - 1) % BLK_DEV
    goal = jnp.where(
        (low | high)[:, None],
        CHANNELS * BLK_DEV + channel,
        inside[:, None] + BLK_DEV * channel,
    )
    goal = jnp.where(live[:, None], base[:, None] + goal, -1)
    meta = jnp.concatenate([target.reshape(-1), goal.reshape(-1)])
    meta = jnp.broadcast_to(meta[:, None], (2 * slot_count * CHANNELS, pixel_width))

    in_vmem = pl.BlockSpec(memory_space=pltpu.VMEM)
    blocks = pl.pallas_call(
        functools.partial(split_kernel, frames_dev, max_slots, groups),
        out_shape=[jax.ShapeDtypeStruct((BLOCK_ROWS, voxels), jnp.float32)] * groups,
        in_specs=[in_vmem] * 3,
        out_specs=[in_vmem] * groups,
        scratch_shapes=[pltpu.VMEM((groups * BLOCK_ROWS, slot_count * pixel_width), jnp.bfloat16)],
        compiler_params=pltpu.CompilerParams(vmem_limit_bytes=24 * 1024 * 1024),
        cost_estimate=pl.CostEstimate(
            flops=2 * groups * BLOCK_ROWS * slot_count * pixel_width * voxels,
            bytes_accessed=2 * slot_count * pixel_width * voxels,
            transcendentals=0,
        ),
        name="split_and_place",
    )(held, meta, splitting.reshape(slot_count * pixel_width, voxels))

    received = [
        lax.ppermute(blocks[step], "frame", [(i, (i + step) % groups) for i in range(groups)])
        for step in range(1, groups)
    ]
    edge = slice(CHANNELS * BLK_DEV, CHANNELS * BLK_DEV + CHANNELS)
    overhang = sum([part[edge] for part in received], blocks[0][edge])
    turn = [(i, i) for i in range(bricks, top * bricks)]
    for i in range(bricks):
        turn.append((i, i + 1 if i + 1 < bricks else top * bricks + i))
        turn.append((top * bricks + i, top * bricks + i - 1 if i else 0))
    handed = lax.ppermute(overhang, ("frame", "brick"), turn)
    interior = slice(0, CHANNELS * BLK_DEV)
    total = sum([part[interior] for part in received], blocks[0][interior])
    total = total.reshape(CHANNELS, BLK_DEV, voxels)
    row = jnp.where(group == 0, 0, jnp.where(group == top, BLK_DEV - 1, -1))
    here = jnp.arange(BLK_DEV, dtype=jnp.int32)[None, :, None] == row
    total = total + jnp.where(here, handed[:, None, :], 0.0)
    weight = total[1]
    merged = total[0] / jnp.maximum(weight, 1.0)
    return (merged[None], weight[None])


def solution(mesh):
    placed = (
        P("frame", "brick", None),
        P("frame", "brick", None),
        P("frame", "brick", None, None, None),
        P("frame", "brick"),
        P("frame", "brick", None),
        P("frame", "brick", None),
    )
    return jax.shard_map(
        on_device,
        mesh=mesh,
        in_specs=placed,
        out_specs=(P("brick", "frame", None), P("brick", "frame", None)),
        check_vma=False,
    )
```

time: 64 us -> 32.7 us (0.51)
  blocking collectives: 24.6 us -> 0 us
  between operations: 14.2 us -> 0.77 us
  starting transfers between devices: 3.58 us -> 9.28 us
  matrix products: 3.29 us -> 0 us
  waiting for transfers between devices: 10.9 us -> 12.5 us
  Pallas kernels: 0 us -> 0.97 us
  other arithmetic: 4.32 us -> 5.29 us
  local copies, waits for them, and re-layouts: 2.73 us -> 3.58 us
    all_gather x1 -> x0, blocking collectives: 24.6 us -> none  [on_device(): gathered = lax.all_gather(local_rows, 'brick', axis=1, tiled=True)]
    ppermute x2 -> x7, waiting for transfers between devices: 1.39 us -> 12.5 us  [the longest x5 5.95 us: gather_rows(): lax.ppermute(held, 'brick', [(i, i ^ step) for i in range(bricks)])]
    reduce_scatter x1 -> x0, waiting for transfers between devices: 9.51 us -> none  [on_device(): lax.psum_scatter(interior, 'frame', scatter_dimension=0, tiled=True)]
    ppermute x2 -> x7, starting transfers between devices: 3.54 us -> 9.28 us  [the longest x5 7.73 us: gather_rows(): lax.ppermute(held, 'brick', [(i, i ^ step) for i in range(bricks)])]
    dot_general x3 -> x0, matrix products: 3.29 us -> none  [the longest x1 2.83 us: on_device(): jnp.einsum('edb,eba->eda', rows_per_slot, divided_blocks, preferred_eleme...]
    unnamed x8 -> x7, local copies, waits for them, and re-layouts: 1.18 us -> 2.78 us
    pallas_call x0 -> x1, Pallas kernels: none -> 0.97 us  [on_device(): pl.pallas_call(functools.partial(split_kernel, frames_dev, max_slots, gro...]
    div x1, other arithmetic: 1.4 us -> 0.63 us  [on_device(): merged = total[0] / jnp.maximum(weight, 1.0)]
  transfers between devices with their start and end apart: 3 -> 7, of which waited for: 2 -> 6; matrix products, arithmetic and copies ran while one was open for 1% -> 15% of each run, Pallas kernels for 0% -> 0%
where the time goes in v1:
time: 32.7 us; the launch traced here: 32.4 us
  waiting for transfers between devices  12.5 us (38%)
  starting transfers between devices  9.28 us (28%)
  other arithmetic  5.29 us (16%)
  local copies, waits for them, and re-layouts  3.58 us (11%)
  Pallas kernels  0.97 us (3%)
  between operations  0.77 us (2%)
    ppermute x5, starting transfers between devices, gather_rows(): lax.ppermute(held, 'brick', [(i, i ^ step) for i in range(bricks)])  7.73 us
    ppermute x5, waiting for transfers between devices, gather_rows(): lax.ppermute(held, 'brick', [(i, i ^ step) for i in range(bricks)])  5.95 us
    ppermute x1, waiting for transfers between devices, on_device(): handed = lax.ppermute(overhang, ('frame', 'brick'), turn)  3.58 us
    ppermute x1, waiting for transfers between devices, on_device(): lax.ppermute(blocks[step], 'frame', [(i, (i + step) % groups) for i in ra...  2.99 us
    unnamed x7, local copies, waits for them, and re-layouts  2.78 us
    ppermute x1, starting transfers between devices, on_device(): lax.ppermute(blocks[step], 'frame', [(i, (i + step) % groups) for i in ra...  1.55 us
    unnamed x1, other arithmetic  1.34 us
    pallas_call x1, Pallas kernels, on_device(): pl.pallas_call(functools.partial(split_kernel, frames_dev, max_slots, gro...  0.97 us
  transfers between devices with their start and end apart: 7, of which 6 were waited for; matrix products, arithmetic and copies ran while one was open for 15% of the time, Pallas kernels for 0%

profile of v1, /device:TPU:0, one launch (start us, length us, event | category | flops | bytes accessed | tf_op | source)
XLA Modules:
  0.0 32.4 jit_solution(11359124799536607049)
XLA Ops:
  0.6 0.8 %convert_bitcast_fusion = (bf16[4,16,1,128]{3,1,0,2:T(8,128)(2,1)S(1)}, bf16[4,16,1,128]{3,1,0,2:T(8,128)(2,1)S(1)}) fusion(f32[4,16,128]{2,1,0:T(8,128)} %param.7, f32[4,16,128]{2,1,0:T(8,128)} %param.6), kind=kLoop, calls=%fused_computation.18 | loop fusion | flops 16384 | bytes 98304 | tf_op jit(solution)/shard_map/stack | solution.py:97
  1.5 4.1 %collective-permute-start = (bf16[1,128,128]{2,1,0:T(8,128)(2,1)S(1)}, bf16[1,128,128]{2,1,0:T(8,128)(2,1)S(1)}, u32[]{:S(2)}, u32[]{:S(2)}) collective-permute-start(bf16[1,128,128]{2,1,0:T(8,128)(2,1)S(1)} %bitcast.9), channel_id=1, source_target_pairs={{0,8},{1,9},{2,10},{3,11},{4,12},{5,13},{6,14},{7,15},{8,0},{9,1},... | collective-permute-start | bytes 98312 | tf_op jit(solution)/shard_map/ppermute | solution.py:29
  5.6 0.7 %compare_reduce_fusion = (pred[4,8]{1,0:T(4,128)(4,1)S(1)}, pred[4,8]{1,0:T(4,128)(4,1)S(1)}) fusion(s32[4,1,8]{2,1,0:T(1,128)} %param.11), kind=kLoop, calls=%fused_computation.20 | loop fusion | flops 64 | bytes 192 | tf_op jit(solution)/shard_map/eq | solution.py:107
  6.3 0.7 %add_reduce_fusion = s32[4,8]{1,0:T(4,128)S(1)} fusion(s32[4,1,8]{2,1,0:T(1,128)} %param.11), kind=kLoop, calls=%fused_computation.25 | loop fusion | flops 32 | bytes 256 | tf_op jit(solution)/shard_map/sub | solution.py:109
  7.0 0.1 eq.63
  7.1 0.1 eq.67
  7.2 0.7 %iota_compare_fusion = pred[4,8]{1,0:T(4,128)(4,1)S(1)} fusion(s32[4]{0:T(128)} %bitcast.13), kind=kLoop, calls=%fused_computation.26 | loop fusion | flops 32 | bytes 48 | tf_op jit(solution)/shard_map/lt | solution.py:106
  7.9 0.1 lt.42
  8.0 0.1 sub.28
  8.1 0.5 %broadcast.346 = s32[]{:T(128)} broadcast(s32[]{:T(128)} %constant.70.clone.1), dimensions={} | broadcast | bytes 8 | tf_op args[4]
  8.6 1.3 %reduce.11 = s32[4,8]{1,0:T(4,128)S(1)} reduce(s32[4,1,8]{2,1,0:T(1,128)} %param.10, s32[]{:T(128)} %broadcast.346), dimensions={1}, to_apply=%param.10.reduce_sub_computation.3 | reduce | bytes 260 | tf_op args[4]
  9.9 0.1 reshape.214
  10.1 0.1 add_select_fusion
  10.2 0.1 select_n.126
  10.3 1.6 %collective-permute-start.1 = (bf16[2,128,128]{2,1,0:T(8,128)(2,1)S(1)}, bf16[2,128,128]{2,1,0:T(8,128)(2,1)S(1)}, u32[]{:S(2)}, u32[]{:S(2)}) collective-permute-start(bf16[2,128,128]{2,1,0:T(8,128)(2,1)S(1)} %pad_maximum_fusion), channel_id=1, source_target_pairs={{0,2},{1,3},{2,0},{3,1},{4,6},{5,7},{6,4},{7,5},{8,10},{9,11},{10,... | collective-permute-start | bytes 196616 | tf_op jit(solution)/shard_map/ppermute | solution.py:29
  11.9 1.6 %collective-permute-start.2 = (bf16[2,128,128]{2,1,0:T(8,128)(2,1)S(1)}, bf16[2,128,128]{2,1,0:T(8,128)(2,1)S(1)}, u32[]{:S(2)}, u32[]{:S(2)}) collective-permute-start(bf16[2,128,128]{2,1,0:T(8,128)(2,1)S(1)} %pad_maximum_fusion), channel_id=1, source_target_pairs={{0,4},{1,5},{2,6},{3,7},{4,0},{5,1},{6,2},{7,3},{8,12},{9,13},{10,... | collective-permute-start | bytes 196616 | tf_op jit(solution)/shard_map/ppermute | solution.py:29
  13.5 0.4 %collective-permute-start.3 = (bf16[2,128,128]{2,1,0:T(8,128)(2,1)S(1)}, bf16[2,128,128]{2,1,0:T(8,128)(2,1)S(1)}, u32[]{:S(2)}, u32[]{:S(2)}) collective-permute-start(bf16[2,128,128]{2,1,0:T(8,128)(2,1)S(1)} %pad_maximum_fusion), channel_id=1, source_target_pairs={{0,6},{1,7},{2,4},{3,5},{4,2},{5,3},{6,0},{7,1},{8,14},{9,15},{10,... | collective-permute-start | bytes 196616 | tf_op jit(solution)/shard_map/ppermute | solution.py:29
  13.9 0.8 %collective-permute-done.1 = bf16[2,128,128]{2,1,0:T(8,128)(2,1)S(1)} collective-permute-done((bf16[2,128,128]{2,1,0:T(8,128)(2,1)S(1)}, bf16[2,128,128]{2,1,0:T(8,128)(2,1)S(1)}, u32[]{:S(2)}, u32[]{:S(2)}) %collective-permute-start.1) | collective-permute-done | bytes 65568 | tf_op jit(solution)/shard_map/ppermute | solution.py:29
  14.7 1.7 %collective-permute-done.2 = bf16[2,128,128]{2,1,0:T(8,128)(2,1)S(1)} collective-permute-done((bf16[2,128,128]{2,1,0:T(8,128)(2,1)S(1)}, bf16[2,128,128]{2,1,0:T(8,128)(2,1)S(1)}, u32[]{:S(2)}, u32[]{:S(2)}) %collective-permute-start.2) | collective-permute-done | bytes 65568 | tf_op jit(solution)/shard_map/ppermute | solution.py:29
  16.4 2.2 %collective-permute-done.3 = bf16[2,128,128]{2,1,0:T(8,128)(2,1)S(1)} collective-permute-done((bf16[2,128,128]{2,1,0:T(8,128)(2,1)S(1)}, bf16[2,128,128]{2,1,0:T(8,128)(2,1)S(1)}, u32[]{:S(2)}, u32[]{:S(2)}) %collective-permute-start.3) | collective-permute-done | bytes 65568 | tf_op jit(solution)/shard_map/ppermute | solution.py:29
  18.7 0.1 iota_add_fusion
  18.8 0.1 add.142
  18.9 0.1 pad_add_fusion
  19.0 1.3 %collective-permute-done.4 = bf16[8,128,128]{2,1,0:T(8,128)(2,1)S(1)} collective-permute-done((bf16[8,128,128]{2,1,0:T(8,128)(2,1)S(1)}, bf16[8,128,128]{2,1,0:T(8,128)(2,1)S(1)}, u32[]{:S(2)}, u32[]{:S(2)}) %collective-permute-start.4) | collective-permute-done | bytes 262176 | tf_op jit(solution)/shard_map/ppermute | solution.py:29
  20.3 0.1 broadcast_in_dim.81.meta_ref
  20.4 2.2 %copy-done = bf16[4,1,8,128,512]{4,3,2,1,0:T(8,128)(2,1)S(1)} copy-done((bf16[4,1,8,128,512]{4,3,2,1,0:T(8,128)(2,1)S(1)}, bf16[4,1,8,128,512]{4,3,2,1,0:T(8,128)(2,1)}, u32[]{:S(2)}) %copy-start) | copy-done | bytes 4194328
  22.6 1.0 %split_and_place.1 = (f32[40,512]{1,0:T(8,128)S(1)}, f32[40,512]{1,0:T(8,128)S(1)}) custom-call(bf16[16,128,128]{2,1,0:T(8,128)(2,1)S(1)} %constant_dynamic-update-slice_fusion.5.held_ref, s32[128,128]{1,0:T(8,128)S(1)} %broadcast_in_dim.81.meta_ref, bf16[4096,512]{1,0:T(8,128)(2,1)S(1)} %bitcast.8), custom_call_target="tpu_custom_call" | custom-call | flops 335544320 | bytes 4194304 | tf_op jit(solution)/shard_map/split_and_place/pallas_call | solution.py:122
  23.5 1.6 %collective-permute-start.5 = (f32[40,512]{1,0:T(8,128)S(1)}, f32[40,512]{1,0:T(8,128)S(1)}, u32[]{:S(2)}, u32[]{:S(2)}) collective-permute-start(f32[40,512]{1,0:T(8,128)S(1)} %get-tuple-element.5), channel_id=1, source_target_pairs={{0,16},{16,0},{1,17},{17,1},{2,18},{18,2},{3,19},{19,3},{4,20},{20... | collective-permute-start | bytes 245768 | tf_op jit(solution)/shard_map/ppermute | solution.py:138
  25.1 3.0 %collective-permute-done.5 = f32[40,512]{1,0:T(8,128)S(1)} collective-permute-done((f32[40,512]{1,0:T(8,128)S(1)}, f32[40,512]{1,0:T(8,128)S(1)}, u32[]{:S(2)}, u32[]{:S(2)}) %collective-permute-start.5) | collective-permute-done | bytes 81952 | tf_op jit(solution)/shard_map/ppermute | solution.py:138
  28.1 3.6 %collective-permute-done.6 = f32[2,512]{1,0:T(2,128)S(1)} collective-permute-done((f32[2,512]{1,0:T(2,128)S(1)}, f32[2,512]{1,0:T(2,128)S(1)}, u32[]{:S(2)}, u32[]{:S(2)}) %collective-permute-start.6) | collective-permute-done | bytes 4128 | tf_op jit(solution)/shard_map/ppermute | solution.py:147
  31.7 0.1 select_add_fusion
  31.8 0.6 %slice_divide_fusion = (f32[1,16,512]{2,1,0:T(8,128)}, f32[1,16,512]{2,1,0:T(8,128)}) fusion(f32[2,16,512]{2,1,0:T(8,128)S(1)} %select_add_fusion), kind=kLoop, calls=%fused_computation.3 | loop fusion | flops 16384 | bytes 131072 | tf_op jit(solution)/shard_map/div | solution.py:155
  (20 shorter events, 0.3 us)
Async XLA Ops:
  1.5 8.8 %collective-permute-start = (bf16[1,128,128]{2,1,0:T(8,128)(2,1)S(1)}, bf16[1,128,128]{2,1,0:T(8,128)(2,1)S(1)}, u32[]{:S(2)}, u32[]{:S(2)}) collective-permute-start(bf16[1,128,128]{2,1,0:T(8,128)(2,1)S(1)} %bitcast.9), channel_id=1, source_target_pairs={{0,8},{1,9},{2,10},{3,11},{4,12},{5,13},{6,14},{7,15},{8,0},{9,1},... | collective-permute-start | bytes 98312 | tf_op jit(solution)/shard_map/ppermute | solution.py:29
  10.3 4.3 %collective-permute-start.1 = (bf16[2,128,128]{2,1,0:T(8,128)(2,1)S(1)}, bf16[2,128,128]{2,1,0:T(8,128)(2,1)S(1)}, u32[]{:S(2)}, u32[]{:S(2)}) collective-permute-start(bf16[2,128,128]{2,1,0:T(8,128)(2,1)S(1)} %pad_maximum_fusion), channel_id=1, source_target_pairs={{0,2},{1,3},{2,0},{3,1},{4,6},{5,7},{6,4},{7,5},{8,10},{9,11},{10,... | collective-permute-start | bytes 196616 | tf_op jit(solution)/shard_map/ppermute | solution.py:29
  11.9 4.5 %collective-permute-start.2 = (bf16[2,128,128]{2,1,0:T(8,128)(2,1)S(1)}, bf16[2,128,128]{2,1,0:T(8,128)(2,1)S(1)}, u32[]{:S(2)}, u32[]{:S(2)}) collective-permute-start(bf16[2,128,128]{2,1,0:T(8,128)(2,1)S(1)} %pad_maximum_fusion), channel_id=1, source_target_pairs={{0,4},{1,5},{2,6},{3,7},{4,0},{5,1},{6,2},{7,3},{8,12},{9,13},{10,... | collective-permute-start | bytes 196616 | tf_op jit(solution)/shard_map/ppermute | solution.py:29
  13.5 5.2 %collective-permute-start.3 = (bf16[2,128,128]{2,1,0:T(8,128)(2,1)S(1)}, bf16[2,128,128]{2,1,0:T(8,128)(2,1)S(1)}, u32[]{:S(2)}, u32[]{:S(2)}) collective-permute-start(bf16[2,128,128]{2,1,0:T(8,128)(2,1)S(1)} %pad_maximum_fusion), channel_id=1, source_target_pairs={{0,6},{1,7},{2,4},{3,5},{4,2},{5,3},{6,0},{7,1},{8,14},{9,15},{10,... | collective-permute-start | bytes 196616 | tf_op jit(solution)/shard_map/ppermute | solution.py:29
  18.7 1.6 %collective-permute-start.4 = (bf16[8,128,128]{2,1,0:T(8,128)(2,1)S(1)}, bf16[8,128,128]{2,1,0:T(8,128)(2,1)S(1)}, u32[]{:S(2)}, u32[]{:S(2)}) collective-permute-start(bf16[8,128,128]{2,1,0:T(8,128)(2,1)S(1)} %get-tuple-element.10), channel_id=1, source_target_pairs={{0,1},{1,0},{2,3},{3,2},{4,5},{5,4},{6,7},{7,6},{8,9},{9,8},{10,11... | collective-permute-start | bytes 786440 | tf_op jit(solution)/shard_map/ppermute | solution.py:29
  20.4 2.2 %copy-start = (bf16[4,1,8,128,512]{4,3,2,1,0:T(8,128)(2,1)S(1)}, bf16[4,1,8,128,512]{4,3,2,1,0:T(8,128)(2,1)}, u32[]{:S(2)}) copy-start(bf16[4,1,8,128,512]{4,3,2,1,0:T(8,128)(2,1)} %param.8) | copy-start | bytes 12582916
  23.5 4.5 %collective-permute-start.5 = (f32[40,512]{1,0:T(8,128)S(1)}, f32[40,512]{1,0:T(8,128)S(1)}, u32[]{:S(2)}, u32[]{:S(2)}) collective-permute-start(f32[40,512]{1,0:T(8,128)S(1)} %get-tuple-element.5), channel_id=1, source_target_pairs={{0,16},{16,0},{1,17},{17,1},{2,18},{18,2},{3,19},{19,3},{4,20},{20... | collective-permute-start | bytes 245768 | tf_op jit(solution)/shard_map/ppermute | solution.py:138
  28.1 3.6 %collective-permute-start.6 = (f32[2,512]{1,0:T(2,128)S(1)}, f32[2,512]{1,0:T(2,128)S(1)}, u32[]{:S(2)}, u32[]{:S(2)}) collective-permute-start(f32[2,512]{1,0:T(2,128)S(1)} %slice_add_fusion.1), channel_id=1, source_target_pairs={{0,1},{16,0},{1,2},{17,16},{2,3},{18,17},{3,4},{19,18},{4,5},{20,1... | collective-permute-start | bytes 12296 | tf_op jit(solution)/shard_map/ppermute | solution.py:147

commit v2 on v1

v2 whole, which is shorter than its diff:
```python
import functools

import jax
import jax.numpy as jnp
from jax import lax
from jax.experimental import pallas as pl
from jax.experimental.pallas import tpu as pltpu
from jax.sharding import PartitionSpec as P

BLK_DEV = 16
CHANNELS = 2
VMEM_LIMIT = 8 * 1024 * 1024
BLOCK_ROWS = CHANNELS * BLK_DEV + 8


def stages_of(bricks):
    if bricks == 16:
        return ((8,), (6, 2, 4), (1,))
    rounds, distance = [], bricks // 2
    while distance:
        rounds.append((distance,))
        distance //= 2
    return tuple(rounds)


def join_kernel(*refs):
    out_ref, at = refs[-1], 0
    for ref in refs[:-2]:
        out_ref[pl.ds(at, ref.shape[0])] = ref[...]
        at += ref.shape[0]


def join(parts, after):
    in_vmem = pl.BlockSpec(memory_space=pltpu.VMEM)
    count = sum(part.shape[0] for part in parts)
    return pl.pallas_call(
        join_kernel,
        out_shape=jax.ShapeDtypeStruct((count,) + parts[0].shape[1:], parts[0].dtype),
        in_specs=[in_vmem] * (len(parts) + 1),
        out_specs=in_vmem,
        compiler_params=pltpu.CompilerParams(vmem_limit_bytes=VMEM_LIMIT),
        name="join_rows",
    )(*parts, after)


def gather_rows(rows, bricks, beside):
    stages = stages_of(bricks)
    held, distances, made = rows[None], [0], None
    for exchange in stages:
        distances = distances + [d ^ step for step in sorted(exchange) for d in distances]
    for at, exchange in enumerate(stages):
        arrived = {
            step: lax.ppermute(held, "brick", [(i, i ^ step) for i in range(bricks)]) for step in exchange
        }
        parts = [held] + [arrived[step] for step in sorted(arrived)]
        if at == len(stages) - 2:
            made = beside(held, distances)
            held = join(parts, made)
        elif at < len(stages) - 1:
            held = jnp.concatenate(parts, axis=0)
    return parts, distances, made


def place_of(distance, distances):
    place, bit = 0, 1
    while bit < len(distances):
        place = place + jnp.where((distance & bit) != 0, distances.index(bit), 0)
        bit *= 2
    return place


def prepare_kernel(
    distances, per_owner, block_rows, bricks, groups, slots, index_ref, after_ref, split_ref, meta_ref
):
    brick, group = lax.axis_index("brick"), lax.axis_index("frame")
    frames = index_ref.shape[0] // 3
    wide = (slots * CHANNELS, meta_ref.shape[1])
    row = lax.broadcasted_iota(jnp.int32, wide, 0)
    channel = row % CHANNELS
    mine = lax.broadcasted_iota(jnp.int32, wide, 1) == row // CHANNELS

    def of_slot(at):
        line = jnp.broadcast_to(index_ref[pl.ds(at, 1), :], wide)
        return jnp.sum(jnp.where(mine, line, 0), axis=1, keepdims=True) + jnp.zeros(wide, jnp.int32)

    for frame in range(frames):
        pixel_block = of_slot(frame)
        owner = pixel_block // per_owner
        place = place_of(owner ^ brick, distances)
        target = (place * CHANNELS + channel) * per_owner + (pixel_block - owner * per_owner)
        meta_ref[pl.ds(frame * wide[0], wide[0]), :] = target
        offset = of_slot(frames + frame)
        low, high = offset == 0, offset == block_rows + 1
        holder = jnp.where(low, groups - 1, jnp.where(high, 0, (offset - 1) // BLK_DEV))
        step = holder - group
        step = jnp.where(step < 0, step + groups, step)
        inside = offset - 1 - holder * BLK_DEV + BLK_DEV * channel
        goal = step * BLOCK_ROWS + jnp.where(low | high, CHANNELS * BLK_DEV + channel, inside)
        live = row // CHANNELS < of_slot(2 * frames + frame)
        live = live & ~(low & (brick == 0)) & ~(high & (brick == bricks - 1))
        meta_ref[pl.ds((frames + frame) * wide[0], wide[0]), :] = jnp.where(live, goal, -1)


def split_kernel(frames, slots, groups, near_ref, far_ref, meta_ref, split_ref, *refs):
    outs, placed_ref = refs[:groups], refs[groups]
    half, per_brick, pixels = near_ref.shape
    per_owner = per_brick // (CHANNELS * frames)
    reach = 2 * half * CHANNELS * per_owner
    pair = CHANNELS * slots
    sub = lax.broadcasted_iota(jnp.int32, (BLK_DEV, pixels), 0)
    lane = lax.broadcasted_iota(jnp.int32, (pair, pixels), 1)
    zero = jnp.zeros((BLK_DEV, pixels), jnp.float32)
    for frame in range(frames):
        target = meta_ref[pl.ds(frame * pair, pair), :]
        chosen = jnp.concatenate(
            [(target == lane + start).astype(jnp.float32) for start in range(0, reach, pixels)], axis=1
        ).astype(jnp.bfloat16)
        own = jnp.concatenate(
            [
                jnp.concatenate(
                    [ref[:, pl.ds((c * frames + frame) * per_owner, per_owner), :] for c in range(CHANNELS)],
                    axis=1,
                ).reshape(reach // 2, pixels)
                for ref in (near_ref, far_ref)
            ],
            axis=0,
        )
        picked = jnp.dot(chosen, own, preferred_element_type=jnp.float32)
        goal = meta_ref[pl.ds((frames + frame) * pair, pair), :]
        for slot in range(slots):
            first, second = CHANNELS * slot, CHANNELS * slot + 1
            value_0 = jnp.broadcast_to(picked[first : first + 1], sub.shape)
            value_1 = jnp.broadcast_to(picked[second : second + 1], sub.shape)
            goal_0 = jnp.broadcast_to(goal[first : first + 1], sub.shape)
            goal_1 = jnp.broadcast_to(goal[second : second + 1], sub.shape)
            parts = []
            for block in range(groups):
                base = block * BLOCK_ROWS
                parts.append(jnp.where(sub + base == goal_0, value_0, zero))
                parts.append(jnp.where(sub + (base + BLK_DEV) == goal_1, value_1, zero))
                edge = sub[:8] + (base + 2 * BLK_DEV)
                parts.append(
                    jnp.where(
                        edge == goal_0[:8], value_0[:8], jnp.where(edge == goal_1[:8], value_1[:8], zero[:8])
                    )
                )
            place = (frame * slots + slot) * pixels
            placed_ref[:, pl.ds(place, pixels)] = jnp.concatenate(parts, axis=0).astype(jnp.bfloat16)
    total = jnp.dot(placed_ref[...], split_ref[...], preferred_element_type=jnp.float32)
    for block in range(groups):
        outs[block][...] = total[block * BLOCK_ROWS : (block + 1) * BLOCK_ROWS]


def finish_kernel(groups, handed_ref, *refs):
    parts, (merged_ref, weight_ref) = refs[:groups], refs[groups:]
    group = lax.axis_index("frame")
    row = jnp.where(group == 0, 0, jnp.where(group == groups - 1, BLK_DEV - 1, -1))
    here = lax.broadcasted_iota(jnp.int32, merged_ref.shape, 0) == row
    totals = []
    for c in range(CHANNELS):
        rows = pl.ds(c * BLK_DEV, BLK_DEV)
        total = jnp.where(here, handed_ref[pl.ds(c, 1), :], 0.0)
        for part in parts:
            total = total + part[rows, :]
        totals.append(total)
    weight_ref[...] = totals[1]
    merged_ref[...] = totals[0] / jnp.maximum(totals[1], 1.0)


def on_device(intensity, correction, splitting, block_count, pix_index, vox_offset):
    frames_dev, blocks_per_device, pixel_width = intensity.shape
    max_slots = splitting.shape[2]
    voxels = splitting.shape[4]
    bricks = lax.axis_size("brick")
    groups = lax.axis_size("frame")
    top = groups - 1
    block_rows = BLK_DEV * groups
    slot_count = frames_dev * max_slots

    in_vmem = pl.BlockSpec(memory_space=pltpu.VMEM)
    row_count = frames_dev * blocks_per_device
    local_rows = jnp.stack([intensity, correction], axis=0).astype(jnp.bfloat16)
    local_rows = local_rows.reshape(CHANNELS * row_count, pixel_width)
    depth = slot_count * pixel_width

    counts = jnp.broadcast_to(block_count, (frames_dev, max_slots))
    indices = [pix_index.reshape(frames_dev, max_slots), vox_offset.reshape(frames_dev, max_slots), counts]
    indices = jnp.pad(jnp.concatenate(indices, axis=0), ((0, 0), (0, pixel_width - max_slots)))
    split = splitting.reshape(depth, voxels)

    def prepare(first, distances):
        return pl.pallas_call(
            functools.partial(
                prepare_kernel, distances, blocks_per_device, block_rows, bricks, groups, max_slots
            ),
            out_shape=jax.ShapeDtypeStruct((2 * CHANNELS * slot_count, pixel_width), jnp.int32),
            in_specs=[in_vmem] * 3,
            out_specs=in_vmem,
            compiler_params=pltpu.CompilerParams(vmem_limit_bytes=VMEM_LIMIT),
            cost_estimate=pl.CostEstimate(flops=0, bytes_accessed=4 * depth * voxels, transcendentals=0),
            name="prepare",
        )(indices, first, split)

    (near, far), distances, meta = gather_rows(local_rows, bricks, prepare)
    blocks = pl.pallas_call(
        functools.partial(split_kernel, frames_dev, max_slots, groups),
        out_shape=[jax.ShapeDtypeStruct((BLOCK_ROWS, voxels), jnp.float32)] * groups,
        in_specs=[in_vmem] * 4,
        out_specs=[in_vmem] * groups,
        scratch_shapes=[pltpu.VMEM((groups * BLOCK_ROWS, slot_count * pixel_width), jnp.bfloat16)],
        compiler_params=pltpu.CompilerParams(vmem_limit_bytes=VMEM_LIMIT),
        cost_estimate=pl.CostEstimate(
            flops=2 * groups * BLOCK_ROWS * slot_count * pixel_width * voxels,
            bytes_accessed=2 * slot_count * pixel_width * voxels,
            transcendentals=0,
        ),
        name="split_and_place",
    )(near, far, meta, split)

    received = [
        lax.ppermute(blocks[step], "frame", [(i, (i + step) % groups) for i in range(groups)])
        for step in range(1, groups)
    ]
    edge = slice(CHANNELS * BLK_DEV, CHANNELS * BLK_DEV + CHANNELS)
    overhang = sum([part[edge] for part in received], blocks[0][edge])
    turn = [(i, i) for i in range(bricks, top * bricks)]
    for i in range(bricks):
        turn.append((i, i + 1 if i + 1 < bricks else top * bricks + i))
        turn.append((top * bricks + i, top * bricks + i - 1 if i else 0))
    handed = lax.ppermute(overhang, ("frame", "brick"), turn)
    merged, weight = pl.pallas_call(
        functools.partial(finish_kernel, groups),
        out_shape=[jax.ShapeDtypeStruct((BLK_DEV, voxels), jnp.float32)] * 2,
        in_specs=[in_vmem] * (groups + 1),
        out_specs=[in_vmem] * 2,
        compiler_params=pltpu.CompilerParams(vmem_limit_bytes=VMEM_LIMIT),
        name="finish",
    )(handed, blocks[0], *received)
    return (merged[None], weight[None])


def solution(mesh):
    placed = (
        P("frame", "brick", None),
        P("frame", "brick", None),
        P("frame", "brick", None, None, None),
        P("frame", "brick"),
        P("frame", "brick", None),
        P("frame", "brick", None),
    )
    return jax.shard_map(
        on_device,
        mesh=mesh,
        in_specs=placed,
        out_specs=(P("brick", "frame", None), P("brick", "frame", None)),
        check_vma=False,
    )
```

time: 32.7 us -> 27 us (0.83)
  other arithmetic: 5.29 us -> 1.57 us
  waiting for transfers between devices: 12.5 us -> 10.4 us
  Pallas kernels: 0.97 us -> 1.82 us
  local copies, waits for them, and re-layouts: 3.58 us -> 2.92 us
    ppermute x5, waiting for transfers between devices: 5.95 us -> 3.83 us  [gather_rows(): lax.ppermute(held, 'brick', [(i, i ^ step) for i in range(bricks)])]
    unnamed x1 -> x0, other arithmetic: 1.34 us -> none
    pallas_call x0 -> x3, Pallas kernels: none -> 0.85 us  [the longest x1 0.64 us: on_device(): pl.pallas_call(functools.partial(finish_kernel, groups), out_shape=[jax.S...]
    lt x1 -> x0, other arithmetic: 0.73 us -> none  [on_device(): jnp.arange(max_slots, dtype=jnp.int32)[None, :] < block_count]
    eq x2 -> x0, other arithmetic: 0.71 us -> none  [the longest x1 0.7 us: on_device(): low, high = (offsets == 0, offsets == block_rows + 1)]
    sub x1 -> x0, other arithmetic: 0.7 us -> none  [on_device(): owner = jnp.where(low, top, jnp.where(high, 0, (offsets - 1) // BLK_DEV))]
    concatenate x2, other arithmetic: 0.08 us -> 0.78 us  [the longest x1 0.77 us: on_device(): jnp.concatenate(indices, axis=0)]
    concatenate x2 -> x1, local copies, waits for them, and re-layouts: 0.06 us -> 0.73 us  [on_device(): jnp.concatenate(indices, axis=0)]
  transfers between devices with their start and end apart: 7 -> 7, of which waited for: 6 -> 6; matrix products, arithmetic and copies ran while one was open for 15% -> 6% of each run, Pallas kernels for 0% -> 1%
where the time goes in v2:
time: 27 us; the launch traced here: 26.7 us
  waiting for transfers between devices  10.4 us (39%)
  starting transfers between devices  9.28 us (34%)
  local copies, waits for them, and re-layouts  2.92 us (11%)
  Pallas kernels  1.82 us (7%)
  other arithmetic  1.57 us (6%)
  between operations  0.68 us (3%)
    ppermute x5, starting transfers between devices, gather_rows(): lax.ppermute(held, 'brick', [(i, i ^ step) for i in range(bricks)])  7.73 us
    ppermute x5, waiting for transfers between devices, gather_rows(): lax.ppermute(held, 'brick', [(i, i ^ step) for i in range(bricks)])  3.83 us
    ppermute x1, waiting for transfers between devices, on_device(): handed = lax.ppermute(overhang, ('frame', 'brick'), turn)  3.6 us
    ppermute x1, waiting for transfers between devices, on_device(): lax.ppermute(blocks[step], 'frame', [(i, (i + step) % groups) for i in ra...  2.99 us
    unnamed x4, local copies, waits for them, and re-layouts  2.19 us
    ppermute x1, starting transfers between devices, on_device(): lax.ppermute(blocks[step], 'frame', [(i, (i + step) % groups) for i in ra...  1.55 us
    pallas_call x1, Pallas kernels, on_device(): pl.pallas_call(functools.partial(split_kernel, frames_dev, max_slots, gro...  0.97 us
    another operation x2, other arithmetic, on_device(): local_rows = jnp.stack([intensity, correction], axis=0).astype(jnp.bfloat16)  0.79 us
  transfers between devices with their start and end apart: 7, of which 6 were waited for; matrix products, arithmetic and copies ran while one was open for 6% of the time, Pallas kernels for 1%

profile of v2, /device:TPU:0, one launch (start us, length us, event | category | flops | bytes accessed | tf_op | source)
XLA Modules:
  0.0 26.7 jit_solution(10584086137550988909)
XLA Ops:
  0.6 0.8 %convert_bitcast_fusion = (bf16[1,4,16,128]{3,2,1,0:T(8,128)(2,1)S(1)}, bf16[1,4,16,128]{3,2,1,0:T(8,128)(2,1)S(1)}) fusion(f32[4,16,128]{2,1,0:T(8,128)} %param.7, f32[4,16,128]{2,1,0:T(8,128)} %param.6), kind=kLoop, calls=%fused_computation.2 | loop fusion | flops 16384 | bytes 98304 | tf_op jit(solution)/shard_map/stack | solution.py:182
  1.4 4.1 %collective-permute-start = (bf16[1,128,128]{2,1,0:T(8,128)(2,1)S(1)}, bf16[1,128,128]{2,1,0:T(8,128)(2,1)S(1)}, u32[]{:S(2)}, u32[]{:S(2)}) collective-permute-start(bf16[1,128,128]{2,1,0:T(8,128)(2,1)S(1)} %bitcast.13), channel_id=1, source_target_pairs={{0,8},{1,9},{2,10},{3,11},{4,12},{5,13},{6,14},{7,15},{8,0},{9,1},... | collective-permute-start | bytes 98312 | tf_op jit(solution)/shard_map/ppermute | solution.py:53
  5.5 0.7 %pad.7.clone = s32[12]{0:T(128)S(1)} pad(s32[4]{0:T(128)} %bitcast.19, s32[]{:T(128)} %constant.0.clone.1), padding=8_0 | pad | bytes 68 | tf_op jit(solution)/shard_map/concatenate | solution.py:188
  6.2 1.5 %collective-permute-done = bf16[1,128,128]{2,1,0:T(8,128)(2,1)S(1)} collective-permute-done((bf16[1,128,128]{2,1,0:T(8,128)(2,1)S(1)}, bf16[1,128,128]{2,1,0:T(8,128)(2,1)S(1)}, u32[]{:S(2)}, u32[]{:S(2)}) %collective-permute-start) | collective-permute-done | bytes 32800 | tf_op jit(solution)/shard_map/ppermute | solution.py:53
  7.8 2.6 %collective-permute-start.3 = (bf16[2,128,128]{2,1,0:T(8,128)(2,1)S(1)}, bf16[2,128,128]{2,1,0:T(8,128)(2,1)S(1)}, u32[]{:S(2)}, u32[]{:S(2)}) collective-permute-start(bf16[2,128,128]{2,1,0:T(8,128)(2,1)S(1)} %pad_maximum_fusion.after_ref.refs_0_), channel_id=1, source_target_pairs={{0,6},{1,7},{2,4},{3,5},{4,2},{5,3},{6,0},{7,1},{8,14},{9,15},{10,... | collective-permute-start | bytes 196616 | tf_op jit(solution)/shard_map/ppermute | solution.py:53
  10.4 0.7 %collective-permute-start.2 = (bf16[2,128,128]{2,1,0:T(8,128)(2,1)S(1)}, bf16[2,128,128]{2,1,0:T(8,128)(2,1)S(1)}, u32[]{:S(2)}, u32[]{:S(2)}) collective-permute-start(bf16[2,128,128]{2,1,0:T(8,128)(2,1)S(1)} %pad_maximum_fusion.after_ref.refs_0_), channel_id=1, source_target_pairs={{0,4},{1,5},{2,6},{3,7},{4,0},{5,1},{6,2},{7,3},{8,12},{9,13},{10,... | collective-permute-start | bytes 196616 | tf_op jit(solution)/shard_map/ppermute | solution.py:53
  11.0 0.3 %collective-permute-start.1 = (bf16[2,128,128]{2,1,0:T(8,128)(2,1)S(1)}, bf16[2,128,128]{2,1,0:T(8,128)(2,1)S(1)}, u32[]{:S(2)}, u32[]{:S(2)}) collective-permute-start(bf16[2,128,128]{2,1,0:T(8,128)(2,1)S(1)} %pad_maximum_fusion.after_ref.refs_0_), channel_id=1, source_target_pairs={{0,2},{1,3},{2,0},{3,1},{4,6},{5,7},{6,4},{7,5},{8,10},{9,11},{10,... | collective-permute-start | bytes 196616 | tf_op jit(solution)/shard_map/ppermute | solution.py:53
  11.3 0.8 %add_add_fusion = s32[12,8]{1,0:T(8,128)S(1)} fusion(s32[4,8]{1,0:T(4,128)} %bitcast.15, s32[4,8]{1,0:T(4,128)} %bitcast.16, s32[12]{0:T(128)S(1)} %pad.7.clone), kind=kLoop, calls=%fused_computation.4 | loop fusion | flops 192 | bytes 688 | tf_op jit(solution)/shard_map/concatenate | solution.py:188
  12.1 0.0 copy-start
  12.1 2.2 %copy-done = bf16[4,1,8,128,512]{4,3,2,1,0:T(8,128)(2,1)S(1)} copy-done((bf16[4,1,8,128,512]{4,3,2,1,0:T(8,128)(2,1)S(1)}, bf16[4,1,8,128,512]{4,3,2,1,0:T(8,128)(2,1)}, u32[]{:S(2)}) %copy-start) | copy-done | bytes 4194328
  14.3 0.0 copy-start.1
  14.3 0.2 prepare.1.refs_4_.meta_ref
  14.5 0.0 collective-permute-done.3.refs_3_
  14.5 0.1 collective-permute-done.2.refs_2_
  14.6 0.7 %collective-permute-done.1.refs_1_ = bf16[2,128,128]{2,1,0:T(8,128)(2,1)S(1)} collective-permute-done((bf16[2,128,128]{2,1,0:T(8,128)(2,1)S(1)}, bf16[2,128,128]{2,1,0:T(8,128)(2,1)S(1)}, u32[]{:S(2)}, u32[]{:S(2)}) %collective-permute-start.1) | collective-permute-done | bytes 65568 | tf_op jit(solution)/shard_map/ppermute | solution.py:53
  15.3 0.1 collective-permute-start.4
  15.4 1.5 %collective-permute-done.4.far_ref = bf16[8,128,128]{2,1,0:T(8,128)(2,1)S(1)} collective-permute-done((bf16[8,128,128]{2,1,0:T(8,128)(2,1)S(1)}, bf16[8,128,128]{2,1,0:T(8,128)(2,1)S(1)}, u32[]{:S(2)}, u32[]{:S(2)}) %collective-permute-start.4) | collective-permute-done | bytes 262176 | tf_op jit(solution)/shard_map/ppermute | solution.py:53
  16.9 0.0 copy-done.1
  16.9 1.0 %split_and_place.1 = (f32[40,512]{1,0:T(8,128)S(1)}, f32[40,512]{1,0:T(8,128)S(1)}) custom-call(bf16[8,128,128]{2,1,0:T(8,128)(2,1)S(1)} %join_rows.1.near_ref, bf16[8,128,128]{2,1,0:T(8,128)(2,1)S(1)} %collective-permute-done.4.far_ref, s32[128,128]{1,0:T(8,128)S(1)} %prepare.1.refs_4_.meta_ref, bf16[4096,512]{1,0:T(8,128)(2,1)S(1)} %bitcast.12), custom_call_target="tpu_custom_call" | custom-call | flops 335544320 | bytes 4194304 | tf_op jit(solution)/shard_map/split_and_place/pallas_call | solution.py:205
  17.9 1.6 %collective-permute-start.5 = (f32[40,512]{1,0:T(8,128)S(1)}, f32[40,512]{1,0:T(8,128)S(1)}, u32[]{:S(2)}, u32[]{:S(2)}) collective-permute-start(f32[40,512]{1,0:T(8,128)S(1)} %get-tuple-element.7), channel_id=1, source_target_pairs={{0,16},{16,0},{1,17},{17,1},{2,18},{18,2},{3,19},{19,3},{4,20},{20... | collective-permute-start | bytes 245768 | tf_op jit(solution)/shard_map/ppermute | solution.py:221
  19.4 3.0 %collective-permute-done.5.refs_1_ = f32[40,512]{1,0:T(8,128)S(1)} collective-permute-done((f32[40,512]{1,0:T(8,128)S(1)}, f32[40,512]{1,0:T(8,128)S(1)}, u32[]{:S(2)}, u32[]{:S(2)}) %collective-permute-start.5) | collective-permute-done | bytes 81952 | tf_op jit(solution)/shard_map/ppermute | solution.py:221
  22.4 0.0 collective-permute-start.6
  22.5 3.6 %collective-permute-done.6.handed_ref = f32[2,512]{1,0:T(2,128)S(1)} collective-permute-done((f32[2,512]{1,0:T(2,128)S(1)}, f32[2,512]{1,0:T(2,128)S(1)}, u32[]{:S(2)}, u32[]{:S(2)}) %collective-permute-start.6) | collective-permute-done | bytes 4128 | tf_op jit(solution)/shard_map/ppermute | solution.py:230
  26.1 0.6 %finish.1 = (f32[16,512]{1,0:T(8,128)}, f32[16,512]{1,0:T(8,128)}) custom-call(f32[2,512]{1,0:T(2,128)S(1)} %collective-permute-done.6.handed_ref, f32[40,512]{1,0:T(8,128)S(1)} %get-tuple-element.6.refs_0_, f32[40,512]{1,0:T(8,128)S(1)} %collective-permute-done.5.refs_1_), custom_call_target="tpu_custom_call" | custom-call | tf_op jit(solution)/shard_map/finish/pallas_call | solution.py:231
  (5 shorter events, 0.0 us)
Async XLA Ops:
  1.4 6.3 %collective-permute-start = (bf16[1,128,128]{2,1,0:T(8,128)(2,1)S(1)}, bf16[1,128,128]{2,1,0:T(8,128)(2,1)S(1)}, u32[]{:S(2)}, u32[]{:S(2)}) collective-permute-start(bf16[1,128,128]{2,1,0:T(8,128)(2,1)S(1)} %bitcast.13), channel_id=1, source_target_pairs={{0,8},{1,9},{2,10},{3,11},{4,12},{5,13},{6,14},{7,15},{8,0},{9,1},... | collective-permute-start | bytes 98312 | tf_op jit(solution)/shard_map/ppermute | solution.py:53
  7.8 6.7 %collective-permute-start.3 = (bf16[2,128,128]{2,1,0:T(8,128)(2,1)S(1)}, bf16[2,128,128]{2,1,0:T(8,128)(2,1)S(1)}, u32[]{:S(2)}, u32[]{:S(2)}) collective-permute-start(bf16[2,128,128]{2,1,0:T(8,128)(2,1)S(1)} %pad_maximum_fusion.after_ref.refs_0_), channel_id=1, source_target_pairs={{0,6},{1,7},{2,4},{3,5},{4,2},{5,3},{6,0},{7,1},{8,14},{9,15},{10,... | collective-permute-start | bytes 196616 | tf_op jit(solution)/shard_map/ppermute | solution.py:53
  10.4 4.3 %collective-permute-start.2 = (bf16[2,128,128]{2,1,0:T(8,128)(2,1)S(1)}, bf16[2,128,128]{2,1,0:T(8,128)(2,1)S(1)}, u32[]{:S(2)}, u32[]{:S(2)}) collective-permute-start(bf16[2,128,128]{2,1,0:T(8,128)(2,1)S(1)} %pad_maximum_fusion.after_ref.refs_0_), channel_id=1, source_target_pairs={{0,4},{1,5},{2,6},{3,7},{4,0},{5,1},{6,2},{7,3},{8,12},{9,13},{10,... | collective-permute-start | bytes 196616 | tf_op jit(solution)/shard_map/ppermute | solution.py:53
  11.0 4.3 %collective-permute-start.1 = (bf16[2,128,128]{2,1,0:T(8,128)(2,1)S(1)}, bf16[2,128,128]{2,1,0:T(8,128)(2,1)S(1)}, u32[]{:S(2)}, u32[]{:S(2)}) collective-permute-start(bf16[2,128,128]{2,1,0:T(8,128)(2,1)S(1)} %pad_maximum_fusion.after_ref.refs_0_), channel_id=1, source_target_pairs={{0,2},{1,3},{2,0},{3,1},{4,6},{5,7},{6,4},{7,5},{8,10},{9,11},{10,... | collective-permute-start | bytes 196616 | tf_op jit(solution)/shard_map/ppermute | solution.py:53
  12.1 2.2 %copy-start = (bf16[4,1,8,128,512]{4,3,2,1,0:T(8,128)(2,1)S(1)}, bf16[4,1,8,128,512]{4,3,2,1,0:T(8,128)(2,1)}, u32[]{:S(2)}) copy-start(bf16[4,1,8,128,512]{4,3,2,1,0:T(8,128)(2,1)} %param.8) | copy-start | bytes 12582916
  14.3 2.6 %copy-start.1 = (bf16[4,1,8,128,512]{4,3,2,1,0:T(8,128)(2,1)S(1)}, bf16[4,1,8,128,512]{4,3,2,1,0:T(8,128)(2,1)}, u32[]{:S(2)}) copy-start(bf16[4,1,8,128,512]{4,3,2,1,0:T(8,128)(2,1)} %param.8) | copy-start | bytes 12582916
  15.3 1.6 %collective-permute-start.4 = (bf16[8,128,128]{2,1,0:T(8,128)(2,1)S(1)}, bf16[8,128,128]{2,1,0:T(8,128)(2,1)S(1)}, u32[]{:S(2)}, u32[]{:S(2)}) collective-permute-start(bf16[8,128,128]{2,1,0:T(8,128)(2,1)S(1)} %join_rows.1.near_ref), channel_id=1, source_target_pairs={{0,1},{1,0},{2,3},{3,2},{4,5},{5,4},{6,7},{7,6},{8,9},{9,8},{10,11... | collective-permute-start | bytes 786440 | tf_op jit(solution)/shard_map/ppermute | solution.py:53
  17.9 4.5 %collective-permute-start.5 = (f32[40,512]{1,0:T(8,128)S(1)}, f32[40,512]{1,0:T(8,128)S(1)}, u32[]{:S(2)}, u32[]{:S(2)}) collective-permute-start(f32[40,512]{1,0:T(8,128)S(1)} %get-tuple-element.7), channel_id=1, source_target_pairs={{0,16},{16,0},{1,17},{17,1},{2,18},{18,2},{3,19},{19,3},{4,20},{20... | collective-permute-start | bytes 245768 | tf_op jit(solution)/shard_map/ppermute | solution.py:221
  22.4 3.6 %collective-permute-start.6 = (f32[2,512]{1,0:T(2,128)S(1)}, f32[2,512]{1,0:T(2,128)S(1)}, u32[]{:S(2)}, u32[]{:S(2)}) collective-permute-start(f32[2,512]{1,0:T(2,128)S(1)} %slice_add_fusion), channel_id=1, source_target_pairs={{0,1},{16,0},{1,2},{17,16},{2,3},{18,17},{3,4},{19,18},{4,5},{20,1... | collective-permute-start | bytes 12296 | tf_op jit(solution)/shard_map/ppermute | solution.py:230

commit v3 on v2

--- a/solution.py
+++ b/solution.py
@@ -101,15 +101,15 @@
         meta_ref[pl.ds((frames + frame) * wide[0], wide[0]), :] = jnp.where(live, goal, -1)
 
 
-def split_kernel(frames, slots, groups, near_ref, far_ref, meta_ref, split_ref, *refs):
-    outs, placed_ref = refs[:groups], refs[groups]
+def edge_kernel(frames, slots, groups, near_ref, far_ref, meta_ref, split_ref, *refs):
+    picked_ref, edges, placed_ref = refs[0], refs[1 : 1 + groups], refs[1 + groups]
     half, per_brick, pixels = near_ref.shape
     per_owner = per_brick // (CHANNELS * frames)
     reach = 2 * half * CHANNELS * per_owner
     pair = CHANNELS * slots
-    sub = lax.broadcasted_iota(jnp.int32, (BLK_DEV, pixels), 0)
     lane = lax.broadcasted_iota(jnp.int32, (pair, pixels), 1)
-    zero = jnp.zeros((BLK_DEV, pixels), jnp.float32)
+    row = lax.broadcasted_iota(jnp.int32, (placed_ref.shape[0], pixels), 0)
+    row = row // CHANNELS * BLOCK_ROWS + CHANNELS * BLK_DEV + row % CHANNELS
     for frame in range(frames):
         target = meta_ref[pl.ds(frame * pair, pair), :]
         chosen = jnp.concatenate(
@@ -126,29 +126,51 @@
             axis=0,
         )
         picked = jnp.dot(chosen, own, preferred_element_type=jnp.float32)
+        picked_ref[pl.ds(frame * pair, pair), :] = picked
         goal = meta_ref[pl.ds((frames + frame) * pair, pair), :]
         for slot in range(slots):
-            first, second = CHANNELS * slot, CHANNELS * slot + 1
-            value_0 = jnp.broadcast_to(picked[first : first + 1], sub.shape)
-            value_1 = jnp.broadcast_to(picked[second : second + 1], sub.shape)
-            goal_0 = jnp.broadcast_to(goal[first : first + 1], sub.shape)
-            goal_1 = jnp.broadcast_to(goal[second : second + 1], sub.shape)
+            laid = jnp.zeros(row.shape, jnp.float32)
+            for c in range(CHANNELS):
+                at = CHANNELS * slot + c
+                value = jnp.broadcast_to(picked[at : at + 1], row.shape)
+                laid = jnp.where(row == jnp.broadcast_to(goal[at : at + 1], row.shape), value, laid)
+            place = (frame * slots + slot) * pixels
+            placed_ref[:, pl.ds(place, pixels)] = laid.astype(jnp.bfloat16)
+    total = jnp.dot(placed_ref[...], split_ref[...], preferred_element_type=jnp.float32)
+    for block in range(groups):
+        edges[block][...] = total[CHANNELS * block : CHANNELS * (block + 1)]
+
+
+def inner_kernel(frames, slots, groups, picked_ref, meta_ref, split_ref, *refs):
+    inner, placed_ref = refs[:groups], refs[groups]
+    pixels = picked_ref.shape[1]
+    pair = CHANNELS * slots
+    row = lax.broadcasted_iota(jnp.int32, (BLK_DEV, pixels), 0)
+    zero = jnp.zeros(row.shape, jnp.float32)
+    for frame in range(frames):
+        picked = picked_ref[pl.ds(frame * pair, pair), :]
+        goal = meta_ref[pl.ds((frames + frame) * pair, pair), :]
+        for slot in range(slots):
             parts = []
             for block in range(groups):
-                base = block * BLOCK_ROWS
-                parts.append(jnp.where(sub + base == goal_0, value_0, zero))
-                parts.append(jnp.where(sub + (base + BLK_DEV) == goal_1, value_1, zero))
-                edge = sub[:8] + (base + 2 * BLK_DEV)
-                parts.append(
-                    jnp.where(
-                        edge == goal_0[:8], value_0[:8], jnp.where(edge == goal_1[:8], value_1[:8], zero[:8])
-                    )
-                )
+                for c in range(CHANNELS):
+                    at = CHANNELS * slot + c
+                    value = jnp.broadcast_to(picked[at : at + 1], row.shape)
+                    here = jnp.broadcast_to(goal[at : at + 1], row.shape) - (block * BLOCK_ROWS + c * BLK_DEV)
+                    parts.append(jnp.where(row == here, value, zero))
             place = (frame * slots + slot) * pixels
             placed_ref[:, pl.ds(place, pixels)] = jnp.concatenate(parts, axis=0).astype(jnp.bfloat16)
     total = jnp.dot(placed_ref[...], split_ref[...], preferred_element_type=jnp.float32)
     for block in range(groups):
-        outs[block][...] = total[block * BLOCK_ROWS : (block + 1) * BLOCK_ROWS]
+        base = block * CHANNELS * BLK_DEV
+        inner[block][...] = total[base : base + CHANNELS * BLK_DEV]
+
+
+def sum_kernel(*refs):
+    total = refs[0][...]
+    for ref in refs[1:-1]:
+        total = total + ref[...]
+    refs[-1][...] = total
 
 
 def finish_kernel(groups, handed_ref, *refs):
@@ -202,27 +224,51 @@
         )(indices, first, split)
 
     (near, far), distances, meta = gather_rows(local_rows, bricks, prepare)
+    edge_rows = -(-CHANNELS * groups // 16) * 16
+    inner_rows = CHANNELS * BLK_DEV * groups
+    picked, *edges = pl.pallas_call(
+        functools.partial(edge_kernel, frames_dev, max_slots, groups),
+        out_shape=[jax.ShapeDtypeStruct((CHANNELS * slot_count, pixel_width), jnp.float32)]
+        + [jax.ShapeDtypeStruct((CHANNELS, voxels), jnp.float32)] * groups,
+        in_specs=[in_vmem] * 4,
+        out_specs=[in_vmem] * (1 + groups),
+        scratch_shapes=[pltpu.VMEM((edge_rows, depth), jnp.bfloat16)],
+        compiler_params=pltpu.CompilerParams(vmem_limit_bytes=VMEM_LIMIT),
+        cost_estimate=pl.CostEstimate(
+            flops=2 * edge_rows * depth * voxels, bytes_accessed=2 * depth * voxels, transcendentals=0
+        ),
+        name="edges",
+    )(near, far, meta, split)
     blocks = pl.pallas_call(
-        functools.partial(split_kernel, frames_dev, max_slots, groups),
-        out_shape=[jax.ShapeDtypeStruct((BLOCK_ROWS, voxels), jnp.float32)] * groups,
-        in_specs=[in_vmem] * 4,
+        functools.partial(inner_kernel, frames_dev, max_slots, groups),
+        out_shape=[jax.ShapeDtypeStruct((CHANNELS * BLK_DEV, voxels), jnp.float32)] * groups,
+        in_specs=[in_vmem] * 3,
         out_specs=[in_vmem] * groups,
-        scratch_shapes=[pltpu.VMEM((groups * BLOCK_ROWS, slot_count * pixel_width), jnp.bfloat16)],
+        scratch_shapes=[pltpu.VMEM((inner_rows, depth), jnp.bfloat16)],
         compiler_params=pltpu.CompilerParams(vmem_limit_bytes=VMEM_LIMIT),
         cost_estimate=pl.CostEstimate(
-            flops=2 * groups * BLOCK_ROWS * slot_count * pixel_width * voxels,
-            bytes_accessed=2 * slot_count * pixel_width * voxels,
-            transcendentals=0,
+            flops=2 * inner_rows * depth * voxels, bytes_accessed=2 * depth * voxels, transcendentals=0
         ),
-        name="split_and_place",
-    )(near, far, meta, split)
-
-    received = [
-        lax.ppermute(blocks[step], "frame", [(i, (i + step) % groups) for i in range(groups)])
-        for step in range(1, groups)
-    ]
-    edge = slice(CHANNELS * BLK_DEV, CHANNELS * BLK_DEV + CHANNELS)
-    overhang = sum([part[edge] for part in received], blocks[0][edge])
+        name="inner",
+    )(picked, meta, split)
+
+    def to_owner(parts):
+        return [
+            lax.ppermute(parts[step], "frame", [(i, (i + step) % groups) for i in range(groups)])
+            for step in range(1, groups)
+        ]
+
+    arrived = to_owner(edges)
+    overhang = pl.pallas_call(
+        sum_kernel,
+        out_shape=jax.ShapeDtypeStruct((CHANNELS, voxels), jnp.float32),
+        in_specs=[in_vmem] * groups,
+        out_specs=in_vmem,
+        compiler_params=pltpu.CompilerParams(vmem_limit_bytes=VMEM_LIMIT),
+        cost_estimate=pl.CostEstimate(flops=10**9, bytes_accessed=0, transcendentals=0),
+        name="sum_edges",
+    )(edges[0], *arrived)
+    received = to_owner(blocks)
     turn = [(i, i) for i in range(bricks, top * bricks)]
     for i in range(bricks):
         turn.append((i, i + 1 if i + 1 < bricks else top * bricks + i))

time: 27 us -> 25.8 us (0.956)
  waiting for transfers between devices: 10.4 us -> 8.1 us
  Pallas kernels: 1.82 us -> 2.46 us
  starting transfers between devices: 9.28 us -> 9.83 us
    ppermute x1 -> x2, waiting for transfers between devices: 2.99 us -> 0.66 us  [to_owner(): lax.ppermute(parts[step], 'frame', [(i, (i + step) % groups) for i in ran...]
    pallas_call x1 -> x3, Pallas kernels: 0.97 us -> 1.61 us  [the longest x1 0.84 us: on_device(): pl.pallas_call(functools.partial(inner_kernel, frames_dev, max_slots, gro...]
    ppermute x1 -> x2, starting transfers between devices: 1.55 us -> 2.1 us  [to_owner(): lax.ppermute(parts[step], 'frame', [(i, (i + step) % groups) for i in ran...]
  transfers between devices with their start and end apart: 7 -> 8, of which waited for: 6 -> 6; matrix products, arithmetic and copies ran while one was open for 6% -> 6% of each run, Pallas kernels for 1% -> 4%
where the time goes in v3:
time: 25.8 us; the launch traced here: 25.6 us
  starting transfers between devices  9.83 us (38%)
  waiting for transfers between devices  8.1 us (31%)
  local copies, waits for them, and re-layouts  2.92 us (11%)
  Pallas kernels  2.46 us (10%)
  other arithmetic  1.57 us (6%)
  between operations  0.69 us (3%)
    ppermute x5, starting transfers between devices, gather_rows(): lax.ppermute(held, 'brick', [(i, i ^ step) for i in range(bricks)])  7.73 us
    ppermute x5, waiting for transfers between devices, gather_rows(): lax.ppermute(held, 'brick', [(i, i ^ step) for i in range(bricks)])  3.83 us
    ppermute x1, waiting for transfers between devices, on_device(): handed = lax.ppermute(overhang, ('frame', 'brick'), turn)  3.6 us
    unnamed x4, local copies, waits for them, and re-layouts  2.19 us
    ppermute x2, starting transfers between devices, to_owner(): lax.ppermute(parts[step], 'frame', [(i, (i + step) % groups) for i in ran...  2.1 us
    pallas_call x1, Pallas kernels, on_device(): pl.pallas_call(functools.partial(inner_kernel, frames_dev, max_slots, gro...  0.84 us
    another operation x2, other arithmetic, on_device(): local_rows = jnp.stack([intensity, correction], axis=0).astype(jnp.bfloat16)  0.79 us
    concatenate x1, other arithmetic, on_device(): jnp.concatenate(indices, axis=0)  0.77 us
  transfers between devices with their start and end apart: 8, of which 6 were waited for; matrix products, arithmetic and copies ran while one was open for 6% of the time, Pallas kernels for 4%

profile of v3, /device:TPU:0, one launch (start us, length us, event | category | flops | bytes accessed | tf_op | source)
XLA Modules:
  0.0 25.6 jit_solution(6143904655957583390)
XLA Ops:
  0.6 0.8 %convert_bitcast_fusion = (bf16[1,4,16,128]{3,2,1,0:T(8,128)(2,1)S(1)}, bf16[1,4,16,128]{3,2,1,0:T(8,128)(2,1)S(1)}) fusion(f32[4,16,128]{2,1,0:T(8,128)} %param.7, f32[4,16,128]{2,1,0:T(8,128)} %param.6), kind=kLoop, calls=%fused_computation.2 | loop fusion | flops 16384 | bytes 98304 | tf_op jit(solution)/shard_map/stack | solution.py:204
  1.4 4.1 %collective-permute-start = (bf16[1,128,128]{2,1,0:T(8,128)(2,1)S(1)}, bf16[1,128,128]{2,1,0:T(8,128)(2,1)S(1)}, u32[]{:S(2)}, u32[]{:S(2)}) collective-permute-start(bf16[1,128,128]{2,1,0:T(8,128)(2,1)S(1)} %bitcast.14), channel_id=1, source_target_pairs={{0,8},{1,9},{2,10},{3,11},{4,12},{5,13},{6,14},{7,15},{8,0},{9,1},... | collective-permute-start | bytes 98312 | tf_op jit(solution)/shard_map/ppermute | solution.py:53
  5.5 0.7 %pad.7.clone = s32[12]{0:T(128)S(1)} pad(s32[4]{0:T(128)} %bitcast.20, s32[]{:T(128)} %constant.0.clone.1), padding=8_0 | pad | bytes 68 | tf_op jit(solution)/shard_map/concatenate | solution.py:210
  6.2 1.5 %collective-permute-done = bf16[1,128,128]{2,1,0:T(8,128)(2,1)S(1)} collective-permute-done((bf16[1,128,128]{2,1,0:T(8,128)(2,1)S(1)}, bf16[1,128,128]{2,1,0:T(8,128)(2,1)S(1)}, u32[]{:S(2)}, u32[]{:S(2)}) %collective-permute-start) | collective-permute-done | bytes 32800 | tf_op jit(solution)/shard_map/ppermute | solution.py:53
  7.8 2.6 %collective-permute-start.3 = (bf16[2,128,128]{2,1,0:T(8,128)(2,1)S(1)}, bf16[2,128,128]{2,1,0:T(8,128)(2,1)S(1)}, u32[]{:S(2)}, u32[]{:S(2)}) collective-permute-start(bf16[2,128,128]{2,1,0:T(8,128)(2,1)S(1)} %pad_maximum_fusion.after_ref.refs_0_), channel_id=1, source_target_pairs={{0,6},{1,7},{2,4},{3,5},{4,2},{5,3},{6,0},{7,1},{8,14},{9,15},{10,... | collective-permute-start | bytes 196616 | tf_op jit(solution)/shard_map/ppermute | solution.py:53
  10.4 0.7 %collective-permute-start.2 = (bf16[2,128,128]{2,1,0:T(8,128)(2,1)S(1)}, bf16[2,128,128]{2,1,0:T(8,128)(2,1)S(1)}, u32[]{:S(2)}, u32[]{:S(2)}) collective-permute-start(bf16[2,128,128]{2,1,0:T(8,128)(2,1)S(1)} %pad_maximum_fusion.after_ref.refs_0_), channel_id=1, source_target_pairs={{0,4},{1,5},{2,6},{3,7},{4,0},{5,1},{6,2},{7,3},{8,12},{9,13},{10,... | collective-permute-start | bytes 196616 | tf_op jit(solution)/shard_map/ppermute | solution.py:53
  11.0 0.3 %collective-permute-start.1 = (bf16[2,128,128]{2,1,0:T(8,128)(2,1)S(1)}, bf16[2,128,128]{2,1,0:T(8,128)(2,1)S(1)}, u32[]{:S(2)}, u32[]{:S(2)}) collective-permute-start(bf16[2,128,128]{2,1,0:T(8,128)(2,1)S(1)} %pad_maximum_fusion.after_ref.refs_0_), channel_id=1, source_target_pairs={{0,2},{1,3},{2,0},{3,1},{4,6},{5,7},{6,4},{7,5},{8,10},{9,11},{10,... | collective-permute-start | bytes 196616 | tf_op jit(solution)/shard_map/ppermute | solution.py:53
  11.3 0.8 %add_add_fusion = s32[12,8]{1,0:T(8,128)S(1)} fusion(s32[4,8]{1,0:T(4,128)} %bitcast.16, s32[4,8]{1,0:T(4,128)} %bitcast.17, s32[12]{0:T(128)S(1)} %pad.7.clone), kind=kLoop, calls=%fused_computation.4 | loop fusion | flops 192 | bytes 688 | tf_op jit(solution)/shard_map/concatenate | solution.py:210
  12.1 0.0 copy-start
  12.1 2.2 %copy-done = bf16[4,1,8,128,512]{4,3,2,1,0:T(8,128)(2,1)S(1)} copy-done((bf16[4,1,8,128,512]{4,3,2,1,0:T(8,128)(2,1)S(1)}, bf16[4,1,8,128,512]{4,3,2,1,0:T(8,128)(2,1)}, u32[]{:S(2)}) %copy-start) | copy-done | bytes 4194328
  14.3 0.0 copy-start.1
  14.3 0.2 prepare.1.refs_4_.meta_ref
  14.5 0.0 collective-permute-done.3.refs_3_
  14.5 0.1 collective-permute-done.2.refs_2_
  14.6 0.7 %collective-permute-done.1.refs_1_ = bf16[2,128,128]{2,1,0:T(8,128)(2,1)S(1)} collective-permute-done((bf16[2,128,128]{2,1,0:T(8,128)(2,1)S(1)}, bf16[2,128,128]{2,1,0:T(8,128)(2,1)S(1)}, u32[]{:S(2)}, u32[]{:S(2)}) %collective-permute-start.1) | collective-permute-done | bytes 65568 | tf_op jit(solution)/shard_map/ppermute | solution.py:53
  15.3 0.1 collective-permute-start.4
  15.4 1.5 %collective-permute-done.4.far_ref = bf16[8,128,128]{2,1,0:T(8,128)(2,1)S(1)} collective-permute-done((bf16[8,128,128]{2,1,0:T(8,128)(2,1)S(1)}, bf16[8,128,128]{2,1,0:T(8,128)(2,1)S(1)}, u32[]{:S(2)}, u32[]{:S(2)}) %collective-permute-start.4) | collective-permute-done | bytes 262176 | tf_op jit(solution)/shard_map/ppermute | solution.py:53
  16.9 0.0 copy-done.1
  16.9 0.8 %edges.1 = (f32[64,128]{1,0:T(8,128)S(1)}, f32[2,512]{1,0:T(2,128)S(1)}, f32[2,512]{1,0:T(2,128)S(1)}) custom-call(bf16[8,128,128]{2,1,0:T(8,128)(2,1)S(1)} %join_rows.1.near_ref, bf16[8,128,128]{2,1,0:T(8,128)(2,1)S(1)} %collective-permute-done.4.far_ref, s32[128,128]{1,0:T(8,128)S(1)} %prepare.1.refs_4_.meta_ref, bf16[4096,512]{1,0:T(8,128)(2,1)S(1)} %bitcast.12), custom_call_target="tpu_custom_call" | custom-call | flops 67108864 | bytes 4194304 | tf_op jit(solution)/shard_map/edges/pallas_call | solution.py:229
  17.7 1.5 %collective-permute-start.5 = (f32[2,512]{1,0:T(2,128)S(1)}, f32[2,512]{1,0:T(2,128)S(1)}, u32[]{:S(2)}, u32[]{:S(2)}) collective-permute-start(f32[2,512]{1,0:T(2,128)S(1)} %get-tuple-element.10), channel_id=1, source_target_pairs={{0,16},{16,0},{1,17},{17,1},{2,18},{18,2},{3,19},{19,3},{4,20},{20... | collective-permute-start | bytes 12296 | tf_op jit(solution)/shard_map/ppermute | solution.py:257
  19.2 0.8 %inner.1 = (f32[32,512]{1,0:T(8,128)S(1)}, f32[32,512]{1,0:T(8,128)S(1)}) custom-call(f32[64,128]{1,0:T(8,128)S(1)} %get-tuple-element.11.picked_ref, s32[128,128]{1,0:T(8,128)S(1)} %prepare.1.refs_4_.meta_ref, bf16[4096,512]{1,0:T(8,128)(2,1)S(1)} %bitcast.13), custom_call_target="tpu_custom_call" | custom-call | flops 268435456 | bytes 4194304 | tf_op jit(solution)/shard_map/inner/pallas_call | solution.py:242
  20.0 0.6 %collective-permute-start.7 = (f32[32,512]{1,0:T(8,128)S(1)}, f32[32,512]{1,0:T(8,128)S(1)}, u32[]{:S(2)}, u32[]{:S(2)}) collective-permute-start(f32[32,512]{1,0:T(8,128)S(1)} %get-tuple-element.13), channel_id=1, source_target_pairs={{0,16},{16,0},{1,17},{17,1},{2,18},{18,2},{3,19},{19,3},{4,20},{20... | collective-permute-start | bytes 196616 | tf_op jit(solution)/shard_map/ppermute | solution.py:257
  20.6 0.7 %collective-permute-done.5.refs_1_ = f32[2,512]{1,0:T(2,128)S(1)} collective-permute-done((f32[2,512]{1,0:T(2,128)S(1)}, f32[2,512]{1,0:T(2,128)S(1)}, u32[]{:S(2)}, u32[]{:S(2)}) %collective-permute-start.5) | collective-permute-done | bytes 4128 | tf_op jit(solution)/shard_map/ppermute | solution.py:257
  21.3 0.0 collective-permute-start.6
  21.3 3.6 %collective-permute-done.6.handed_ref = f32[2,512]{1,0:T(2,128)S(1)} collective-permute-done((f32[2,512]{1,0:T(2,128)S(1)}, f32[2,512]{1,0:T(2,128)S(1)}, u32[]{:S(2)}, u32[]{:S(2)}) %collective-permute-start.6) | collective-permute-done | bytes 4128 | tf_op jit(solution)/shard_map/ppermute | solution.py:276
  24.9 0.0 collective-permute-done.7.refs_1_
  24.9 0.6 %finish.1 = (f32[16,512]{1,0:T(8,128)}, f32[16,512]{1,0:T(8,128)}) custom-call(f32[2,512]{1,0:T(2,128)S(1)} %collective-permute-done.6.handed_ref, f32[32,512]{1,0:T(8,128)S(1)} %get-tuple-element.12.refs_0_, f32[32,512]{1,0:T(8,128)S(1)} %collective-permute-done.7.refs_1_), custom_call_target="tpu_custom_call" | custom-call | tf_op jit(solution)/shard_map/finish/pallas_call | solution.py:277
  (5 shorter events, 0.0 us)
Async XLA Ops:
  1.4 6.3 %collective-permute-start = (bf16[1,128,128]{2,1,0:T(8,128)(2,1)S(1)}, bf16[1,128,128]{2,1,0:T(8,128)(2,1)S(1)}, u32[]{:S(2)}, u32[]{:S(2)}) collective-permute-start(bf16[1,128,128]{2,1,0:T(8,128)(2,1)S(1)} %bitcast.14), channel_id=1, source_target_pairs={{0,8},{1,9},{2,10},{3,11},{4,12},{5,13},{6,14},{7,15},{8,0},{9,1},... | collective-permute-start | bytes 98312 | tf_op jit(solution)/shard_map/ppermute | solution.py:53
  7.8 6.7 %collective-permute-start.3 = (bf16[2,128,128]{2,1,0:T(8,128)(2,1)S(1)}, bf16[2,128,128]{2,1,0:T(8,128)(2,1)S(1)}, u32[]{:S(2)}, u32[]{:S(2)}) collective-permute-start(bf16[2,128,128]{2,1,0:T(8,128)(2,1)S(1)} %pad_maximum_fusion.after_ref.refs_0_), channel_id=1, source_target_pairs={{0,6},{1,7},{2,4},{3,5},{4,2},{5,3},{6,0},{7,1},{8,14},{9,15},{10,... | collective-permute-start | bytes 196616 | tf_op jit(solution)/shard_map/ppermute | solution.py:53
  10.4 4.3 %collective-permute-start.2 = (bf16[2,128,128]{2,1,0:T(8,128)(2,1)S(1)}, bf16[2,128,128]{2,1,0:T(8,128)(2,1)S(1)}, u32[]{:S(2)}, u32[]{:S(2)}) collective-permute-start(bf16[2,128,128]{2,1,0:T(8,128)(2,1)S(1)} %pad_maximum_fusion.after_ref.refs_0_), channel_id=1, source_target_pairs={{0,4},{1,5},{2,6},{3,7},{4,0},{5,1},{6,2},{7,3},{8,12},{9,13},{10,... | collective-permute-start | bytes 196616 | tf_op jit(solution)/shard_map/ppermute | solution.py:53
  11.0 4.3 %collective-permute-start.1 = (bf16[2,128,128]{2,1,0:T(8,128)(2,1)S(1)}, bf16[2,128,128]{2,1,0:T(8,128)(2,1)S(1)}, u32[]{:S(2)}, u32[]{:S(2)}) collective-permute-start(bf16[2,128,128]{2,1,0:T(8,128)(2,1)S(1)} %pad_maximum_fusion.after_ref.refs_0_), channel_id=1, source_target_pairs={{0,2},{1,3},{2,0},{3,1},{4,6},{5,7},{6,4},{7,5},{8,10},{9,11},{10,... | collective-permute-start | bytes 196616 | tf_op jit(solution)/shard_map/ppermute | solution.py:53
  12.1 2.2 %copy-start = (bf16[4,1,8,128,512]{4,3,2,1,0:T(8,128)(2,1)S(1)}, bf16[4,1,8,128,512]{4,3,2,1,0:T(8,128)(2,1)}, u32[]{:S(2)}) copy-start(bf16[4,1,8,128,512]{4,3,2,1,0:T(8,128)(2,1)} %param.8) | copy-start | bytes 12582916
  14.3 2.6 %copy-start.1 = (bf16[4,1,8,128,512]{4,3,2,1,0:T(8,128)(2,1)S(1)}, bf16[4,1,8,128,512]{4,3,2,1,0:T(8,128)(2,1)}, u32[]{:S(2)}) copy-start(bf16[4,1,8,128,512]{4,3,2,1,0:T(8,128)(2,1)} %param.8) | copy-start | bytes 12582916
  15.3 1.6 %collective-permute-start.4 = (bf16[8,128,128]{2,1,0:T(8,128)(2,1)S(1)}, bf16[8,128,128]{2,1,0:T(8,128)(2,1)S(1)}, u32[]{:S(2)}, u32[]{:S(2)}) collective-permute-start(bf16[8,128,128]{2,1,0:T(8,128)(2,1)S(1)} %join_rows.1.near_ref), channel_id=1, source_target_pairs={{0,1},{1,0},{2,3},{3,2},{4,5},{5,4},{6,7},{7,6},{8,9},{9,8},{10,11... | collective-permute-start | bytes 786440 | tf_op jit(solution)/shard_map/ppermute | solution.py:53
  17.7 3.6 %collective-permute-start.5 = (f32[2,512]{1,0:T(2,128)S(1)}, f32[2,512]{1,0:T(2,128)S(1)}, u32[]{:S(2)}, u32[]{:S(2)}) collective-permute-start(f32[2,512]{1,0:T(2,128)S(1)} %get-tuple-element.10), channel_id=1, source_target_pairs={{0,16},{16,0},{1,17},{17,1},{2,18},{18,2},{3,19},{19,3},{4,20},{20... | collective-permute-start | bytes 12296 | tf_op jit(solution)/shard_map/ppermute | solution.py:257
  20.0 4.9 %collective-permute-start.7 = (f32[32,512]{1,0:T(8,128)S(1)}, f32[32,512]{1,0:T(8,128)S(1)}, u32[]{:S(2)}, u32[]{:S(2)}) collective-permute-start(f32[32,512]{1,0:T(8,128)S(1)} %get-tuple-element.13), channel_id=1, source_target_pairs={{0,16},{16,0},{1,17},{17,1},{2,18},{18,2},{3,19},{19,3},{4,20},{20... | collective-permute-start | bytes 196616 | tf_op jit(solution)/shard_map/ppermute | solution.py:257
  21.3 3.6 %collective-permute-start.6 = (f32[2,512]{1,0:T(2,128)S(1)}, f32[2,512]{1,0:T(2,128)S(1)}, u32[]{:S(2)}, u32[]{:S(2)}) collective-permute-start(f32[2,512]{1,0:T(2,128)S(1)} %sum_edges.1), channel_id=1, source_target_pairs={{0,1},{16,0},{1,2},{17,16},{2,3},{18,17},{3,4},{19,18},{4,5},{20,1... | collective-permute-start | bytes 12296 | tf_op jit(solution)/shard_map/ppermute | solution.py:276

commit v4 on v3

--- a/solution.py
+++ b/solution.py
@@ -13,92 +13,83 @@
 BLOCK_ROWS = CHANNELS * BLK_DEV + 8
 
 
-def stages_of(bricks):
-    if bricks == 16:
-        return ((8,), (6, 2, 4), (1,))
-    rounds, distance = [], bricks // 2
-    while distance:
-        rounds.append((distance,))
-        distance //= 2
-    return tuple(rounds)
-
-
 def join_kernel(*refs):
     out_ref, at = refs[-1], 0
-    for ref in refs[:-2]:
+    for ref in refs[:-1]:
         out_ref[pl.ds(at, ref.shape[0])] = ref[...]
         at += ref.shape[0]
 
 
-def join(parts, after):
+def join(parts):
     in_vmem = pl.BlockSpec(memory_space=pltpu.VMEM)
     count = sum(part.shape[0] for part in parts)
     return pl.pallas_call(
         join_kernel,
         out_shape=jax.ShapeDtypeStruct((count,) + parts[0].shape[1:], parts[0].dtype),
-        in_specs=[in_vmem] * (len(parts) + 1),
+        in_specs=[in_vmem] * len(parts),
         out_specs=in_vmem,
         compiler_params=pltpu.CompilerParams(vmem_limit_bytes=VMEM_LIMIT),
+        cost_estimate=pl.CostEstimate(flops=10**11, bytes_accessed=0, transcendentals=0),
         name="join_rows",
-    )(*parts, after)
-
-
-def gather_rows(rows, bricks, beside):
-    stages = stages_of(bricks)
-    held, distances, made = rows[None], [0], None
-    for exchange in stages:
-        distances = distances + [d ^ step for step in sorted(exchange) for d in distances]
-    for at, exchange in enumerate(stages):
-        arrived = {
-            step: lax.ppermute(held, "brick", [(i, i ^ step) for i in range(bricks)]) for step in exchange
-        }
-        parts = [held] + [arrived[step] for step in sorted(arrived)]
-        if at == len(stages) - 2:
-            made = beside(held, distances)
-            held = join(parts, made)
-        elif at < len(stages) - 1:
-            held = jnp.concatenate(parts, axis=0)
-    return parts, distances, made
+    )(*parts)
+
+
+def swap(rows, bricks, step):
+    return lax.ppermute(rows, "brick", [(i, i ^ step) for i in range(bricks)])
+
+
+def gather_half(rows, bricks):
+    held, distances = rows[None], [0]
+    if bricks == 16:
+        parts = [held, swap(held, bricks, 8), swap(held, bricks, 2)]
+        corner = swap(held, bricks, 14)
+        three = jnp.concatenate(parts, axis=0)
+        parts = [join([three]), swap(three, bricks, 4), swap(parts[1], bricks, 2), corner]
+        distances = [0, 8, 2, 4, 12, 6, 10, 14]
+    else:
+        parts, step = [held], bricks // 2
+        while step > 1:
+            arrived = swap(jnp.concatenate(parts, axis=0), bricks, step)
+            parts, distances = parts + [arrived], distances + [d ^ step for d in distances]
+            step //= 2
+    return join(parts), distances + [d ^ 1 for d in distances]
 
 
 def place_of(distance, distances):
-    place, bit = 0, 1
-    while bit < len(distances):
-        place = place + jnp.where((distance & bit) != 0, distances.index(bit), 0)
-        bit *= 2
+    place = 0
+    for at, d in enumerate(distances):
+        place = place + jnp.where(distance == d, at, 0)
     return place
 
 
-def prepare_kernel(
-    distances, per_owner, block_rows, bricks, groups, slots, index_ref, after_ref, split_ref, meta_ref
-):
+def prepare_kernel(distances, per_owner, block_rows, bricks, groups, slots, index_ref, meta_ref):
     brick, group = lax.axis_index("brick"), lax.axis_index("frame")
-    frames = index_ref.shape[0] // 3
-    wide = (slots * CHANNELS, meta_ref.shape[1])
+    frames = index_ref.shape[0]
+    pair = slots * CHANNELS
+    wide = (pair, meta_ref.shape[1])
     row = lax.broadcasted_iota(jnp.int32, wide, 0)
     channel = row % CHANNELS
-    mine = lax.broadcasted_iota(jnp.int32, wide, 1) == row // CHANNELS
-
-    def of_slot(at):
-        line = jnp.broadcast_to(index_ref[pl.ds(at, 1), :], wide)
-        return jnp.sum(jnp.where(mine, line, 0), axis=1, keepdims=True) + jnp.zeros(wide, jnp.int32)
-
+    mine = lax.broadcasted_iota(jnp.int32, (pair, slots), 1) == (
+        lax.broadcasted_iota(jnp.int32, (pair, slots), 0) // CHANNELS
+    )
     for frame in range(frames):
-        pixel_block = of_slot(frame)
+        line = jnp.broadcast_to(index_ref[pl.ds(frame, 1), :], mine.shape)
+        index = jnp.broadcast_to(jnp.sum(jnp.where(mine, line, 0), axis=1, keepdims=True), wide)
+        pixel_block = index // (block_rows + 3)
+        offset = index - pixel_block * (block_rows + 3)
         owner = pixel_block // per_owner
         place = place_of(owner ^ brick, distances)
         target = (place * CHANNELS + channel) * per_owner + (pixel_block - owner * per_owner)
-        meta_ref[pl.ds(frame * wide[0], wide[0]), :] = target
-        offset = of_slot(frames + frame)
+        meta_ref[pl.ds(frame * pair, pair), :] = target
         low, high = offset == 0, offset == block_rows + 1
         holder = jnp.where(low, groups - 1, jnp.where(high, 0, (offset - 1) // BLK_DEV))
         step = holder - group
         step = jnp.where(step < 0, step + groups, step)
         inside = offset - 1 - holder * BLK_DEV + BLK_DEV * channel
         goal = step * BLOCK_ROWS + jnp.where(low | high, CHANNELS * BLK_DEV + channel, inside)
-        live = row // CHANNELS < of_slot(2 * frames + frame)
+        live = offset < block_rows + 2
         live = live & ~(low & (brick == 0)) & ~(high & (brick == bricks - 1))
-        meta_ref[pl.ds((frames + frame) * wide[0], wide[0]), :] = jnp.where(live, goal, -1)
+        meta_ref[pl.ds((frames + frame) * pair, pair), :] = jnp.where(live, goal, -1)
 
 
 def edge_kernel(frames, slots, groups, near_ref, far_ref, meta_ref, split_ref, *refs):
@@ -205,25 +196,26 @@
     local_rows = local_rows.reshape(CHANNELS * row_count, pixel_width)
     depth = slot_count * pixel_width
 
-    counts = jnp.broadcast_to(block_count, (frames_dev, max_slots))
-    indices = [pix_index.reshape(frames_dev, max_slots), vox_offset.reshape(frames_dev, max_slots), counts]
-    indices = jnp.pad(jnp.concatenate(indices, axis=0), ((0, 0), (0, pixel_width - max_slots)))
     split = splitting.reshape(depth, voxels)
 
-    def prepare(first, distances):
-        return pl.pallas_call(
-            functools.partial(
-                prepare_kernel, distances, blocks_per_device, block_rows, bricks, groups, max_slots
-            ),
-            out_shape=jax.ShapeDtypeStruct((2 * CHANNELS * slot_count, pixel_width), jnp.int32),
-            in_specs=[in_vmem] * 3,
-            out_specs=in_vmem,
-            compiler_params=pltpu.CompilerParams(vmem_limit_bytes=VMEM_LIMIT),
-            cost_estimate=pl.CostEstimate(flops=0, bytes_accessed=4 * depth * voxels, transcendentals=0),
-            name="prepare",
-        )(indices, first, split)
-
-    (near, far), distances, meta = gather_rows(local_rows, bricks, prepare)
+    near, distances = gather_half(local_rows, bricks)
+    near, block_count, pix_index, vox_offset = lax.optimization_barrier(
+        (near, block_count, pix_index, vox_offset)
+    )
+    far = swap(near, bricks, 1)
+    live = jnp.arange(max_slots, dtype=jnp.int32) < block_count[:, :, None]
+    index = pix_index * (block_rows + 3) + jnp.where(live, vox_offset, block_rows + 2)
+    meta = pl.pallas_call(
+        functools.partial(
+            prepare_kernel, distances, blocks_per_device, block_rows, bricks, groups, max_slots
+        ),
+        out_shape=jax.ShapeDtypeStruct((2 * CHANNELS * slot_count, pixel_width), jnp.int32),
+        in_specs=[in_vmem],
+        out_specs=in_vmem,
+        compiler_params=pltpu.CompilerParams(vmem_limit_bytes=VMEM_LIMIT),
+        name="prepare",
+    )(index.reshape(frames_dev, max_slots))
+
     edge_rows = -(-CHANNELS * groups // 16) * 16
     inner_rows = CHANNELS * BLK_DEV * groups
     picked, *edges = pl.pallas_call(

time: 25.8 us -> 25.4 us (0.984)
  local copies, waits for them, and re-layouts: 2.92 us -> 0.02 us
  waiting for transfers between devices: 8.1 us -> 9.83 us
  starting transfers between devices: 9.83 us -> 11.2 us
  other arithmetic: 1.57 us -> 0.88 us
    unnamed x4 -> x8, local copies, waits for them, and re-layouts: 2.19 us -> 0.02 us
    ppermute x5 -> x6, waiting for transfers between devices: 3.83 us -> 5.56 us  [swap(): return lax.ppermute(rows, 'brick', [(i, i ^ step) for i in range(bricks)])]
    ppermute x5 -> x6, starting transfers between devices: 7.73 us -> 9.13 us  [swap(): return lax.ppermute(rows, 'brick', [(i, i ^ step) for i in range(bricks)])]
    concatenate x2 -> x1, other arithmetic: 0.78 us -> 0.01 us  [gather_half(): three = jnp.concatenate(parts, axis=0)]
    concatenate x1 -> x0, local copies, waits for them, and re-layouts: 0.73 us -> none  [on_device(): jnp.concatenate(indices, axis=0)]
  transfers between devices with their start and end apart: 8 -> 9, of which waited for: 6 -> 6; matrix products, arithmetic and copies ran while one was open for 6% -> 0% of each run, Pallas kernels for 4% -> 4%
where the time goes in v4:
time: 25.4 us; the launch traced here: 25.2 us
  starting transfers between devices  11.2 us (44%)
  waiting for transfers between devices  9.83 us (39%)
  Pallas kernels  2.52 us (10%)
  other arithmetic  0.88 us (3%)
  between operations  0.73 us (3%)
    ppermute x6, starting transfers between devices, swap(): return lax.ppermute(rows, 'brick', [(i, i ^ step) for i in range(bricks)])  9.13 us
    ppermute x6, waiting for transfers between devices, swap(): return lax.ppermute(rows, 'brick', [(i, i ^ step) for i in range(bricks)])  5.56 us
    ppermute x1, waiting for transfers between devices, on_device(): handed = lax.ppermute(overhang, ('frame', 'brick'), turn)  3.6 us
    ppermute x2, starting transfers between devices, to_owner(): lax.ppermute(parts[step], 'frame', [(i, (i + step) % groups) for i in ran...  2.1 us
    pallas_call x1, Pallas kernels, on_device(): pl.pallas_call(functools.partial(inner_kernel, frames_dev, max_slots, gro...  0.85 us
    another operation x2, other arithmetic, on_device(): local_rows = jnp.stack([intensity, correction], axis=0).astype(jnp.bfloat16)  0.79 us
    pallas_call x1, Pallas kernels, on_device(): pl.pallas_call(functools.partial(edge_kernel, frames_dev, max_slots, grou...  0.77 us
    ppermute x2, waiting for transfers between devices, to_owner(): lax.ppermute(parts[step], 'frame', [(i, (i + step) % groups) for i in ran...  0.66 us
  transfers between devices with their start and end apart: 9, of which 6 were waited for; matrix products, arithmetic and copies ran while one was open for 0% of the time, Pallas kernels for 4%

profile of v4, /device:TPU:0, one launch (start us, length us, event | category | flops | bytes accessed | tf_op | source)
XLA Modules:
  0.0 25.2 jit_solution(8774041579976751954)
XLA Ops:
  0.6 0.8 %convert_bitcast_fusion = (bf16[1,4,16,128]{3,2,1,0:T(8,128)(2,1)S(1)}, bf16[1,4,16,128]{3,2,1,0:T(8,128)(2,1)S(1)}) fusion(f32[4,16,128]{2,1,0:T(8,128)} %param.7, f32[4,16,128]{2,1,0:T(8,128)} %param.6), kind=kLoop, calls=%fused_computation.2 | loop fusion | flops 16384 | bytes 98304 | tf_op jit(solution)/shard_map/stack | solution.py:195
  1.4 3.0 %collective-permute-start.1 = (bf16[1,128,128]{2,1,0:T(8,128)(2,1)S(1)}, bf16[1,128,128]{2,1,0:T(8,128)(2,1)S(1)}, u32[]{:S(2)}, u32[]{:S(2)}) collective-permute-start(bf16[1,128,128]{2,1,0:T(8,128)(2,1)S(1)} %bitcast.13), channel_id=1, source_target_pairs={{0,2},{1,3},{2,0},{3,1},{4,6},{5,7},{6,4},{7,5},{8,10},{9,11},{10,... | collective-permute-start | bytes 98312 | tf_op jit(solution)/shard_map/ppermute | solution.py:38
  4.5 2.6 %collective-permute-start = (bf16[1,128,128]{2,1,0:T(8,128)(2,1)S(1)}, bf16[1,128,128]{2,1,0:T(8,128)(2,1)S(1)}, u32[]{:S(2)}, u32[]{:S(2)}) collective-permute-start(bf16[1,128,128]{2,1,0:T(8,128)(2,1)S(1)} %bitcast.14), channel_id=1, source_target_pairs={{0,8},{1,9},{2,10},{3,11},{4,12},{5,13},{6,14},{7,15},{8,0},{9,1},... | collective-permute-start | bytes 98312 | tf_op jit(solution)/shard_map/ppermute | solution.py:38
  7.0 1.3 %collective-permute-start.4 = (bf16[1,128,128]{2,1,0:T(8,128)(2,1)S(1)}, bf16[1,128,128]{2,1,0:T(8,128)(2,1)S(1)}, u32[]{:S(2)}, u32[]{:S(2)}) collective-permute-start(bf16[1,128,128]{2,1,0:T(8,128)(2,1)S(1)} %bitcast.15), channel_id=1, source_target_pairs={{0,14},{1,15},{2,12},{3,13},{4,10},{5,11},{6,8},{7,9},{8,6},{9,7},... | collective-permute-start | bytes 98312 | tf_op jit(solution)/shard_map/ppermute | solution.py:38
  8.3 0.0 collective-permute-done.1
  8.3 0.9 %collective-permute-done = bf16[1,128,128]{2,1,0:T(8,128)(2,1)S(1)} collective-permute-done((bf16[1,128,128]{2,1,0:T(8,128)(2,1)S(1)}, bf16[1,128,128]{2,1,0:T(8,128)(2,1)S(1)}, u32[]{:S(2)}, u32[]{:S(2)}) %collective-permute-start) | collective-permute-done | bytes 32800 | tf_op jit(solution)/shard_map/ppermute | solution.py:38
  9.3 1.7 %collective-permute-start.2 = (bf16[3,128,128]{2,1,0:T(8,128)(2,1)S(1)}, bf16[3,128,128]{2,1,0:T(8,128)(2,1)S(1)}, u32[]{:S(2)}, u32[]{:S(2)}) collective-permute-start(bf16[3,128,128]{2,1,0:T(8,128)(2,1)S(1)} %pad_maximum_fusion.refs_0_), channel_id=1, source_target_pairs={{0,4},{1,5},{2,6},{3,7},{4,0},{5,1},{6,2},{7,3},{8,12},{9,13},{10,... | collective-permute-start | bytes 294920 | tf_op jit(solution)/shard_map/ppermute | solution.py:38
  11.0 0.4 %collective-permute-start.3 = (bf16[1,128,128]{2,1,0:T(8,128)(2,1)S(1)}, bf16[1,128,128]{2,1,0:T(8,128)(2,1)S(1)}, u32[]{:S(2)}, u32[]{:S(2)}) collective-permute-start(bf16[1,128,128]{2,1,0:T(8,128)(2,1)S(1)} %collective-permute-done), channel_id=1, source_target_pairs={{0,2},{1,3},{2,0},{3,1},{4,6},{5,7},{6,4},{7,5},{8,10},{9,11},{10,... | collective-permute-start | bytes 98312 | tf_op jit(solution)/shard_map/ppermute | solution.py:38
  11.4 0.0 copy-start.1
  11.4 0.0 copy-start.2
  11.5 0.0 copy-start.3
  11.5 0.0 copy-start
  11.5 2.3 %collective-permute-done.4.refs_3_ = bf16[1,128,128]{2,1,0:T(8,128)(2,1)S(1)} collective-permute-done((bf16[1,128,128]{2,1,0:T(8,128)(2,1)S(1)}, bf16[1,128,128]{2,1,0:T(8,128)(2,1)S(1)}, u32[]{:S(2)}, u32[]{:S(2)}) %collective-permute-start.4) | collective-permute-done | bytes 32800 | tf_op jit(solution)/shard_map/ppermute | solution.py:38
  13.8 1.1 %collective-permute-done.3.refs_2_ = bf16[1,128,128]{2,1,0:T(8,128)(2,1)S(1)} collective-permute-done((bf16[1,128,128]{2,1,0:T(8,128)(2,1)S(1)}, bf16[1,128,128]{2,1,0:T(8,128)(2,1)S(1)}, u32[]{:S(2)}, u32[]{:S(2)}) %collective-permute-start.3) | collective-permute-done | bytes 32800 | tf_op jit(solution)/shard_map/ppermute | solution.py:38
  14.9 0.0 collective-permute-done.2.refs_1_
  15.0 0.1 collective-permute-start.5
  15.0 0.0 copy-done.1
  15.1 0.0 copy-done.2
  15.1 0.0 copy-done.3
  15.1 0.1 fusion
  15.2 0.2 prepare.1.meta_ref
  15.4 1.2 %collective-permute-done.5.far_ref = bf16[8,128,128]{2,1,0:T(8,128)(2,1)S(1)} collective-permute-done((bf16[8,128,128]{2,1,0:T(8,128)(2,1)S(1)}, bf16[8,128,128]{2,1,0:T(8,128)(2,1)S(1)}, u32[]{:S(2)}, u32[]{:S(2)}) %collective-permute-start.5) | collective-permute-done | bytes 262176 | tf_op jit(solution)/shard_map/ppermute | solution.py:38
  16.6 0.0 copy-done
  16.6 0.8 %edges.1 = (f32[64,128]{1,0:T(8,128)S(1)}, f32[2,512]{1,0:T(2,128)S(1)}, f32[2,512]{1,0:T(2,128)S(1)}) custom-call(bf16[8,128,128]{2,1,0:T(8,128)(2,1)S(1)} %join_rows.3.near_ref, bf16[8,128,128]{2,1,0:T(8,128)(2,1)S(1)} %collective-permute-done.5.far_ref, s32[128,128]{1,0:T(8,128)S(1)} %prepare.1.meta_ref, bf16[4096,512]{1,0:T(8,128)(2,1)S(1)} %bitcast.10), custom_call_target="tpu_custom_call" | custom-call | flops 67108864 | bytes 4194304 | tf_op jit(solution)/shard_map/edges/pallas_call | solution.py:221
  17.3 1.5 %collective-permute-start.6 = (f32[2,512]{1,0:T(2,128)S(1)}, f32[2,512]{1,0:T(2,128)S(1)}, u32[]{:S(2)}, u32[]{:S(2)}) collective-permute-start(f32[2,512]{1,0:T(2,128)S(1)} %get-tuple-element.18), channel_id=1, source_target_pairs={{0,16},{16,0},{1,17},{17,1},{2,18},{18,2},{3,19},{19,3},{4,20},{20... | collective-permute-start | bytes 12296 | tf_op jit(solution)/shard_map/ppermute | solution.py:249
  18.8 0.8 %inner.1 = (f32[32,512]{1,0:T(8,128)S(1)}, f32[32,512]{1,0:T(8,128)S(1)}) custom-call(f32[64,128]{1,0:T(8,128)S(1)} %get-tuple-element.19.picked_ref, s32[128,128]{1,0:T(8,128)S(1)} %prepare.1.meta_ref, bf16[4096,512]{1,0:T(8,128)(2,1)S(1)} %bitcast.11), custom_call_target="tpu_custom_call" | custom-call | flops 268435456 | bytes 4194304 | tf_op jit(solution)/shard_map/inner/pallas_call | solution.py:234
  19.7 0.6 %collective-permute-start.8 = (f32[32,512]{1,0:T(8,128)S(1)}, f32[32,512]{1,0:T(8,128)S(1)}, u32[]{:S(2)}, u32[]{:S(2)}) collective-permute-start(f32[32,512]{1,0:T(8,128)S(1)} %get-tuple-element.21), channel_id=1, source_target_pairs={{0,16},{16,0},{1,17},{17,1},{2,18},{18,2},{3,19},{19,3},{4,20},{20... | collective-permute-start | bytes 196616 | tf_op jit(solution)/shard_map/ppermute | solution.py:249
  20.3 0.7 %collective-permute-done.6.refs_1_ = f32[2,512]{1,0:T(2,128)S(1)} collective-permute-done((f32[2,512]{1,0:T(2,128)S(1)}, f32[2,512]{1,0:T(2,128)S(1)}, u32[]{:S(2)}, u32[]{:S(2)}) %collective-permute-start.6) | collective-permute-done | bytes 4128 | tf_op jit(solution)/shard_map/ppermute | solution.py:249
  21.0 0.0 collective-permute-start.7
  21.0 3.6 %collective-permute-done.7.handed_ref = f32[2,512]{1,0:T(2,128)S(1)} collective-permute-done((f32[2,512]{1,0:T(2,128)S(1)}, f32[2,512]{1,0:T(2,128)S(1)}, u32[]{:S(2)}, u32[]{:S(2)}) %collective-permute-start.7) | collective-permute-done | bytes 4128 | tf_op jit(solution)/shard_map/ppermute | solution.py:268
  24.6 0.0 collective-permute-done.8.refs_1_
  24.6 0.6 %finish.1 = (f32[16,512]{1,0:T(8,128)}, f32[16,512]{1,0:T(8,128)}) custom-call(f32[2,512]{1,0:T(2,128)S(1)} %collective-permute-done.7.handed_ref, f32[32,512]{1,0:T(8,128)S(1)} %get-tuple-element.20.refs_0_, f32[32,512]{1,0:T(8,128)S(1)} %collective-permute-done.8.refs_1_), custom_call_target="tpu_custom_call" | custom-call | tf_op jit(solution)/shard_map/finish/pallas_call | solution.py:269
  (5 shorter events, 0.0 us)
Async XLA Ops:
  1.4 6.9 %collective-permute-start.1 = (bf16[1,128,128]{2,1,0:T(8,128)(2,1)S(1)}, bf16[1,128,128]{2,1,0:T(8,128)(2,1)S(1)}, u32[]{:S(2)}, u32[]{:S(2)}) collective-permute-start(bf16[1,128,128]{2,1,0:T(8,128)(2,1)S(1)} %bitcast.13), channel_id=1, source_target_pairs={{0,2},{1,3},{2,0},{3,1},{4,6},{5,7},{6,4},{7,5},{8,10},{9,11},{10,... | collective-permute-start | bytes 98312 | tf_op jit(solution)/shard_map/ppermute | solution.py:38
  4.5 4.8 %collective-permute-start = (bf16[1,128,128]{2,1,0:T(8,128)(2,1)S(1)}, bf16[1,128,128]{2,1,0:T(8,128)(2,1)S(1)}, u32[]{:S(2)}, u32[]{:S(2)}) collective-permute-start(bf16[1,128,128]{2,1,0:T(8,128)(2,1)S(1)} %bitcast.14), channel_id=1, source_target_pairs={{0,8},{1,9},{2,10},{3,11},{4,12},{5,13},{6,14},{7,15},{8,0},{9,1},... | collective-permute-start | bytes 98312 | tf_op jit(solution)/shard_map/ppermute | solution.py:38
  7.0 6.8 %collective-permute-start.4 = (bf16[1,128,128]{2,1,0:T(8,128)(2,1)S(1)}, bf16[1,128,128]{2,1,0:T(8,128)(2,1)S(1)}, u32[]{:S(2)}, u32[]{:S(2)}) collective-permute-start(bf16[1,128,128]{2,1,0:T(8,128)(2,1)S(1)} %bitcast.15), channel_id=1, source_target_pairs={{0,14},{1,15},{2,12},{3,13},{4,10},{5,11},{6,8},{7,9},{8,6},{9,7},... | collective-permute-start | bytes 98312 | tf_op jit(solution)/shard_map/ppermute | solution.py:38
  9.3 5.7 %collective-permute-start.2 = (bf16[3,128,128]{2,1,0:T(8,128)(2,1)S(1)}, bf16[3,128,128]{2,1,0:T(8,128)(2,1)S(1)}, u32[]{:S(2)}, u32[]{:S(2)}) collective-permute-start(bf16[3,128,128]{2,1,0:T(8,128)(2,1)S(1)} %pad_maximum_fusion.refs_0_), channel_id=1, source_target_pairs={{0,4},{1,5},{2,6},{3,7},{4,0},{5,1},{6,2},{7,3},{8,12},{9,13},{10,... | collective-permute-start | bytes 294920 | tf_op jit(solution)/shard_map/ppermute | solution.py:38
  11.0 3.9 %collective-permute-start.3 = (bf16[1,128,128]{2,1,0:T(8,128)(2,1)S(1)}, bf16[1,128,128]{2,1,0:T(8,128)(2,1)S(1)}, u32[]{:S(2)}, u32[]{:S(2)}) collective-permute-start(bf16[1,128,128]{2,1,0:T(8,128)(2,1)S(1)} %collective-permute-done), channel_id=1, source_target_pairs={{0,2},{1,3},{2,0},{3,1},{4,6},{5,7},{6,4},{7,5},{8,10},{9,11},{10,... | collective-permute-start | bytes 98312 | tf_op jit(solution)/shard_map/ppermute | solution.py:38
  11.4 3.6 %copy-start.1 = (s32[4,1,8]{2,1,0:T(1,128)S(1)}, s32[4,1,8]{2,1,0:T(1,128)}, u32[]{:S(2)}) copy-start(s32[4,1,8]{2,1,0:T(1,128)} %param.11) | copy-start | bytes 388
  11.4 3.6 %copy-start.2 = (s32[4,1,8]{2,1,0:T(1,128)S(1)}, s32[4,1,8]{2,1,0:T(1,128)}, u32[]{:S(2)}) copy-start(s32[4,1,8]{2,1,0:T(1,128)} %param.10) | copy-start | bytes 388
  11.5 3.6 %copy-start.3 = (s32[4,1]{0,1:T(1,128)S(1)}, s32[4,1]{0,1:T(1,128)}, u32[]{:S(2)}) copy-start(s32[4,1]{0,1:T(1,128)} %param.9) | copy-start | bytes 52
  11.5 5.1 %copy-start = (bf16[4,1,8,128,512]{4,3,2,1,0:T(8,128)(2,1)S(1)}, bf16[4,1,8,128,512]{4,3,2,1,0:T(8,128)(2,1)}, u32[]{:S(2)}) copy-start(bf16[4,1,8,128,512]{4,3,2,1,0:T(8,128)(2,1)} %param.8) | copy-start | bytes 12582916
  15.0 1.6 %collective-permute-start.5 = (bf16[8,128,128]{2,1,0:T(8,128)(2,1)S(1)}, bf16[8,128,128]{2,1,0:T(8,128)(2,1)S(1)}, u32[]{:S(2)}, u32[]{:S(2)}) collective-permute-start(bf16[8,128,128]{2,1,0:T(8,128)(2,1)S(1)} %join_rows.3.near_ref), channel_id=1, source_target_pairs={{0,1},{1,0},{2,3},{3,2},{4,5},{5,4},{6,7},{7,6},{8,9},{9,8},{10,11... | collective-permute-start | bytes 786440 | tf_op jit(solution)/shard_map/ppermute | solution.py:38
  17.3 3.6 %collective-permute-start.6 = (f32[2,512]{1,0:T(2,128)S(1)}, f32[2,512]{1,0:T(2,128)S(1)}, u32[]{:S(2)}, u32[]{:S(2)}) collective-permute-start(f32[2,512]{1,0:T(2,128)S(1)} %get-tuple-element.18), channel_id=1, source_target_pairs={{0,16},{16,0},{1,17},{17,1},{2,18},{18,2},{3,19},{19,3},{4,20},{20... | collective-permute-start | bytes 12296 | tf_op jit(solution)/shard_map/ppermute | solution.py:249
  19.7 4.9 %collective-permute-start.8 = (f32[32,512]{1,0:T(8,128)S(1)}, f32[32,512]{1,0:T(8,128)S(1)}, u32[]{:S(2)}, u32[]{:S(2)}) collective-permute-start(f32[32,512]{1,0:T(8,128)S(1)} %get-tuple-element.21), channel_id=1, source_target_pairs={{0,16},{16,0},{1,17},{17,1},{2,18},{18,2},{3,19},{19,3},{4,20},{20... | collective-permute-start | bytes 196616 | tf_op jit(solution)/shard_map/ppermute | solution.py:249
  21.0 3.6 %collective-permute-start.7 = (f32[2,512]{1,0:T(2,128)S(1)}, f32[2,512]{1,0:T(2,128)S(1)}, u32[]{:S(2)}, u32[]{:S(2)}) collective-permute-start(f32[2,512]{1,0:T(2,128)S(1)} %sum_edges.1), channel_id=1, source_target_pairs={{0,1},{16,0},{1,2},{17,16},{2,3},{18,17},{3,4},{19,18},{4,5},{20,1... | collective-permute-start | bytes 12296 | tf_op jit(solution)/shard_map/ppermute | solution.py:268

commit v5 on v4

--- a/solution.py
+++ b/solution.py
@@ -13,18 +13,24 @@
 BLOCK_ROWS = CHANNELS * BLK_DEV + 8
 
 
-def join_kernel(*refs):
-    out_ref, at = refs[-1], 0
-    for ref in refs[:-1]:
+def join_kernel(spare, *refs):
+    refs, out_ref, at = refs[:-1], refs[-1], 0
+    for ref in refs if spare is None else refs[:-1]:
         out_ref[pl.ds(at, ref.shape[0])] = ref[...]
         at += ref.shape[0]
-
-
-def join(parts):
+    if spare is not None:
+        own = refs[-1]
+
+        @pl.when(lax.axis_index("brick") % 2 == 0)
+        def _():
+            out_ref[pl.ds(spare * own.shape[0], own.shape[0])] = own[...]
+
+
+def join(parts, spare=None):
     in_vmem = pl.BlockSpec(memory_space=pltpu.VMEM)
-    count = sum(part.shape[0] for part in parts)
+    count = sum(part.shape[0] for part in (parts if spare is None else parts[:-1]))
     return pl.pallas_call(
-        join_kernel,
+        functools.partial(join_kernel, spare),
         out_shape=jax.ShapeDtypeStruct((count,) + parts[0].shape[1:], parts[0].dtype),
         in_specs=[in_vmem] * len(parts),
         out_specs=in_vmem,
@@ -34,25 +40,30 @@
     )(*parts)
 
 
-def swap(rows, bricks, step):
-    return lax.ppermute(rows, "brick", [(i, i ^ step) for i in range(bricks)])
+def swap(rows, bricks, even, odd):
+    return lax.ppermute(rows, "brick", [(i, i ^ (odd if i % 2 else even)) for i in range(bricks)])
 
 
 def gather_half(rows, bricks):
-    held, distances = rows[None], [0]
+    held = rows[None]
     if bricks == 16:
-        parts = [held, swap(held, bricks, 8), swap(held, bricks, 2)]
-        corner = swap(held, bricks, 14)
-        three = jnp.concatenate(parts, axis=0)
-        parts = [join([three]), swap(three, bricks, 4), swap(parts[1], bricks, 2), corner]
-        distances = [0, 8, 2, 4, 12, 6, 10, 14]
-    else:
-        parts, step = [held], bricks // 2
-        while step > 1:
-            arrived = swap(jnp.concatenate(parts, axis=0), bricks, step)
-            parts, distances = parts + [arrived], distances + [d ^ step for d in distances]
-            step //= 2
-    return join(parts), distances + [d ^ 1 for d in distances]
+        held = jnp.concatenate([held, swap(held, bricks, 1, 1)], axis=0)
+        even, odd, spare = (2, 4, 2), (8, 14, 10), 2
+        arrived = {at: swap(held, bricks, even[at], odd[at]) for at in (0, 1, 2)}
+        arrived = [arrived[at] for at in range(len(even))]
+        handed = swap(arrived[0], bricks, 4, 4)
+        even, odd = even + (even[0] ^ 4,), odd + (odd[0] ^ 4,)
+        of_even = [d ^ c for at, d in enumerate(even) for d in (0 if at == spare else d,) for c in (0, 1)]
+        of_odd = [d ^ c for d in odd for c in (0, 1)]
+        of_even, of_odd = of_even + [d ^ 1 for d in of_odd], of_odd + [d ^ 1 for d in of_even]
+        return join([join(arrived[:1])] + arrived[1:] + [handed, held], spare), of_even, of_odd
+    parts, distances, step = [held], [0], bricks // 2
+    while step > 1:
+        arrived = swap(jnp.concatenate(parts, axis=0), bricks, step, step)
+        parts, distances = parts + [arrived], distances + [d ^ step for d in distances]
+        step //= 2
+    distances = distances + [d ^ 1 for d in distances]
+    return join(parts), distances, distances
 
 
 def place_of(distance, distances):
@@ -62,7 +73,7 @@
     return place
 
 
-def prepare_kernel(distances, per_owner, block_rows, bricks, groups, slots, index_ref, meta_ref):
+def prepare_kernel(of_even, of_odd, per_owner, block_rows, bricks, groups, slots, index_ref, meta_ref):
     brick, group = lax.axis_index("brick"), lax.axis_index("frame")
     frames = index_ref.shape[0]
     pair = slots * CHANNELS
@@ -78,7 +89,7 @@
         pixel_block = index // (block_rows + 3)
         offset = index - pixel_block * (block_rows + 3)
         owner = pixel_block // per_owner
-        place = place_of(owner ^ brick, distances)
+        place = jnp.where(brick % 2 == 0, place_of(owner ^ brick, of_even), place_of(owner ^ brick, of_odd))
         target = (place * CHANNELS + channel) * per_owner + (pixel_block - owner * per_owner)
         meta_ref[pl.ds(frame * pair, pair), :] = target
         low, high = offset == 0, offset == block_rows + 1
@@ -198,16 +209,16 @@
 
     split = splitting.reshape(depth, voxels)
 
-    near, distances = gather_half(local_rows, bricks)
+    near, of_even, of_odd = gather_half(local_rows, bricks)
     near, block_count, pix_index, vox_offset = lax.optimization_barrier(
         (near, block_count, pix_index, vox_offset)
     )
-    far = swap(near, bricks, 1)
+    far = swap(near, bricks, 1, 1)
     live = jnp.arange(max_slots, dtype=jnp.int32) < block_count[:, :, None]
     index = pix_index * (block_rows + 3) + jnp.where(live, vox_offset, block_rows + 2)
     meta = pl.pallas_call(
         functools.partial(
-            prepare_kernel, distances, blocks_per_device, block_rows, bricks, groups, max_slots
+            prepare_kernel, of_even, of_odd, blocks_per_device, block_rows, bricks, groups, max_slots
         ),
         out_shape=jax.ShapeDtypeStruct((2 * CHANNELS * slot_count, pixel_width), jnp.int32),
         in_specs=[in_vmem],

time: 25.4 us -> 24.6 us (0.969)
  waiting for transfers between devices: 9.83 us -> 8.46 us
  starting transfers between devices: 11.2 us -> 11.8 us
    ppermute x6, waiting for transfers between devices: 5.56 us -> 4.19 us  [swap(): lax.ppermute(rows, 'brick', [(i, i ^ (odd if i % 2 else even)) for i in r...]
    ppermute x6, starting transfers between devices: 9.13 us -> 9.63 us  [swap(): lax.ppermute(rows, 'brick', [(i, i ^ (odd if i % 2 else even)) for i in r...]
  transfers between devices with their start and end apart: 9 -> 9, of which waited for: 6 -> 6; matrix products, arithmetic and copies ran while one was open for 0% -> 0% of each run, Pallas kernels for 4% -> 5%
where the time goes in v5:
time: 24.6 us; the launch traced here: 24.4 us
  starting transfers between devices  11.8 us (48%)
  waiting for transfers between devices  8.46 us (34%)
  Pallas kernels  2.56 us (10%)
  other arithmetic  0.87 us (4%)
  between operations  0.7 us (3%)
    ppermute x6, starting transfers between devices, swap(): lax.ppermute(rows, 'brick', [(i, i ^ (odd if i % 2 else even)) for i in r...  9.63 us
    ppermute x6, waiting for transfers between devices, swap(): lax.ppermute(rows, 'brick', [(i, i ^ (odd if i % 2 else even)) for i in r...  4.19 us
    ppermute x1, waiting for transfers between devices, on_device(): handed = lax.ppermute(overhang, ('frame', 'brick'), turn)  3.6 us
    ppermute x2, starting transfers between devices, to_owner(): lax.ppermute(parts[step], 'frame', [(i, (i + step) % groups) for i in ran...  2.11 us
    pallas_call x1, Pallas kernels, on_device(): pl.pallas_call(functools.partial(inner_kernel, frames_dev, max_slots, gro...  0.85 us
    another operation x2, other arithmetic, on_device(): local_rows = jnp.stack([intensity, correction], axis=0).astype(jnp.bfloat16)  0.79 us
    pallas_call x1, Pallas kernels, on_device(): pl.pallas_call(functools.partial(edge_kernel, frames_dev, max_slots, grou...  0.76 us
    ppermute x2, waiting for transfers between devices, to_owner(): lax.ppermute(parts[step], 'frame', [(i, (i + step) % groups) for i in ran...  0.66 us
  transfers between devices with their start and end apart: 9, of which 6 were waited for; matrix products, arithmetic and copies ran while one was open for 0% of the time, Pallas kernels for 5%

profile of v5, /device:TPU:0, one launch (start us, length us, event | category | flops | bytes accessed | tf_op | source)
XLA Modules:
  0.0 24.4 jit_solution(6612019462200351669)
XLA Ops:
  0.6 0.8 %convert_bitcast_fusion = (bf16[1,4,16,128]{3,2,1,0:T(8,128)(2,1)S(1)}, bf16[1,4,16,128]{3,2,1,0:T(8,128)(2,1)S(1)}) fusion(f32[4,16,128]{2,1,0:T(8,128)} %param.7, f32[4,16,128]{2,1,0:T(8,128)} %param.6), kind=kLoop, calls=%fused_computation.2 | loop fusion | flops 16384 | bytes 98304 | tf_op jit(solution)/shard_map/stack | solution.py:206
  1.4 0.5 %collective-permute-start = (bf16[1,128,128]{2,1,0:T(8,128)(2,1)S(1)}, bf16[1,128,128]{2,1,0:T(8,128)(2,1)S(1)}, u32[]{:S(2)}, u32[]{:S(2)}) collective-permute-start(bf16[1,128,128]{2,1,0:T(8,128)(2,1)S(1)} %bitcast.13), channel_id=1, source_target_pairs={{0,1},{1,0},{2,3},{3,2},{4,5},{5,4},{6,7},{7,6},{8,9},{9,8},{10,11... | collective-permute-start | bytes 98312 | tf_op jit(solution)/shard_map/ppermute | solution.py:44
  1.9 0.9 %collective-permute-done = bf16[1,128,128]{2,1,0:T(8,128)(2,1)S(1)} collective-permute-done((bf16[1,128,128]{2,1,0:T(8,128)(2,1)S(1)}, bf16[1,128,128]{2,1,0:T(8,128)(2,1)S(1)}, u32[]{:S(2)}, u32[]{:S(2)}) %collective-permute-start) | collective-permute-done | bytes 32800 | tf_op jit(solution)/shard_map/ppermute | solution.py:44
  2.8 2.9 %collective-permute-start.1 = (bf16[2,128,128]{2,1,0:T(8,128)(2,1)S(1)}, bf16[2,128,128]{2,1,0:T(8,128)(2,1)S(1)}, u32[]{:S(2)}, u32[]{:S(2)}) collective-permute-start(bf16[2,128,128]{2,1,0:T(8,128)(2,1)S(1)} %pad_maximum_fusion.refs_4_), channel_id=1, source_target_pairs={{0,2},{1,9},{2,0},{3,11},{4,6},{5,13},{6,4},{7,15},{8,10},{9,1},{1... | collective-permute-start | bytes 196616 | tf_op jit(solution)/shard_map/ppermute | solution.py:44
  5.7 0.1 collective-permute-start.3
  5.8 2.0 %collective-permute-start.2 = (bf16[2,128,128]{2,1,0:T(8,128)(2,1)S(1)}, bf16[2,128,128]{2,1,0:T(8,128)(2,1)S(1)}, u32[]{:S(2)}, u32[]{:S(2)}) collective-permute-start(bf16[2,128,128]{2,1,0:T(8,128)(2,1)S(1)} %pad_maximum_fusion.refs_4_), channel_id=1, source_target_pairs={{0,4},{1,15},{2,6},{3,13},{4,0},{5,11},{6,2},{7,9},{8,12},{9,7},{1... | collective-permute-start | bytes 196616 | tf_op jit(solution)/shard_map/ppermute | solution.py:44
  7.8 0.2 collective-permute-done.1.refs_0_
  8.0 2.1 %collective-permute-start.4 = (bf16[2,128,128]{2,1,0:T(8,128)(2,1)S(1)}, bf16[2,128,128]{2,1,0:T(8,128)(2,1)S(1)}, u32[]{:S(2)}, u32[]{:S(2)}) collective-permute-start(bf16[2,128,128]{2,1,0:T(8,128)(2,1)S(1)} %collective-permute-done.1.refs_0_), channel_id=1, source_target_pairs={{0,4},{1,5},{2,6},{3,7},{4,0},{5,1},{6,2},{7,3},{8,12},{9,13},{10,... | collective-permute-start | bytes 196616 | tf_op jit(solution)/shard_map/ppermute | solution.py:44
  10.1 0.0 copy-start.1
  10.1 0.0 copy-start.2
  10.1 0.0 copy-start.3
  10.1 0.0 copy-start
  10.1 0.0 collective-permute-done.3.refs_2_
  10.1 0.0 collective-permute-done.2.refs_1_
  10.1 2.4 %collective-permute-done.4.refs_3_ = bf16[2,128,128]{2,1,0:T(8,128)(2,1)S(1)} collective-permute-done((bf16[2,128,128]{2,1,0:T(8,128)(2,1)S(1)}, bf16[2,128,128]{2,1,0:T(8,128)(2,1)S(1)}, u32[]{:S(2)}, u32[]{:S(2)}) %collective-permute-start.4) | collective-permute-done | bytes 65568 | tf_op jit(solution)/shard_map/ppermute | solution.py:44
  12.5 2.0 %collective-permute-start.5 = (bf16[8,128,128]{2,1,0:T(8,128)(2,1)S(1)}, bf16[8,128,128]{2,1,0:T(8,128)(2,1)S(1)}, u32[]{:S(2)}, u32[]{:S(2)}) collective-permute-start(bf16[8,128,128]{2,1,0:T(8,128)(2,1)S(1)} %join_rows.3.near_ref), channel_id=1, source_target_pairs={{0,1},{1,0},{2,3},{3,2},{4,5},{5,4},{6,7},{7,6},{8,9},{9,8},{10,11... | collective-permute-start | bytes 786440 | tf_op jit(solution)/shard_map/ppermute | solution.py:44
  14.5 0.0 copy-done.1
  14.6 0.0 copy-done.2
  14.6 0.0 copy-done.3
  14.6 0.1 fusion
  14.6 0.3 %prepare.1.meta_ref = s32[128,128]{1,0:T(8,128)S(1)} custom-call(s32[4,8]{1,0:T(4,128)S(1)} %bitcast.12), custom_call_target="tpu_custom_call" | custom-call | tf_op jit(solution)/shard_map/prepare/pallas_call | solution.py:219
  14.9 0.8 %collective-permute-done.5.far_ref = bf16[8,128,128]{2,1,0:T(8,128)(2,1)S(1)} collective-permute-done((bf16[8,128,128]{2,1,0:T(8,128)(2,1)S(1)}, bf16[8,128,128]{2,1,0:T(8,128)(2,1)S(1)}, u32[]{:S(2)}, u32[]{:S(2)}) %collective-permute-start.5) | collective-permute-done | bytes 262176 | tf_op jit(solution)/shard_map/ppermute | solution.py:44
  15.7 0.0 copy-done
  15.7 0.8 %edges.1 = (f32[64,128]{1,0:T(8,128)S(1)}, f32[2,512]{1,0:T(2,128)S(1)}, f32[2,512]{1,0:T(2,128)S(1)}) custom-call(bf16[8,128,128]{2,1,0:T(8,128)(2,1)S(1)} %join_rows.3.near_ref, bf16[8,128,128]{2,1,0:T(8,128)(2,1)S(1)} %collective-permute-done.5.far_ref, s32[128,128]{1,0:T(8,128)S(1)} %prepare.1.meta_ref, bf16[4096,512]{1,0:T(8,128)(2,1)S(1)} %bitcast.10), custom_call_target="tpu_custom_call" | custom-call | flops 67108864 | bytes 4194304 | tf_op jit(solution)/shard_map/edges/pallas_call | solution.py:232
  16.5 1.5 %collective-permute-start.6 = (f32[2,512]{1,0:T(2,128)S(1)}, f32[2,512]{1,0:T(2,128)S(1)}, u32[]{:S(2)}, u32[]{:S(2)}) collective-permute-start(f32[2,512]{1,0:T(2,128)S(1)} %get-tuple-element.18), channel_id=1, source_target_pairs={{0,16},{16,0},{1,17},{17,1},{2,18},{18,2},{3,19},{19,3},{4,20},{20... | collective-permute-start | bytes 12296 | tf_op jit(solution)/shard_map/ppermute | solution.py:260
  18.0 0.8 %inner.1 = (f32[32,512]{1,0:T(8,128)S(1)}, f32[32,512]{1,0:T(8,128)S(1)}) custom-call(f32[64,128]{1,0:T(8,128)S(1)} %get-tuple-element.19.picked_ref, s32[128,128]{1,0:T(8,128)S(1)} %prepare.1.meta_ref, bf16[4096,512]{1,0:T(8,128)(2,1)S(1)} %bitcast.11), custom_call_target="tpu_custom_call" | custom-call | flops 268435456 | bytes 4194304 | tf_op jit(solution)/shard_map/inner/pallas_call | solution.py:245
  18.8 0.6 %collective-permute-start.8 = (f32[32,512]{1,0:T(8,128)S(1)}, f32[32,512]{1,0:T(8,128)S(1)}, u32[]{:S(2)}, u32[]{:S(2)}) collective-permute-start(f32[32,512]{1,0:T(8,128)S(1)} %get-tuple-element.21), channel_id=1, source_target_pairs={{0,16},{16,0},{1,17},{17,1},{2,18},{18,2},{3,19},{19,3},{4,20},{20... | collective-permute-start | bytes 196616 | tf_op jit(solution)/shard_map/ppermute | solution.py:260
  19.4 0.7 %collective-permute-done.6.refs_1_ = f32[2,512]{1,0:T(2,128)S(1)} collective-permute-done((f32[2,512]{1,0:T(2,128)S(1)}, f32[2,512]{1,0:T(2,128)S(1)}, u32[]{:S(2)}, u32[]{:S(2)}) %collective-permute-start.6) | collective-permute-done | bytes 4128 | tf_op jit(solution)/shard_map/ppermute | solution.py:260
  20.1 0.0 collective-permute-start.7
  20.1 3.6 %collective-permute-done.7.handed_ref = f32[2,512]{1,0:T(2,128)S(1)} collective-permute-done((f32[2,512]{1,0:T(2,128)S(1)}, f32[2,512]{1,0:T(2,128)S(1)}, u32[]{:S(2)}, u32[]{:S(2)}) %collective-permute-start.7) | collective-permute-done | bytes 4128 | tf_op jit(solution)/shard_map/ppermute | solution.py:279
  23.7 0.0 collective-permute-done.8.refs_1_
  23.7 0.6 %finish.1 = (f32[16,512]{1,0:T(8,128)}, f32[16,512]{1,0:T(8,128)}) custom-call(f32[2,512]{1,0:T(2,128)S(1)} %collective-permute-done.7.handed_ref, f32[32,512]{1,0:T(8,128)S(1)} %get-tuple-element.20.refs_0_, f32[32,512]{1,0:T(8,128)S(1)} %collective-permute-done.8.refs_1_), custom_call_target="tpu_custom_call" | custom-call | tf_op jit(solution)/shard_map/finish/pallas_call | solution.py:280
  (5 shorter events, 0.0 us)
Async XLA Ops:
  1.4 1.4 %collective-permute-start = (bf16[1,128,128]{2,1,0:T(8,128)(2,1)S(1)}, bf16[1,128,128]{2,1,0:T(8,128)(2,1)S(1)}, u32[]{:S(2)}, u32[]{:S(2)}) collective-permute-start(bf16[1,128,128]{2,1,0:T(8,128)(2,1)S(1)} %bitcast.13), channel_id=1, source_target_pairs={{0,1},{1,0},{2,3},{3,2},{4,5},{5,4},{6,7},{7,6},{8,9},{9,8},{10,11... | collective-permute-start | bytes 98312 | tf_op jit(solution)/shard_map/ppermute | solution.py:44
  2.8 5.2 %collective-permute-start.1 = (bf16[2,128,128]{2,1,0:T(8,128)(2,1)S(1)}, bf16[2,128,128]{2,1,0:T(8,128)(2,1)S(1)}, u32[]{:S(2)}, u32[]{:S(2)}) collective-permute-start(bf16[2,128,128]{2,1,0:T(8,128)(2,1)S(1)} %pad_maximum_fusion.refs_4_), channel_id=1, source_target_pairs={{0,2},{1,9},{2,0},{3,11},{4,6},{5,13},{6,4},{7,15},{8,10},{9,1},{1... | collective-permute-start | bytes 196616 | tf_op jit(solution)/shard_map/ppermute | solution.py:44
  5.7 4.4 %collective-permute-start.3 = (bf16[2,128,128]{2,1,0:T(8,128)(2,1)S(1)}, bf16[2,128,128]{2,1,0:T(8,128)(2,1)S(1)}, u32[]{:S(2)}, u32[]{:S(2)}) collective-permute-start(bf16[2,128,128]{2,1,0:T(8,128)(2,1)S(1)} %pad_maximum_fusion.refs_4_), channel_id=1, source_target_pairs={{0,2},{1,11},{2,0},{3,9},{4,6},{5,15},{6,4},{7,13},{8,10},{9,3},{1... | collective-permute-start | bytes 196616 | tf_op jit(solution)/shard_map/ppermute | solution.py:44
  5.8 4.3 %collective-permute-start.2 = (bf16[2,128,128]{2,1,0:T(8,128)(2,1)S(1)}, bf16[2,128,128]{2,1,0:T(8,128)(2,1)S(1)}, u32[]{:S(2)}, u32[]{:S(2)}) collective-permute-start(bf16[2,128,128]{2,1,0:T(8,128)(2,1)S(1)} %pad_maximum_fusion.refs_4_), channel_id=1, source_target_pairs={{0,4},{1,15},{2,6},{3,13},{4,0},{5,11},{6,2},{7,9},{8,12},{9,7},{1... | collective-permute-start | bytes 196616 | tf_op jit(solution)/shard_map/ppermute | solution.py:44
  8.0 4.5 %collective-permute-start.4 = (bf16[2,128,128]{2,1,0:T(8,128)(2,1)S(1)}, bf16[2,128,128]{2,1,0:T(8,128)(2,1)S(1)}, u32[]{:S(2)}, u32[]{:S(2)}) collective-permute-start(bf16[2,128,128]{2,1,0:T(8,128)(2,1)S(1)} %collective-permute-done.1.refs_0_), channel_id=1, source_target_pairs={{0,4},{1,5},{2,6},{3,7},{4,0},{5,1},{6,2},{7,3},{8,12},{9,13},{10,... | collective-permute-start | bytes 196616 | tf_op jit(solution)/shard_map/ppermute | solution.py:44
  10.1 4.5 %copy-start.1 = (s32[4,1,8]{2,1,0:T(1,128)S(1)}, s32[4,1,8]{2,1,0:T(1,128)}, u32[]{:S(2)}) copy-start(s32[4,1,8]{2,1,0:T(1,128)} %param.11) | copy-start | bytes 388
  10.1 4.5 %copy-start.2 = (s32[4,1,8]{2,1,0:T(1,128)S(1)}, s32[4,1,8]{2,1,0:T(1,128)}, u32[]{:S(2)}) copy-start(s32[4,1,8]{2,1,0:T(1,128)} %param.10) | copy-start | bytes 388
  10.1 4.5 %copy-start.3 = (s32[4,1]{0,1:T(1,128)S(1)}, s32[4,1]{0,1:T(1,128)}, u32[]{:S(2)}) copy-start(s32[4,1]{0,1:T(1,128)} %param.9) | copy-start | bytes 52
  10.1 5.6 %copy-start = (bf16[4,1,8,128,512]{4,3,2,1,0:T(8,128)(2,1)S(1)}, bf16[4,1,8,128,512]{4,3,2,1,0:T(8,128)(2,1)}, u32[]{:S(2)}) copy-start(bf16[4,1,8,128,512]{4,3,2,1,0:T(8,128)(2,1)} %param.8) | copy-start | bytes 12582916
  12.5 3.2 %collective-permute-start.5 = (bf16[8,128,128]{2,1,0:T(8,128)(2,1)S(1)}, bf16[8,128,128]{2,1,0:T(8,128)(2,1)S(1)}, u32[]{:S(2)}, u32[]{:S(2)}) collective-permute-start(bf16[8,128,128]{2,1,0:T(8,128)(2,1)S(1)} %join_rows.3.near_ref), channel_id=1, source_target_pairs={{0,1},{1,0},{2,3},{3,2},{4,5},{5,4},{6,7},{7,6},{8,9},{9,8},{10,11... | collective-permute-start | bytes 786440 | tf_op jit(solution)/shard_map/ppermute | solution.py:44
  16.5 3.6 %collective-permute-start.6 = (f32[2,512]{1,0:T(2,128)S(1)}, f32[2,512]{1,0:T(2,128)S(1)}, u32[]{:S(2)}, u32[]{:S(2)}) collective-permute-start(f32[2,512]{1,0:T(2,128)S(1)} %get-tuple-element.18), channel_id=1, source_target_pairs={{0,16},{16,0},{1,17},{17,1},{2,18},{18,2},{3,19},{19,3},{4,20},{20... | collective-permute-start | bytes 12296 | tf_op jit(solution)/shard_map/ppermute | solution.py:260
  18.8 4.9 %collective-permute-start.8 = (f32[32,512]{1,0:T(8,128)S(1)}, f32[32,512]{1,0:T(8,128)S(1)}, u32[]{:S(2)}, u32[]{:S(2)}) collective-permute-start(f32[32,512]{1,0:T(8,128)S(1)} %get-tuple-element.21), channel_id=1, source_target_pairs={{0,16},{16,0},{1,17},{17,1},{2,18},{18,2},{3,19},{19,3},{4,20},{20... | collective-permute-start | bytes 196616 | tf_op jit(solution)/shard_map/ppermute | solution.py:260
  20.1 3.6 %collective-permute-start.7 = (f32[2,512]{1,0:T(2,128)S(1)}, f32[2,512]{1,0:T(2,128)S(1)}, u32[]{:S(2)}, u32[]{:S(2)}) collective-permute-start(f32[2,512]{1,0:T(2,128)S(1)} %sum_edges.1), channel_id=1, source_target_pairs={{0,1},{16,0},{1,2},{17,16},{2,3},{18,17},{3,4},{19,18},{4,5},{20,1... | collective-permute-start | bytes 12296 | tf_op jit(solution)/shard_map/ppermute | solution.py:279

commit v6 on v5

--- a/solution.py
+++ b/solution.py
@@ -44,15 +44,34 @@
     return lax.ppermute(rows, "brick", [(i, i ^ (odd if i % 2 else even)) for i in range(bricks)])
 
 
-def gather_half(rows, bricks):
+def pair_kernel(own_ref, *refs):
+    refs, out_ref = refs[:-1], refs[-1]
+    out_ref[0] = own_ref[...]
+    for at, ref in enumerate(refs):
+        out_ref[1, pl.ds(at * ref.shape[0], ref.shape[0]), :] = ref[...].astype(jnp.bfloat16)
+
+
+def pair_up(own, others):
+    in_vmem = pl.BlockSpec(memory_space=pltpu.VMEM)
+    return pl.pallas_call(
+        pair_kernel,
+        out_shape=jax.ShapeDtypeStruct((2,) + own.shape, own.dtype),
+        in_specs=[in_vmem] * (1 + len(others)),
+        out_specs=in_vmem,
+        compiler_params=pltpu.CompilerParams(vmem_limit_bytes=VMEM_LIMIT),
+        name="pair_rows",
+    )(own, *others)
+
+
+def gather_half(rows, exact, bricks):
     held = rows[None]
     if bricks == 16:
-        held = jnp.concatenate([held, swap(held, bricks, 1, 1)], axis=0)
-        even, odd, spare = (2, 4, 2), (8, 14, 10), 2
+        held = pair_up(rows, [swap(part, bricks, 1, 1) for part in exact])
+        even, odd, spare = (2, 2, 4), (8, 12, 14), 1
         arrived = {at: swap(held, bricks, even[at], odd[at]) for at in (0, 1, 2)}
         arrived = [arrived[at] for at in range(len(even))]
-        handed = swap(arrived[0], bricks, 4, 4)
-        even, odd = even + (even[0] ^ 4,), odd + (odd[0] ^ 4,)
+        handed = swap(arrived[0], bricks, 4, 2)
+        even, odd = even + (even[0] ^ 4,), odd + (odd[0] ^ 2,)
         of_even = [d ^ c for at, d in enumerate(even) for d in (0 if at == spare else d,) for c in (0, 1)]
         of_odd = [d ^ c for d in odd for c in (0, 1)]
         of_even, of_odd = of_even + [d ^ 1 for d in of_odd], of_odd + [d ^ 1 for d in of_even]
@@ -103,31 +122,37 @@
         meta_ref[pl.ds((frames + frame) * pair, pair), :] = jnp.where(live, goal, -1)
 
 
-def edge_kernel(frames, slots, groups, near_ref, far_ref, meta_ref, split_ref, *refs):
+def pick(frames, slots, frame, start, rows_ref, meta_ref):
+    count, per_brick, pixels = rows_ref.shape
+    per_owner = per_brick // (CHANNELS * frames)
+    reach = count * CHANNELS * per_owner
+    pair = CHANNELS * slots
+    lane = lax.broadcasted_iota(jnp.int32, (pair, pixels), 1) + start * CHANNELS * per_owner
+    target = meta_ref[pl.ds(frame * pair, pair), :]
+    chosen = jnp.concatenate(
+        [(target == lane + at).astype(jnp.float32) for at in range(0, reach, pixels)], axis=1
+    ).astype(jnp.bfloat16)
+    own = jnp.concatenate(
+        [rows_ref[:, pl.ds((c * frames + frame) * per_owner, per_owner), :] for c in range(CHANNELS)], axis=1
+    )
+    return jnp.dot(chosen, own.reshape(reach, pixels), preferred_element_type=jnp.float32)
+
+
+def pick_kernel(frames, slots, near_ref, meta_ref, picked_ref):
+    pair = CHANNELS * slots
+    for frame in range(frames):
+        picked_ref[pl.ds(frame * pair, pair), :] = pick(frames, slots, frame, 0, near_ref, meta_ref)
+
+
+def edge_kernel(frames, slots, groups, early_ref, far_ref, meta_ref, split_ref, *refs):
     picked_ref, edges, placed_ref = refs[0], refs[1 : 1 + groups], refs[1 + groups]
-    half, per_brick, pixels = near_ref.shape
-    per_owner = per_brick // (CHANNELS * frames)
-    reach = 2 * half * CHANNELS * per_owner
+    half, _, pixels = far_ref.shape
     pair = CHANNELS * slots
-    lane = lax.broadcasted_iota(jnp.int32, (pair, pixels), 1)
     row = lax.broadcasted_iota(jnp.int32, (placed_ref.shape[0], pixels), 0)
     row = row // CHANNELS * BLOCK_ROWS + CHANNELS * BLK_DEV + row % CHANNELS
     for frame in range(frames):
-        target = meta_ref[pl.ds(frame * pair, pair), :]
-        chosen = jnp.concatenate(
-            [(target == lane + start).astype(jnp.float32) for start in range(0, reach, pixels)], axis=1
-        ).astype(jnp.bfloat16)
-        own = jnp.concatenate(
-            [
-                jnp.concatenate(
-                    [ref[:, pl.ds((c * frames + frame) * per_owner, per_owner), :] for c in range(CHANNELS)],
-                    axis=1,
-                ).reshape(reach // 2, pixels)
-                for ref in (near_ref, far_ref)
-            ],
-            axis=0,
-        )
-        picked = jnp.dot(chosen, own, preferred_element_type=jnp.float32)
+        picked = early_ref[pl.ds(frame * pair, pair), :]
+        picked = picked + pick(frames, slots, frame, half, far_ref, meta_ref)
         picked_ref[pl.ds(frame * pair, pair), :] = picked
         goal = meta_ref[pl.ds((frames + frame) * pair, pair), :]
         for slot in range(slots):
@@ -203,13 +228,14 @@
 
     in_vmem = pl.BlockSpec(memory_space=pltpu.VMEM)
     row_count = frames_dev * blocks_per_device
-    local_rows = jnp.stack([intensity, correction], axis=0).astype(jnp.bfloat16)
-    local_rows = local_rows.reshape(CHANNELS * row_count, pixel_width)
+    exact = [part.reshape(row_count, pixel_width) for part in (intensity, correction)]
+    local_rows = jnp.pad(exact[0], ((0, row_count), (0, 0))) + jnp.pad(exact[1], ((row_count, 0), (0, 0)))
+    local_rows = local_rows.astype(jnp.bfloat16)
     depth = slot_count * pixel_width
 
     split = splitting.reshape(depth, voxels)
 
-    near, of_even, of_odd = gather_half(local_rows, bricks)
+    near, of_even, of_odd = gather_half(local_rows, exact, bricks)
     near, block_count, pix_index, vox_offset = lax.optimization_barrier(
         (near, block_count, pix_index, vox_offset)
     )
@@ -227,6 +253,14 @@
         name="prepare",
     )(index.reshape(frames_dev, max_slots))
 
+    early = pl.pallas_call(
+        functools.partial(pick_kernel, frames_dev, max_slots),
+        out_shape=jax.ShapeDtypeStruct((CHANNELS * slot_count, pixel_width), jnp.float32),
+        in_specs=[in_vmem] * 2,
+        out_specs=in_vmem,
+        compiler_params=pltpu.CompilerParams(vmem_limit_bytes=VMEM_LIMIT),
+        name="pick_near",
+    )(near, meta)
     edge_rows = -(-CHANNELS * groups // 16) * 16
     inner_rows = CHANNELS * BLK_DEV * groups
     picked, *edges = pl.pallas_call(
@@ -241,7 +275,7 @@
             flops=2 * edge_rows * depth * voxels, bytes_accessed=2 * depth * voxels, transcendentals=0
         ),
         name="edges",
-    )(near, far, meta, split)
+    )(early, far, meta, split)
     blocks = pl.pallas_call(
         functools.partial(inner_kernel, frames_dev, max_slots, groups),
         out_shape=[jax.ShapeDtypeStruct((CHANNELS * BLK_DEV, voxels), jnp.float32)] * groups,

time: 24.6 us -> 23.9 us (0.972)
  waiting for transfers between devices: 8.46 us -> 7.85 us
    another operation x2 -> x0, other arithmetic: 0.79 us -> none  [on_device(): local_rows = jnp.stack([intensity, correction], axis=0).astype(jnp.bfloat16)]
    convert_element_type x0 -> x1, other arithmetic: none -> 0.78 us  [on_device(): local_rows = local_rows.astype(jnp.bfloat16)]
    ppermute x6 -> x7, waiting for transfers between devices: 4.19 us -> 3.58 us  [swap(): lax.ppermute(rows, 'brick', [(i, i ^ (odd if i % 2 else even)) for i in r...]
    ppermute x6 -> x7, starting transfers between devices: 9.63 us -> 9.46 us  [swap(): lax.ppermute(rows, 'brick', [(i, i ^ (odd if i % 2 else even)) for i in r...]
  transfers between devices with their start and end apart: 9 -> 10, of which waited for: 6 -> 8; matrix products, arithmetic and copies ran while one was open for 0% -> 4% of each run, Pallas kernels for 5% -> 5%
where the time goes in v6:
time: 23.9 us; the launch traced here: 23.7 us
  starting transfers between devices  11.6 us (49%)
  waiting for transfers between devices  7.85 us (33%)
  Pallas kernels  2.71 us (11%)
  other arithmetic  0.85 us (4%)
  between operations  0.69 us (3%)
    ppermute x7, starting transfers between devices, swap(): lax.ppermute(rows, 'brick', [(i, i ^ (odd if i % 2 else even)) for i in r...  9.46 us
    ppermute x1, waiting for transfers between devices, on_device(): handed = lax.ppermute(overhang, ('frame', 'brick'), turn)  3.6 us
    ppermute x7, waiting for transfers between devices, swap(): lax.ppermute(rows, 'brick', [(i, i ^ (odd if i % 2 else even)) for i in r...  3.58 us
    ppermute x2, starting transfers between devices, to_owner(): lax.ppermute(parts[step], 'frame', [(i, (i + step) % groups) for i in ran...  2.11 us
    pallas_call x1, Pallas kernels, on_device(): pl.pallas_call(functools.partial(inner_kernel, frames_dev, max_slots, gro...  0.85 us
    convert_element_type x1, other arithmetic, on_device(): local_rows = local_rows.astype(jnp.bfloat16)  0.78 us
    pallas_call x1, Pallas kernels, on_device(): pl.pallas_call(functools.partial(edge_kernel, frames_dev, max_slots, grou...  0.76 us
    ppermute x2, waiting for transfers between devices, to_owner(): lax.ppermute(parts[step], 'frame', [(i, (i + step) % groups) for i in ran...  0.67 us
  transfers between devices with their start and end apart: 10, of which 8 were waited for; matrix products, arithmetic and copies ran while one was open for 4% of the time, Pallas kernels for 5%

profile of v6, /device:TPU:0, one launch (start us, length us, event | category | flops | bytes accessed | tf_op | source)
XLA Modules:
  0.0 23.7 jit_solution(5367888816294033842)
XLA Ops:
  0.6 0.5 %collective-permute-start = (f32[64,128]{1,0:T(8,128)}, f32[64,128]{1,0:T(8,128)S(1)}, u32[]{:S(2)}, u32[]{:S(2)}) collective-permute-start(f32[64,128]{1,0:T(8,128)} %bitcast.10), channel_id=1, source_target_pairs={{0,1},{1,0},{2,3},{3,2},{4,5},{5,4},{6,7},{7,6},{8,9},{9,8},{10,11... | collective-permute-start | bytes 98312 | tf_op jit(solution)/shard_map/ppermute | solution.py:44
  1.1 0.1 collective-permute-start.1
  1.2 0.8 %add_convert_fusion.own_ref = bf16[128,128]{1,0:T(8,128)(2,1)S(1)} fusion(f32[64,128]{1,0:T(8,128)} %bitcast.13, f32[64,128]{1,0:T(8,128)} %bitcast.11), kind=kLoop, calls=%fused_computation | loop fusion | flops 32768 | bytes 98304 | tf_op jit(solution)/shard_map/convert_element_type | solution.py:233
  2.0 0.2 collective-permute-done.refs_0_
  2.2 0.3 %collective-permute-done.1.refs_1_ = f32[64,128]{1,0:T(8,128)S(1)} collective-permute-done((f32[64,128]{1,0:T(8,128)}, f32[64,128]{1,0:T(8,128)S(1)}, u32[]{:S(2)}, u32[]{:S(2)}) %collective-permute-start.1) | collective-permute-done | bytes 32800 | tf_op jit(solution)/shard_map/ppermute | solution.py:44
  2.6 2.7 %collective-permute-start.2 = (bf16[2,128,128]{2,1,0:T(8,128)(2,1)S(1)}, bf16[2,128,128]{2,1,0:T(8,128)(2,1)S(1)}, u32[]{:S(2)}, u32[]{:S(2)}) collective-permute-start(bf16[2,128,128]{2,1,0:T(8,128)(2,1)S(1)} %pair_rows.1.refs_4_), channel_id=1, source_target_pairs={{0,2},{1,9},{2,0},{3,11},{4,6},{5,13},{6,4},{7,15},{8,10},{9,1},{1... | collective-permute-start | bytes 196616 | tf_op jit(solution)/shard_map/ppermute | solution.py:44
  5.3 1.6 %collective-permute-start.4 = (bf16[2,128,128]{2,1,0:T(8,128)(2,1)S(1)}, bf16[2,128,128]{2,1,0:T(8,128)(2,1)S(1)}, u32[]{:S(2)}, u32[]{:S(2)}) collective-permute-start(bf16[2,128,128]{2,1,0:T(8,128)(2,1)S(1)} %pair_rows.1.refs_4_), channel_id=1, source_target_pairs={{0,4},{1,15},{2,6},{3,13},{4,0},{5,11},{6,2},{7,9},{8,12},{9,7},{1... | collective-permute-start | bytes 196616 | tf_op jit(solution)/shard_map/ppermute | solution.py:44
  6.9 0.5 %collective-permute-start.3 = (bf16[2,128,128]{2,1,0:T(8,128)(2,1)S(1)}, bf16[2,128,128]{2,1,0:T(8,128)(2,1)S(1)}, u32[]{:S(2)}, u32[]{:S(2)}) collective-permute-start(bf16[2,128,128]{2,1,0:T(8,128)(2,1)S(1)} %pair_rows.1.refs_4_), channel_id=1, source_target_pairs={{0,2},{1,13},{2,0},{3,15},{4,6},{5,9},{6,4},{7,11},{8,10},{9,5},{1... | collective-permute-start | bytes 196616 | tf_op jit(solution)/shard_map/ppermute | solution.py:44
  7.4 0.2 collective-permute-done.2.refs_0_
  7.5 2.1 %collective-permute-start.5 = (bf16[2,128,128]{2,1,0:T(8,128)(2,1)S(1)}, bf16[2,128,128]{2,1,0:T(8,128)(2,1)S(1)}, u32[]{:S(2)}, u32[]{:S(2)}) collective-permute-start(bf16[2,128,128]{2,1,0:T(8,128)(2,1)S(1)} %collective-permute-done.2.refs_0_), channel_id=1, source_target_pairs={{0,4},{1,3},{2,6},{3,1},{4,0},{5,7},{6,2},{7,5},{8,12},{9,11},{10,... | collective-permute-start | bytes 196616 | tf_op jit(solution)/shard_map/ppermute | solution.py:44
  9.6 0.0 copy-start.3
  9.6 0.0 copy-start
  9.7 0.0 collective-permute-done.4.refs_2_
  9.7 1.5 %collective-permute-done.3.refs_1_ = bf16[2,128,128]{2,1,0:T(8,128)(2,1)S(1)} collective-permute-done((bf16[2,128,128]{2,1,0:T(8,128)(2,1)S(1)}, bf16[2,128,128]{2,1,0:T(8,128)(2,1)S(1)}, u32[]{:S(2)}, u32[]{:S(2)}) %collective-permute-start.3) | collective-permute-done | bytes 65568 | tf_op jit(solution)/shard_map/ppermute | solution.py:44
  11.1 0.7 %collective-permute-done.5.refs_3_ = bf16[2,128,128]{2,1,0:T(8,128)(2,1)S(1)} collective-permute-done((bf16[2,128,128]{2,1,0:T(8,128)(2,1)S(1)}, bf16[2,128,128]{2,1,0:T(8,128)(2,1)S(1)}, u32[]{:S(2)}, u32[]{:S(2)}) %collective-permute-start.5) | collective-permute-done | bytes 65568 | tf_op jit(solution)/shard_map/ppermute | solution.py:44
  11.9 2.0 %collective-permute-start.6 = (bf16[8,128,128]{2,1,0:T(8,128)(2,1)S(1)}, bf16[8,128,128]{2,1,0:T(8,128)(2,1)S(1)}, u32[]{:S(2)}, u32[]{:S(2)}) collective-permute-start(bf16[8,128,128]{2,1,0:T(8,128)(2,1)S(1)} %join_rows.3.near_ref), channel_id=1, source_target_pairs={{0,1},{1,0},{2,3},{3,2},{4,5},{5,4},{6,7},{7,6},{8,9},{9,8},{10,11... | collective-permute-start | bytes 786440 | tf_op jit(solution)/shard_map/ppermute | solution.py:44
  13.9 0.0 copy-done.1
  13.9 0.0 copy-done.2
  13.9 0.0 copy-done.3
  13.9 0.1 fusion
  14.0 0.3 %prepare.1.meta_ref = s32[128,128]{1,0:T(8,128)S(1)} custom-call(s32[4,8]{1,0:T(4,128)S(1)} %bitcast.9), custom_call_target="tpu_custom_call" | custom-call | tf_op jit(solution)/shard_map/prepare/pallas_call | solution.py:245
  14.3 0.1 pick_near.1.early_ref
  14.4 0.6 %collective-permute-done.6.far_ref = bf16[8,128,128]{2,1,0:T(8,128)(2,1)S(1)} collective-permute-done((bf16[8,128,128]{2,1,0:T(8,128)(2,1)S(1)}, bf16[8,128,128]{2,1,0:T(8,128)(2,1)S(1)}, u32[]{:S(2)}, u32[]{:S(2)}) %collective-permute-start.6) | collective-permute-done | bytes 262176 | tf_op jit(solution)/shard_map/ppermute | solution.py:44
  15.1 0.8 %edges.1 = (f32[64,128]{1,0:T(8,128)S(1)}, f32[2,512]{1,0:T(2,128)S(1)}, f32[2,512]{1,0:T(2,128)S(1)}) custom-call(f32[64,128]{1,0:T(8,128)S(1)} %pick_near.1.early_ref, bf16[8,128,128]{2,1,0:T(8,128)(2,1)S(1)} %collective-permute-done.6.far_ref, s32[128,128]{1,0:T(8,128)S(1)} %prepare.1.meta_ref, bf16[4096,512]{1,0:T(8,128)(2,1)S(1)} %bitcast.7), custom_call_target="tpu_custom_call" | custom-call | flops 67108864 | bytes 4194304 | tf_op jit(solution)/shard_map/edges/pallas_call | solution.py:266
  15.8 1.8 %collective-permute-start.7 = (f32[2,512]{1,0:T(2,128)S(1)}, f32[2,512]{1,0:T(2,128)S(1)}, u32[]{:S(2)}, u32[]{:S(2)}) collective-permute-start(f32[2,512]{1,0:T(2,128)S(1)} %get-tuple-element.18), channel_id=1, source_target_pairs={{0,16},{16,0},{1,17},{17,1},{2,18},{18,2},{3,19},{19,3},{4,20},{20... | collective-permute-start | bytes 12296 | tf_op jit(solution)/shard_map/ppermute | solution.py:294
  17.6 0.8 %inner.1 = (f32[32,512]{1,0:T(8,128)S(1)}, f32[32,512]{1,0:T(8,128)S(1)}) custom-call(f32[64,128]{1,0:T(8,128)S(1)} %get-tuple-element.19.picked_ref, s32[128,128]{1,0:T(8,128)S(1)} %prepare.1.meta_ref, bf16[4096,512]{1,0:T(8,128)(2,1)S(1)} %bitcast.8), custom_call_target="tpu_custom_call" | custom-call | flops 268435456 | bytes 4194304 | tf_op jit(solution)/shard_map/inner/pallas_call | solution.py:279
  18.5 0.3 %collective-permute-start.9 = (f32[32,512]{1,0:T(8,128)S(1)}, f32[32,512]{1,0:T(8,128)S(1)}, u32[]{:S(2)}, u32[]{:S(2)}) collective-permute-start(f32[32,512]{1,0:T(8,128)S(1)} %get-tuple-element.21), channel_id=1, source_target_pairs={{0,16},{16,0},{1,17},{17,1},{2,18},{18,2},{3,19},{19,3},{4,20},{20... | collective-permute-start | bytes 196616 | tf_op jit(solution)/shard_map/ppermute | solution.py:294
  18.8 0.7 %collective-permute-done.7.refs_1_ = f32[2,512]{1,0:T(2,128)S(1)} collective-permute-done((f32[2,512]{1,0:T(2,128)S(1)}, f32[2,512]{1,0:T(2,128)S(1)}, u32[]{:S(2)}, u32[]{:S(2)}) %collective-permute-start.7) | collective-permute-done | bytes 4128 | tf_op jit(solution)/shard_map/ppermute | solution.py:294
  19.4 0.0 collective-permute-start.8
  19.5 3.6 %collective-permute-done.8.handed_ref = f32[2,512]{1,0:T(2,128)S(1)} collective-permute-done((f32[2,512]{1,0:T(2,128)S(1)}, f32[2,512]{1,0:T(2,128)S(1)}, u32[]{:S(2)}, u32[]{:S(2)}) %collective-permute-start.8) | collective-permute-done | bytes 4128 | tf_op jit(solution)/shard_map/ppermute | solution.py:313
  23.1 0.0 collective-permute-done.9.refs_1_
  23.1 0.6 %finish.1 = (f32[16,512]{1,0:T(8,128)}, f32[16,512]{1,0:T(8,128)}) custom-call(f32[2,512]{1,0:T(2,128)S(1)} %collective-permute-done.8.handed_ref, f32[32,512]{1,0:T(8,128)S(1)} %get-tuple-element.20.refs_0_, f32[32,512]{1,0:T(8,128)S(1)} %collective-permute-done.9.refs_1_), custom_call_target="tpu_custom_call" | custom-call | tf_op jit(solution)/shard_map/finish/pallas_call | solution.py:314
  (7 shorter events, 0.0 us)
Async XLA Ops:
  0.6 1.6 %collective-permute-start = (f32[64,128]{1,0:T(8,128)}, f32[64,128]{1,0:T(8,128)S(1)}, u32[]{:S(2)}, u32[]{:S(2)}) collective-permute-start(f32[64,128]{1,0:T(8,128)} %bitcast.10), channel_id=1, source_target_pairs={{0,1},{1,0},{2,3},{3,2},{4,5},{5,4},{6,7},{7,6},{8,9},{9,8},{10,11... | collective-permute-start | bytes 98312 | tf_op jit(solution)/shard_map/ppermute | solution.py:44
  1.1 1.4 %collective-permute-start.1 = (f32[64,128]{1,0:T(8,128)}, f32[64,128]{1,0:T(8,128)S(1)}, u32[]{:S(2)}, u32[]{:S(2)}) collective-permute-start(f32[64,128]{1,0:T(8,128)} %bitcast.12), channel_id=1, source_target_pairs={{0,1},{1,0},{2,3},{3,2},{4,5},{5,4},{6,7},{7,6},{8,9},{9,8},{10,11... | collective-permute-start | bytes 98312 | tf_op jit(solution)/shard_map/ppermute | solution.py:44
  2.6 5.0 %collective-permute-start.2 = (bf16[2,128,128]{2,1,0:T(8,128)(2,1)S(1)}, bf16[2,128,128]{2,1,0:T(8,128)(2,1)S(1)}, u32[]{:S(2)}, u32[]{:S(2)}) collective-permute-start(bf16[2,128,128]{2,1,0:T(8,128)(2,1)S(1)} %pair_rows.1.refs_4_), channel_id=1, source_target_pairs={{0,2},{1,9},{2,0},{3,11},{4,6},{5,13},{6,4},{7,15},{8,10},{9,1},{1... | collective-permute-start | bytes 196616 | tf_op jit(solution)/shard_map/ppermute | solution.py:44
  5.3 4.4 %collective-permute-start.4 = (bf16[2,128,128]{2,1,0:T(8,128)(2,1)S(1)}, bf16[2,128,128]{2,1,0:T(8,128)(2,1)S(1)}, u32[]{:S(2)}, u32[]{:S(2)}) collective-permute-start(bf16[2,128,128]{2,1,0:T(8,128)(2,1)S(1)} %pair_rows.1.refs_4_), channel_id=1, source_target_pairs={{0,4},{1,15},{2,6},{3,13},{4,0},{5,11},{6,2},{7,9},{8,12},{9,7},{1... | collective-permute-start | bytes 196616 | tf_op jit(solution)/shard_map/ppermute | solution.py:44
  6.9 4.3 %collective-permute-start.3 = (bf16[2,128,128]{2,1,0:T(8,128)(2,1)S(1)}, bf16[2,128,128]{2,1,0:T(8,128)(2,1)S(1)}, u32[]{:S(2)}, u32[]{:S(2)}) collective-permute-start(bf16[2,128,128]{2,1,0:T(8,128)(2,1)S(1)} %pair_rows.1.refs_4_), channel_id=1, source_target_pairs={{0,2},{1,13},{2,0},{3,15},{4,6},{5,9},{6,4},{7,11},{8,10},{9,5},{1... | collective-permute-start | bytes 196616 | tf_op jit(solution)/shard_map/ppermute | solution.py:44
  7.5 4.3 %collective-permute-start.5 = (bf16[2,128,128]{2,1,0:T(8,128)(2,1)S(1)}, bf16[2,128,128]{2,1,0:T(8,128)(2,1)S(1)}, u32[]{:S(2)}, u32[]{:S(2)}) collective-permute-start(bf16[2,128,128]{2,1,0:T(8,128)(2,1)S(1)} %collective-permute-done.2.refs_0_), channel_id=1, source_target_pairs={{0,4},{1,3},{2,6},{3,1},{4,0},{5,7},{6,2},{7,5},{8,12},{9,11},{10,... | collective-permute-start | bytes 196616 | tf_op jit(solution)/shard_map/ppermute | solution.py:44
  9.6 4.3 %copy-start.1 = (s32[4,1,8]{2,1,0:T(1,128)S(1)}, s32[4,1,8]{2,1,0:T(1,128)}, u32[]{:S(2)}) copy-start(s32[4,1,8]{2,1,0:T(1,128)} %param.11) | copy-start | bytes 388
  9.6 4.3 %copy-start.2 = (s32[4,1,8]{2,1,0:T(1,128)S(1)}, s32[4,1,8]{2,1,0:T(1,128)}, u32[]{:S(2)}) copy-start(s32[4,1,8]{2,1,0:T(1,128)} %param.10) | copy-start | bytes 388
  9.6 4.3 %copy-start.3 = (s32[4,1]{0,1:T(1,128)S(1)}, s32[4,1]{0,1:T(1,128)}, u32[]{:S(2)}) copy-start(s32[4,1]{0,1:T(1,128)} %param.9) | copy-start | bytes 52
  9.6 5.4 %copy-start = (bf16[4,1,8,128,512]{4,3,2,1,0:T(8,128)(2,1)S(1)}, bf16[4,1,8,128,512]{4,3,2,1,0:T(8,128)(2,1)}, u32[]{:S(2)}) copy-start(bf16[4,1,8,128,512]{4,3,2,1,0:T(8,128)(2,1)} %param.8) | copy-start | bytes 12582916
  11.9 3.2 %collective-permute-start.6 = (bf16[8,128,128]{2,1,0:T(8,128)(2,1)S(1)}, bf16[8,128,128]{2,1,0:T(8,128)(2,1)S(1)}, u32[]{:S(2)}, u32[]{:S(2)}) collective-permute-start(bf16[8,128,128]{2,1,0:T(8,128)(2,1)S(1)} %join_rows.3.near_ref), channel_id=1, source_target_pairs={{0,1},{1,0},{2,3},{3,2},{4,5},{5,4},{6,7},{7,6},{8,9},{9,8},{10,11... | collective-permute-start | bytes 786440 | tf_op jit(solution)/shard_map/ppermute | solution.py:44
  15.8 3.6 %collective-permute-start.7 = (f32[2,512]{1,0:T(2,128)S(1)}, f32[2,512]{1,0:T(2,128)S(1)}, u32[]{:S(2)}, u32[]{:S(2)}) collective-permute-start(f32[2,512]{1,0:T(2,128)S(1)} %get-tuple-element.18), channel_id=1, source_target_pairs={{0,16},{16,0},{1,17},{17,1},{2,18},{18,2},{3,19},{19,3},{4,20},{20... | collective-permute-start | bytes 12296 | tf_op jit(solution)/shard_map/ppermute | solution.py:294
  18.5 4.6 %collective-permute-start.9 = (f32[32,512]{1,0:T(8,128)S(1)}, f32[32,512]{1,0:T(8,128)S(1)}, u32[]{:S(2)}, u32[]{:S(2)}) collective-permute-start(f32[32,512]{1,0:T(8,128)S(1)} %get-tuple-element.21), channel_id=1, source_target_pairs={{0,16},{16,0},{1,17},{17,1},{2,18},{18,2},{3,19},{19,3},{4,20},{20... | collective-permute-start | bytes 196616 | tf_op jit(solution)/shard_map/ppermute | solution.py:294
  19.4 3.6 %collective-permute-start.8 = (f32[2,512]{1,0:T(2,128)S(1)}, f32[2,512]{1,0:T(2,128)S(1)}, u32[]{:S(2)}, u32[]{:S(2)}) collective-permute-start(f32[2,512]{1,0:T(2,128)S(1)} %sum_edges.1), channel_id=1, source_target_pairs={{0,1},{16,0},{1,2},{17,16},{2,3},{18,17},{3,4},{19,18},{4,5},{20,1... | collective-permute-start | bytes 12296 | tf_op jit(solution)/shard_map/ppermute | solution.py:313

commit v7 on v6

--- a/solution.py
+++ b/solution.py
@@ -67,7 +67,7 @@
     held = rows[None]
     if bricks == 16:
         held = pair_up(rows, [swap(part, bricks, 1, 1) for part in exact])
-        even, odd, spare = (2, 2, 4), (8, 12, 14), 1
+        even, odd, spare = (2, 4, 2), (8, 14, 12), 2
         arrived = {at: swap(held, bricks, even[at], odd[at]) for at in (0, 1, 2)}
         arrived = [arrived[at] for at in range(len(even))]
         handed = swap(arrived[0], bricks, 4, 2)
@@ -75,14 +75,14 @@
         of_even = [d ^ c for at, d in enumerate(even) for d in (0 if at == spare else d,) for c in (0, 1)]
         of_odd = [d ^ c for d in odd for c in (0, 1)]
         of_even, of_odd = of_even + [d ^ 1 for d in of_odd], of_odd + [d ^ 1 for d in of_even]
-        return join([join(arrived[:1])] + arrived[1:] + [handed, held], spare), of_even, of_odd
+        return [join(arrived[:2]), join([arrived[2], handed, held], 0)], of_even, of_odd
     parts, distances, step = [held], [0], bricks // 2
     while step > 1:
         arrived = swap(jnp.concatenate(parts, axis=0), bricks, step, step)
         parts, distances = parts + [arrived], distances + [d ^ step for d in distances]
         step //= 2
     distances = distances + [d ^ 1 for d in distances]
-    return join(parts), distances, distances
+    return [join(parts)], distances, distances
 
 
 def place_of(distance, distances):
@@ -138,21 +138,31 @@
     return jnp.dot(chosen, own.reshape(reach, pixels), preferred_element_type=jnp.float32)
 
 
-def pick_kernel(frames, slots, near_ref, meta_ref, picked_ref):
+def pick_all(frames, slots, frame, start, refs, meta_ref):
+    total = 0.0
+    for ref in refs:
+        total = total + pick(frames, slots, frame, start, ref, meta_ref)
+        start += ref.shape[0]
+    return total
+
+
+def pick_kernel(frames, slots, *refs):
+    near, (meta_ref, picked_ref) = refs[:-2], refs[-2:]
     pair = CHANNELS * slots
     for frame in range(frames):
-        picked_ref[pl.ds(frame * pair, pair), :] = pick(frames, slots, frame, 0, near_ref, meta_ref)
-
-
-def edge_kernel(frames, slots, groups, early_ref, far_ref, meta_ref, split_ref, *refs):
+        picked_ref[pl.ds(frame * pair, pair), :] = pick_all(frames, slots, frame, 0, near, meta_ref)
+
+
+def edge_kernel(frames, slots, groups, count, early_ref, *refs):
+    far, (meta_ref, split_ref), refs = refs[:count], refs[count : count + 2], refs[count + 2 :]
     picked_ref, edges, placed_ref = refs[0], refs[1 : 1 + groups], refs[1 + groups]
-    half, _, pixels = far_ref.shape
+    half, pixels = sum(ref.shape[0] for ref in far), far[0].shape[2]
     pair = CHANNELS * slots
     row = lax.broadcasted_iota(jnp.int32, (placed_ref.shape[0], pixels), 0)
     row = row // CHANNELS * BLOCK_ROWS + CHANNELS * BLK_DEV + row % CHANNELS
     for frame in range(frames):
         picked = early_ref[pl.ds(frame * pair, pair), :]
-        picked = picked + pick(frames, slots, frame, half, far_ref, meta_ref)
+        picked = picked + pick_all(frames, slots, frame, half, far, meta_ref)
         picked_ref[pl.ds(frame * pair, pair), :] = picked
         goal = meta_ref[pl.ds((frames + frame) * pair, pair), :]
         for slot in range(slots):
@@ -236,10 +246,10 @@
     split = splitting.reshape(depth, voxels)
 
     near, of_even, of_odd = gather_half(local_rows, exact, bricks)
-    near, block_count, pix_index, vox_offset = lax.optimization_barrier(
-        (near, block_count, pix_index, vox_offset)
-    )
-    far = swap(near, bricks, 1, 1)
+    *near, block_count, pix_index, vox_offset = lax.optimization_barrier(
+        (*near, block_count, pix_index, vox_offset)
+    ) if len(near) == 1 else (near[0], *lax.optimization_barrier((near[1], block_count, pix_index, vox_offset)))
+    far = [swap(part, bricks, 1, 1) for part in near]
     live = jnp.arange(max_slots, dtype=jnp.int32) < block_count[:, :, None]
     index = pix_index * (block_rows + 3) + jnp.where(live, vox_offset, block_rows + 2)
     meta = pl.pallas_call(
@@ -256,18 +266,18 @@
     early = pl.pallas_call(
         functools.partial(pick_kernel, frames_dev, max_slots),
         out_shape=jax.ShapeDtypeStruct((CHANNELS * slot_count, pixel_width), jnp.float32),
-        in_specs=[in_vmem] * 2,
+        in_specs=[in_vmem] * (len(near) + 1),
         out_specs=in_vmem,
         compiler_params=pltpu.CompilerParams(vmem_limit_bytes=VMEM_LIMIT),
         name="pick_near",
-    )(near, meta)
+    )(*near, meta)
     edge_rows = -(-CHANNELS * groups // 16) * 16
     inner_rows = CHANNELS * BLK_DEV * groups
     picked, *edges = pl.pallas_call(
-        functools.partial(edge_kernel, frames_dev, max_slots, groups),
+        functools.partial(edge_kernel, frames_dev, max_slots, groups, len(far)),
         out_shape=[jax.ShapeDtypeStruct((CHANNELS * slot_count, pixel_width), jnp.float32)]
         + [jax.ShapeDtypeStruct((CHANNELS, voxels), jnp.float32)] * groups,
-        in_specs=[in_vmem] * 4,
+        in_specs=[in_vmem] * (len(far) + 3),
         out_specs=[in_vmem] * (1 + groups),
         scratch_shapes=[pltpu.VMEM((edge_rows, depth), jnp.bfloat16)],
         compiler_params=pltpu.CompilerParams(vmem_limit_bytes=VMEM_LIMIT),
@@ -275,7 +285,7 @@
             flops=2 * edge_rows * depth * voxels, bytes_accessed=2 * depth * voxels, transcendentals=0
         ),
         name="edges",
-    )(early, far, meta, split)
+    )(early, *far, meta, split)
     blocks = pl.pallas_call(
         functools.partial(inner_kernel, frames_dev, max_slots, groups),
         out_shape=[jax.ShapeDtypeStruct((CHANNELS * BLK_DEV, voxels), jnp.float32)] * groups,

time: 23.9 us -> 23.7 us (level)
  waiting for transfers between devices: 7.85 us -> 5.43 us
  starting transfers between devices: 11.6 us -> 13.8 us
    ppermute x7 -> x8, waiting for transfers between devices: 3.58 us -> 1.16 us  [swap(): lax.ppermute(rows, 'brick', [(i, i ^ (odd if i % 2 else even)) for i in r...]
    ppermute x7 -> x8, starting transfers between devices: 9.46 us -> 11.6 us  [swap(): lax.ppermute(rows, 'brick', [(i, i ^ (odd if i % 2 else even)) for i in r...]
  transfers between devices with their start and end apart: 10 -> 11, of which waited for: 8 -> 6; matrix products, arithmetic and copies ran while one was open for 4% -> 4% of each run, Pallas kernels for 5% -> 6%
where the time goes in v7:
time: 23.7 us; the launch traced here: 23.5 us
  starting transfers between devices  13.8 us (58%)
  waiting for transfers between devices  5.43 us (23%)
  Pallas kernels  2.75 us (12%)
  other arithmetic  0.85 us (4%)
  between operations  0.71 us (3%)
    ppermute x8, starting transfers between devices, swap(): lax.ppermute(rows, 'brick', [(i, i ^ (odd if i % 2 else even)) for i in r...  11.6 us
    ppermute x1, waiting for transfers between devices, on_device(): handed = lax.ppermute(overhang, ('frame', 'brick'), turn)  3.6 us
    ppermute x2, starting transfers between devices, to_owner(): lax.ppermute(parts[step], 'frame', [(i, (i + step) % groups) for i in ran...  2.11 us
    ppermute x8, waiting for transfers between devices, swap(): lax.ppermute(rows, 'brick', [(i, i ^ (odd if i % 2 else even)) for i in r...  1.16 us
    pallas_call x1, Pallas kernels, on_device(): pl.pallas_call(functools.partial(inner_kernel, frames_dev, max_slots, gro...  0.85 us
    convert_element_type x1, other arithmetic, on_device(): local_rows = local_rows.astype(jnp.bfloat16)  0.78 us
    pallas_call x1, Pallas kernels, on_device(): pl.pallas_call(functools.partial(edge_kernel, frames_dev, max_slots, grou...  0.76 us
    ppermute x2, waiting for transfers between devices, to_owner(): lax.ppermute(parts[step], 'frame', [(i, (i + step) % groups) for i in ran...  0.66 us
  transfers between devices with their start and end apart: 11, of which 6 were waited for; matrix products, arithmetic and copies ran while one was open for 4% of the time, Pallas kernels for 6%

profile of v7, /device:TPU:0, one launch (start us, length us, event | category | flops | bytes accessed | tf_op | source)
XLA Modules:
  0.0 23.5 jit_solution(4761959123218655882)
XLA Ops:
  0.6 0.5 %collective-permute-start = (f32[64,128]{1,0:T(8,128)}, f32[64,128]{1,0:T(8,128)S(1)}, u32[]{:S(2)}, u32[]{:S(2)}) collective-permute-start(f32[64,128]{1,0:T(8,128)} %bitcast.10), channel_id=1, source_target_pairs={{0,1},{1,0},{2,3},{3,2},{4,5},{5,4},{6,7},{7,6},{8,9},{9,8},{10,11... | collective-permute-start | bytes 98312 | tf_op jit(solution)/shard_map/ppermute | solution.py:44
  1.1 0.1 collective-permute-start.1
  1.2 0.8 %add_convert_fusion.own_ref = bf16[128,128]{1,0:T(8,128)(2,1)S(1)} fusion(f32[64,128]{1,0:T(8,128)} %bitcast.13, f32[64,128]{1,0:T(8,128)} %bitcast.11), kind=kLoop, calls=%fused_computation | loop fusion | flops 32768 | bytes 98304 | tf_op jit(solution)/shard_map/convert_element_type | solution.py:243
  2.0 0.2 collective-permute-done.refs_0_
  2.2 0.3 %collective-permute-done.1.refs_1_ = f32[64,128]{1,0:T(8,128)S(1)} collective-permute-done((f32[64,128]{1,0:T(8,128)}, f32[64,128]{1,0:T(8,128)S(1)}, u32[]{:S(2)}, u32[]{:S(2)}) %collective-permute-start.1) | collective-permute-done | bytes 32800 | tf_op jit(solution)/shard_map/ppermute | solution.py:44
  2.6 2.7 %collective-permute-start.2 = (bf16[2,128,128]{2,1,0:T(8,128)(2,1)S(1)}, bf16[2,128,128]{2,1,0:T(8,128)(2,1)S(1)}, u32[]{:S(2)}, u32[]{:S(2)}) collective-permute-start(bf16[2,128,128]{2,1,0:T(8,128)(2,1)S(1)} %pair_rows.1.refs_2_), channel_id=1, source_target_pairs={{0,2},{1,9},{2,0},{3,11},{4,6},{5,13},{6,4},{7,15},{8,10},{9,1},{1... | collective-permute-start | bytes 196616 | tf_op jit(solution)/shard_map/ppermute | solution.py:44
  5.3 1.6 %collective-permute-start.3 = (bf16[2,128,128]{2,1,0:T(8,128)(2,1)S(1)}, bf16[2,128,128]{2,1,0:T(8,128)(2,1)S(1)}, u32[]{:S(2)}, u32[]{:S(2)}) collective-permute-start(bf16[2,128,128]{2,1,0:T(8,128)(2,1)S(1)} %pair_rows.1.refs_2_), channel_id=1, source_target_pairs={{0,4},{1,15},{2,6},{3,13},{4,0},{5,11},{6,2},{7,9},{8,12},{9,7},{1... | collective-permute-start | bytes 196616 | tf_op jit(solution)/shard_map/ppermute | solution.py:44
  6.9 0.5 %collective-permute-start.4 = (bf16[2,128,128]{2,1,0:T(8,128)(2,1)S(1)}, bf16[2,128,128]{2,1,0:T(8,128)(2,1)S(1)}, u32[]{:S(2)}, u32[]{:S(2)}) collective-permute-start(bf16[2,128,128]{2,1,0:T(8,128)(2,1)S(1)} %pair_rows.1.refs_2_), channel_id=1, source_target_pairs={{0,2},{1,13},{2,0},{3,15},{4,6},{5,9},{6,4},{7,11},{8,10},{9,5},{1... | collective-permute-start | bytes 196616 | tf_op jit(solution)/shard_map/ppermute | solution.py:44
  7.4 0.2 collective-permute-done.2.refs_0_
  7.5 2.1 %collective-permute-start.5 = (bf16[2,128,128]{2,1,0:T(8,128)(2,1)S(1)}, bf16[2,128,128]{2,1,0:T(8,128)(2,1)S(1)}, u32[]{:S(2)}, u32[]{:S(2)}) collective-permute-start(bf16[2,128,128]{2,1,0:T(8,128)(2,1)S(1)} %collective-permute-done.2.refs_0_), channel_id=1, source_target_pairs={{0,4},{1,3},{2,6},{3,1},{4,0},{5,7},{6,2},{7,5},{8,12},{9,11},{10,... | collective-permute-start | bytes 196616 | tf_op jit(solution)/shard_map/ppermute | solution.py:44
  9.6 0.0 collective-permute-done.3.refs_1_
  9.6 0.0 copy-start.1
  9.6 0.0 copy-start.2
  9.7 0.0 copy-start.3
  9.7 0.0 copy-start
  9.7 2.8 %collective-permute-start.6 = (bf16[4,128,128]{2,1,0:T(8,128)(2,1)S(1)}, bf16[4,128,128]{2,1,0:T(8,128)(2,1)S(1)}, u32[]{:S(2)}, u32[]{:S(2)}) collective-permute-start(bf16[4,128,128]{2,1,0:T(8,128)(2,1)S(1)} %join_rows.2.refs_0_), channel_id=1, source_target_pairs={{0,1},{1,0},{2,3},{3,2},{4,5},{5,4},{6,7},{7,6},{8,9},{9,8},{10,11... | collective-permute-start | bytes 393224 | tf_op jit(solution)/shard_map/ppermute | solution.py:44
  12.5 0.0 collective-permute-done.4.refs_0_
  12.5 0.0 collective-permute-done.5.refs_1_
  12.5 1.3 %collective-permute-start.7 = (bf16[4,128,128]{2,1,0:T(8,128)(2,1)S(1)}, bf16[4,128,128]{2,1,0:T(8,128)(2,1)S(1)}, u32[]{:S(2)}, u32[]{:S(2)}) collective-permute-start(bf16[4,128,128]{2,1,0:T(8,128)(2,1)S(1)} %join_rows.3.refs_1_), channel_id=1, source_target_pairs={{0,1},{1,0},{2,3},{3,2},{4,5},{5,4},{6,7},{7,6},{8,9},{9,8},{10,11... | collective-permute-start | bytes 393224 | tf_op jit(solution)/shard_map/ppermute | solution.py:44
  13.9 0.1 fusion
  14.0 0.3 %prepare.1.refs_2_.meta_ref = s32[128,128]{1,0:T(8,128)S(1)} custom-call(s32[4,8]{1,0:T(4,128)S(1)} %bitcast.9), custom_call_target="tpu_custom_call" | custom-call | tf_op jit(solution)/shard_map/prepare/pallas_call | solution.py:255
  14.3 0.2 pick_near.1.early_ref
  14.4 0.0 collective-permute-done.6.refs_0_
  14.4 0.4 %collective-permute-done.7.refs_1_ = bf16[4,128,128]{2,1,0:T(8,128)(2,1)S(1)} collective-permute-done((bf16[4,128,128]{2,1,0:T(8,128)(2,1)S(1)}, bf16[4,128,128]{2,1,0:T(8,128)(2,1)S(1)}, u32[]{:S(2)}, u32[]{:S(2)}) %collective-permute-start.7) | collective-permute-done | bytes 131104 | tf_op jit(solution)/shard_map/ppermute | solution.py:44
  14.9 0.8 %edges.1 = (f32[64,128]{1,0:T(8,128)S(1)}, f32[2,512]{1,0:T(2,128)S(1)}, f32[2,512]{1,0:T(2,128)S(1)}) custom-call(f32[64,128]{1,0:T(8,128)S(1)} %pick_near.1.early_ref, bf16[4,128,128]{2,1,0:T(8,128)(2,1)S(1)} %collective-permute-done.6.refs_0_, bf16[4,128,128]{2,1,0:T(8,128)(2,1)S(1)} %collective-permute-done.7.refs_1_, ...), custom_call_target="tpu_custom_call" | custom-call | flops 67108864 | bytes 4194304 | tf_op jit(solution)/shard_map/edges/pallas_call | solution.py:276
  15.6 1.8 %collective-permute-start.8 = (f32[2,512]{1,0:T(2,128)S(1)}, f32[2,512]{1,0:T(2,128)S(1)}, u32[]{:S(2)}, u32[]{:S(2)}) collective-permute-start(f32[2,512]{1,0:T(2,128)S(1)} %get-tuple-element.18), channel_id=1, source_target_pairs={{0,16},{16,0},{1,17},{17,1},{2,18},{18,2},{3,19},{19,3},{4,20},{20... | collective-permute-start | bytes 12296 | tf_op jit(solution)/shard_map/ppermute | solution.py:304
  17.4 0.8 %inner.1 = (f32[32,512]{1,0:T(8,128)S(1)}, f32[32,512]{1,0:T(8,128)S(1)}) custom-call(f32[64,128]{1,0:T(8,128)S(1)} %get-tuple-element.19.picked_ref, s32[128,128]{1,0:T(8,128)S(1)} %prepare.1.refs_2_.meta_ref, bf16[4096,512]{1,0:T(8,128)(2,1)S(1)} %bitcast.8), custom_call_target="tpu_custom_call" | custom-call | flops 268435456 | bytes 4194304 | tf_op jit(solution)/shard_map/inner/pallas_call | solution.py:289
  18.3 0.3 %collective-permute-start.10 = (f32[32,512]{1,0:T(8,128)S(1)}, f32[32,512]{1,0:T(8,128)S(1)}, u32[]{:S(2)}, u32[]{:S(2)}) collective-permute-start(f32[32,512]{1,0:T(8,128)S(1)} %get-tuple-element.21), channel_id=1, source_target_pairs={{0,16},{16,0},{1,17},{17,1},{2,18},{18,2},{3,19},{19,3},{4,20},{20... | collective-permute-start | bytes 196616 | tf_op jit(solution)/shard_map/ppermute | solution.py:304
  18.6 0.7 %collective-permute-done.8.refs_1_ = f32[2,512]{1,0:T(2,128)S(1)} collective-permute-done((f32[2,512]{1,0:T(2,128)S(1)}, f32[2,512]{1,0:T(2,128)S(1)}, u32[]{:S(2)}, u32[]{:S(2)}) %collective-permute-start.8) | collective-permute-done | bytes 4128 | tf_op jit(solution)/shard_map/ppermute | solution.py:304
  19.3 0.0 collective-permute-start.9
  19.3 3.6 %collective-permute-done.9.handed_ref = f32[2,512]{1,0:T(2,128)S(1)} collective-permute-done((f32[2,512]{1,0:T(2,128)S(1)}, f32[2,512]{1,0:T(2,128)S(1)}, u32[]{:S(2)}, u32[]{:S(2)}) %collective-permute-start.9) | collective-permute-done | bytes 4128 | tf_op jit(solution)/shard_map/ppermute | solution.py:323
  22.9 0.6 %finish.1 = (f32[16,512]{1,0:T(8,128)}, f32[16,512]{1,0:T(8,128)}) custom-call(f32[2,512]{1,0:T(2,128)S(1)} %collective-permute-done.9.handed_ref, f32[32,512]{1,0:T(8,128)S(1)} %get-tuple-element.20.refs_0_, f32[32,512]{1,0:T(8,128)S(1)} %collective-permute-done.10.refs_1_), custom_call_target="tpu_custom_call" | custom-call | tf_op jit(solution)/shard_map/finish/pallas_call | solution.py:324
  (9 shorter events, 0.0 us)
Async XLA Ops:
  0.6 1.6 %collective-permute-start = (f32[64,128]{1,0:T(8,128)}, f32[64,128]{1,0:T(8,128)S(1)}, u32[]{:S(2)}, u32[]{:S(2)}) collective-permute-start(f32[64,128]{1,0:T(8,128)} %bitcast.10), channel_id=1, source_target_pairs={{0,1},{1,0},{2,3},{3,2},{4,5},{5,4},{6,7},{7,6},{8,9},{9,8},{10,11... | collective-permute-start | bytes 98312 | tf_op jit(solution)/shard_map/ppermute | solution.py:44
  1.1 1.4 %collective-permute-start.1 = (f32[64,128]{1,0:T(8,128)}, f32[64,128]{1,0:T(8,128)S(1)}, u32[]{:S(2)}, u32[]{:S(2)}) collective-permute-start(f32[64,128]{1,0:T(8,128)} %bitcast.12), channel_id=1, source_target_pairs={{0,1},{1,0},{2,3},{3,2},{4,5},{5,4},{6,7},{7,6},{8,9},{9,8},{10,11... | collective-permute-start | bytes 98312 | tf_op jit(solution)/shard_map/ppermute | solution.py:44
  2.6 5.0 %collective-permute-start.2 = (bf16[2,128,128]{2,1,0:T(8,128)(2,1)S(1)}, bf16[2,128,128]{2,1,0:T(8,128)(2,1)S(1)}, u32[]{:S(2)}, u32[]{:S(2)}) collective-permute-start(bf16[2,128,128]{2,1,0:T(8,128)(2,1)S(1)} %pair_rows.1.refs_2_), channel_id=1, source_target_pairs={{0,2},{1,9},{2,0},{3,11},{4,6},{5,13},{6,4},{7,15},{8,10},{9,1},{1... | collective-permute-start | bytes 196616 | tf_op jit(solution)/shard_map/ppermute | solution.py:44
  5.3 4.3 %collective-permute-start.3 = (bf16[2,128,128]{2,1,0:T(8,128)(2,1)S(1)}, bf16[2,128,128]{2,1,0:T(8,128)(2,1)S(1)}, u32[]{:S(2)}, u32[]{:S(2)}) collective-permute-start(bf16[2,128,128]{2,1,0:T(8,128)(2,1)S(1)} %pair_rows.1.refs_2_), channel_id=1, source_target_pairs={{0,4},{1,15},{2,6},{3,13},{4,0},{5,11},{6,2},{7,9},{8,12},{9,7},{1... | collective-permute-start | bytes 196616 | tf_op jit(solution)/shard_map/ppermute | solution.py:44
  6.9 5.6 %collective-permute-start.4 = (bf16[2,128,128]{2,1,0:T(8,128)(2,1)S(1)}, bf16[2,128,128]{2,1,0:T(8,128)(2,1)S(1)}, u32[]{:S(2)}, u32[]{:S(2)}) collective-permute-start(bf16[2,128,128]{2,1,0:T(8,128)(2,1)S(1)} %pair_rows.1.refs_2_), channel_id=1, source_target_pairs={{0,2},{1,13},{2,0},{3,15},{4,6},{5,9},{6,4},{7,11},{8,10},{9,5},{1... | collective-permute-start | bytes 196616 | tf_op jit(solution)/shard_map/ppermute | solution.py:44
  7.5 5.0 %collective-permute-start.5 = (bf16[2,128,128]{2,1,0:T(8,128)(2,1)S(1)}, bf16[2,128,128]{2,1,0:T(8,128)(2,1)S(1)}, u32[]{:S(2)}, u32[]{:S(2)}) collective-permute-start(bf16[2,128,128]{2,1,0:T(8,128)(2,1)S(1)} %collective-permute-done.2.refs_0_), channel_id=1, source_target_pairs={{0,4},{1,3},{2,6},{3,1},{4,0},{5,7},{6,2},{7,5},{8,12},{9,11},{10,... | collective-permute-start | bytes 196616 | tf_op jit(solution)/shard_map/ppermute | solution.py:44
  9.6 4.3 %copy-start.1 = (s32[4,1,8]{2,1,0:T(1,128)S(1)}, s32[4,1,8]{2,1,0:T(1,128)}, u32[]{:S(2)}) copy-start(s32[4,1,8]{2,1,0:T(1,128)} %param.11) | copy-start | bytes 388
  9.6 4.2 %copy-start.2 = (s32[4,1,8]{2,1,0:T(1,128)S(1)}, s32[4,1,8]{2,1,0:T(1,128)}, u32[]{:S(2)}) copy-start(s32[4,1,8]{2,1,0:T(1,128)} %param.10) | copy-start | bytes 388
  9.7 4.2 %copy-start.3 = (s32[4,1]{0,1:T(1,128)S(1)}, s32[4,1]{0,1:T(1,128)}, u32[]{:S(2)}) copy-start(s32[4,1]{0,1:T(1,128)} %param.9) | copy-start | bytes 52
  9.7 5.2 %copy-start = (bf16[4,1,8,128,512]{4,3,2,1,0:T(8,128)(2,1)S(1)}, bf16[4,1,8,128,512]{4,3,2,1,0:T(8,128)(2,1)}, u32[]{:S(2)}) copy-start(bf16[4,1,8,128,512]{4,3,2,1,0:T(8,128)(2,1)} %param.8) | copy-start | bytes 12582916
  9.7 4.8 %collective-permute-start.6 = (bf16[4,128,128]{2,1,0:T(8,128)(2,1)S(1)}, bf16[4,128,128]{2,1,0:T(8,128)(2,1)S(1)}, u32[]{:S(2)}, u32[]{:S(2)}) collective-permute-start(bf16[4,128,128]{2,1,0:T(8,128)(2,1)S(1)} %join_rows.2.refs_0_), channel_id=1, source_target_pairs={{0,1},{1,0},{2,3},{3,2},{4,5},{5,4},{6,7},{7,6},{8,9},{9,8},{10,11... | collective-permute-start | bytes 393224 | tf_op jit(solution)/shard_map/ppermute | solution.py:44
  12.5 2.3 %collective-permute-start.7 = (bf16[4,128,128]{2,1,0:T(8,128)(2,1)S(1)}, bf16[4,128,128]{2,1,0:T(8,128)(2,1)S(1)}, u32[]{:S(2)}, u32[]{:S(2)}) collective-permute-start(bf16[4,128,128]{2,1,0:T(8,128)(2,1)S(1)} %join_rows.3.refs_1_), channel_id=1, source_target_pairs={{0,1},{1,0},{2,3},{3,2},{4,5},{5,4},{6,7},{7,6},{8,9},{9,8},{10,11... | collective-permute-start | bytes 393224 | tf_op jit(solution)/shard_map/ppermute | solution.py:44
  15.6 3.6 %collective-permute-start.8 = (f32[2,512]{1,0:T(2,128)S(1)}, f32[2,512]{1,0:T(2,128)S(1)}, u32[]{:S(2)}, u32[]{:S(2)}) collective-permute-start(f32[2,512]{1,0:T(2,128)S(1)} %get-tuple-element.18), channel_id=1, source_target_pairs={{0,16},{16,0},{1,17},{17,1},{2,18},{18,2},{3,19},{19,3},{4,20},{20... | collective-permute-start | bytes 12296 | tf_op jit(solution)/shard_map/ppermute | solution.py:304
  18.3 4.6 %collective-permute-start.10 = (f32[32,512]{1,0:T(8,128)S(1)}, f32[32,512]{1,0:T(8,128)S(1)}, u32[]{:S(2)}, u32[]{:S(2)}) collective-permute-start(f32[32,512]{1,0:T(8,128)S(1)} %get-tuple-element.21), channel_id=1, source_target_pairs={{0,16},{16,0},{1,17},{17,1},{2,18},{18,2},{3,19},{19,3},{4,20},{20... | collective-permute-start | bytes 196616 | tf_op jit(solution)/shard_map/ppermute | solution.py:304
  19.3 3.6 %collective-permute-start.9 = (f32[2,512]{1,0:T(2,128)S(1)}, f32[2,512]{1,0:T(2,128)S(1)}, u32[]{:S(2)}, u32[]{:S(2)}) collective-permute-start(f32[2,512]{1,0:T(2,128)S(1)} %sum_edges.1), channel_id=1, source_target_pairs={{0,1},{16,0},{1,2},{17,16},{2,3},{18,17},{3,4},{19,18},{4,5},{20,1... | collective-permute-start | bytes 12296 | tf_op jit(solution)/shard_map/ppermute | solution.py:323

commit v8 on v7

--- a/solution.py
+++ b/solution.py
@@ -67,11 +67,11 @@
     held = rows[None]
     if bricks == 16:
         held = pair_up(rows, [swap(part, bricks, 1, 1) for part in exact])
-        even, odd, spare = (2, 4, 2), (8, 14, 12), 2
+        even, odd, spare = (4, 2, 4), (8, 14, 12), 2
         arrived = {at: swap(held, bricks, even[at], odd[at]) for at in (0, 1, 2)}
         arrived = [arrived[at] for at in range(len(even))]
-        handed = swap(arrived[0], bricks, 4, 2)
-        even, odd = even + (even[0] ^ 4,), odd + (odd[0] ^ 2,)
+        handed = swap(arrived[0], bricks, 2, 2)
+        even, odd = even + (even[0] ^ 2,), odd + (odd[0] ^ 2,)
         of_even = [d ^ c for at, d in enumerate(even) for d in (0 if at == spare else d,) for c in (0, 1)]
         of_odd = [d ^ c for d in odd for c in (0, 1)]
         of_even, of_odd = of_even + [d ^ 1 for d in of_odd], of_odd + [d ^ 1 for d in of_even]

time: 23.7 us -> 23.7 us (level)
  starting transfers between devices: 13.8 us -> 13.1 us
  waiting for transfers between devices: 5.43 us -> 6.12 us
    ppermute x8, waiting for transfers between devices: 1.16 us -> 1.86 us  [swap(): lax.ppermute(rows, 'brick', [(i, i ^ (odd if i % 2 else even)) for i in r...]
    ppermute x8, starting transfers between devices: 11.6 us -> 11 us  [swap(): lax.ppermute(rows, 'brick', [(i, i ^ (odd if i % 2 else even)) for i in r...]
  transfers between devices with their start and end apart: 11 -> 11, of which waited for: 6 -> 7; matrix products, arithmetic and copies ran while one was open for 4% -> 4% of each run, Pallas kernels for 6% -> 6%
where the time goes in v8:
time: 23.7 us; the launch traced here: 23.5 us
  starting transfers between devices  13.1 us (55%)
  waiting for transfers between devices  6.12 us (26%)
  Pallas kernels  2.75 us (12%)
  other arithmetic  0.85 us (4%)
  between operations  0.7 us (3%)
    ppermute x8, starting transfers between devices, swap(): lax.ppermute(rows, 'brick', [(i, i ^ (odd if i % 2 else even)) for i in r...  11 us
    ppermute x1, waiting for transfers between devices, on_device(): handed = lax.ppermute(overhang, ('frame', 'brick'), turn)  3.6 us
    ppermute x2, starting transfers between devices, to_owner(): lax.ppermute(parts[step], 'frame', [(i, (i + step) % groups) for i in ran...  2.11 us
    ppermute x8, waiting for transfers between devices, swap(): lax.ppermute(rows, 'brick', [(i, i ^ (odd if i % 2 else even)) for i in r...  1.86 us
    pallas_call x1, Pallas kernels, on_device(): pl.pallas_call(functools.partial(inner_kernel, frames_dev, max_slots, gro...  0.85 us
    convert_element_type x1, other arithmetic, on_device(): local_rows = local_rows.astype(jnp.bfloat16)  0.78 us
    pallas_call x1, Pallas kernels, on_device(): pl.pallas_call(functools.partial(edge_kernel, frames_dev, max_slots, grou...  0.76 us
    ppermute x2, waiting for transfers between devices, to_owner(): lax.ppermute(parts[step], 'frame', [(i, (i + step) % groups) for i in ran...  0.66 us
  transfers between devices with their start and end apart: 11, of which 7 were waited for; matrix products, arithmetic and copies ran while one was open for 4% of the time, Pallas kernels for 6%

profile of v8, /device:TPU:0, one launch (start us, length us, event | category | flops | bytes accessed | tf_op | source)
XLA Modules:
  0.0 23.5 jit_solution(8444237311409292170)
XLA Ops:
  0.6 0.5 %collective-permute-start = (f32[64,128]{1,0:T(8,128)}, f32[64,128]{1,0:T(8,128)S(1)}, u32[]{:S(2)}, u32[]{:S(2)}) collective-permute-start(f32[64,128]{1,0:T(8,128)} %bitcast.10), channel_id=1, source_target_pairs={{0,1},{1,0},{2,3},{3,2},{4,5},{5,4},{6,7},{7,6},{8,9},{9,8},{10,11... | collective-permute-start | bytes 98312 | tf_op jit(solution)/shard_map/ppermute | solution.py:44
  1.1 0.1 collective-permute-start.1
  1.2 0.8 %add_convert_fusion.own_ref = bf16[128,128]{1,0:T(8,128)(2,1)S(1)} fusion(f32[64,128]{1,0:T(8,128)} %bitcast.13, f32[64,128]{1,0:T(8,128)} %bitcast.11), kind=kLoop, calls=%fused_computation | loop fusion | flops 32768 | bytes 98304 | tf_op jit(solution)/shard_map/convert_element_type | solution.py:243
  2.0 0.2 collective-permute-done.refs_0_
  2.2 0.3 %collective-permute-done.1.refs_1_ = f32[64,128]{1,0:T(8,128)S(1)} collective-permute-done((f32[64,128]{1,0:T(8,128)}, f32[64,128]{1,0:T(8,128)S(1)}, u32[]{:S(2)}, u32[]{:S(2)}) %collective-permute-start.1) | collective-permute-done | bytes 32800 | tf_op jit(solution)/shard_map/ppermute | solution.py:44
  2.6 2.8 %collective-permute-start.2 = (bf16[2,128,128]{2,1,0:T(8,128)(2,1)S(1)}, bf16[2,128,128]{2,1,0:T(8,128)(2,1)S(1)}, u32[]{:S(2)}, u32[]{:S(2)}) collective-permute-start(bf16[2,128,128]{2,1,0:T(8,128)(2,1)S(1)} %pair_rows.1.refs_2_), channel_id=1, source_target_pairs={{0,4},{1,9},{2,6},{3,11},{4,0},{5,13},{6,2},{7,15},{8,12},{9,1},{1... | collective-permute-start | bytes 196616 | tf_op jit(solution)/shard_map/ppermute | solution.py:44
  5.3 1.5 %collective-permute-start.3 = (bf16[2,128,128]{2,1,0:T(8,128)(2,1)S(1)}, bf16[2,128,128]{2,1,0:T(8,128)(2,1)S(1)}, u32[]{:S(2)}, u32[]{:S(2)}) collective-permute-start(bf16[2,128,128]{2,1,0:T(8,128)(2,1)S(1)} %pair_rows.1.refs_2_), channel_id=1, source_target_pairs={{0,2},{1,15},{2,0},{3,13},{4,6},{5,11},{6,4},{7,9},{8,10},{9,7},{1... | collective-permute-start | bytes 196616 | tf_op jit(solution)/shard_map/ppermute | solution.py:44
  6.9 0.4 %collective-permute-start.4 = (bf16[2,128,128]{2,1,0:T(8,128)(2,1)S(1)}, bf16[2,128,128]{2,1,0:T(8,128)(2,1)S(1)}, u32[]{:S(2)}, u32[]{:S(2)}) collective-permute-start(bf16[2,128,128]{2,1,0:T(8,128)(2,1)S(1)} %pair_rows.1.refs_2_), channel_id=1, source_target_pairs={{0,4},{1,13},{2,6},{3,15},{4,0},{5,9},{6,2},{7,11},{8,12},{9,5},{1... | collective-permute-start | bytes 196616 | tf_op jit(solution)/shard_map/ppermute | solution.py:44
  7.3 0.3 %collective-permute-done.2.refs_0_ = bf16[2,128,128]{2,1,0:T(8,128)(2,1)S(1)} collective-permute-done((bf16[2,128,128]{2,1,0:T(8,128)(2,1)S(1)}, bf16[2,128,128]{2,1,0:T(8,128)(2,1)S(1)}, u32[]{:S(2)}, u32[]{:S(2)}) %collective-permute-start.2) | collective-permute-done | bytes 65568 | tf_op jit(solution)/shard_map/ppermute | solution.py:44
  7.6 2.7 %collective-permute-start.5 = (bf16[2,128,128]{2,1,0:T(8,128)(2,1)S(1)}, bf16[2,128,128]{2,1,0:T(8,128)(2,1)S(1)}, u32[]{:S(2)}, u32[]{:S(2)}) collective-permute-start(bf16[2,128,128]{2,1,0:T(8,128)(2,1)S(1)} %collective-permute-done.2.refs_0_), channel_id=1, source_target_pairs={{0,2},{1,3},{2,0},{3,1},{4,6},{5,7},{6,4},{7,5},{8,10},{9,11},{10,... | collective-permute-start | bytes 196616 | tf_op jit(solution)/shard_map/ppermute | solution.py:44
  10.3 0.0 collective-permute-done.3.refs_1_
  10.3 0.0 copy-start.1
  10.3 0.0 copy-start.2
  10.3 0.0 copy-start.3
  10.3 0.0 copy-start
  10.3 2.3 %collective-permute-start.6 = (bf16[4,128,128]{2,1,0:T(8,128)(2,1)S(1)}, bf16[4,128,128]{2,1,0:T(8,128)(2,1)S(1)}, u32[]{:S(2)}, u32[]{:S(2)}) collective-permute-start(bf16[4,128,128]{2,1,0:T(8,128)(2,1)S(1)} %join_rows.2.refs_0_), channel_id=1, source_target_pairs={{0,1},{1,0},{2,3},{3,2},{4,5},{5,4},{6,7},{7,6},{8,9},{9,8},{10,11... | collective-permute-start | bytes 393224 | tf_op jit(solution)/shard_map/ppermute | solution.py:44
  12.6 0.0 collective-permute-done.4.refs_0_
  12.6 0.6 %collective-permute-done.5.refs_1_ = bf16[2,128,128]{2,1,0:T(8,128)(2,1)S(1)} collective-permute-done((bf16[2,128,128]{2,1,0:T(8,128)(2,1)S(1)}, bf16[2,128,128]{2,1,0:T(8,128)(2,1)S(1)}, u32[]{:S(2)}, u32[]{:S(2)}) %collective-permute-start.5) | collective-permute-done | bytes 65568 | tf_op jit(solution)/shard_map/ppermute | solution.py:44
  13.2 0.7 %collective-permute-start.7 = (bf16[4,128,128]{2,1,0:T(8,128)(2,1)S(1)}, bf16[4,128,128]{2,1,0:T(8,128)(2,1)S(1)}, u32[]{:S(2)}, u32[]{:S(2)}) collective-permute-start(bf16[4,128,128]{2,1,0:T(8,128)(2,1)S(1)} %join_rows.3.refs_1_), channel_id=1, source_target_pairs={{0,1},{1,0},{2,3},{3,2},{4,5},{5,4},{6,7},{7,6},{8,9},{9,8},{10,11... | collective-permute-start | bytes 393224 | tf_op jit(solution)/shard_map/ppermute | solution.py:44
  13.9 0.1 fusion
  14.0 0.3 %prepare.1.refs_2_.meta_ref = s32[128,128]{1,0:T(8,128)S(1)} custom-call(s32[4,8]{1,0:T(4,128)S(1)} %bitcast.9), custom_call_target="tpu_custom_call" | custom-call | tf_op jit(solution)/shard_map/prepare/pallas_call | solution.py:255
  14.3 0.2 pick_near.1.early_ref
  14.4 0.0 collective-permute-done.6.refs_0_
  14.4 0.4 %collective-permute-done.7.refs_1_ = bf16[4,128,128]{2,1,0:T(8,128)(2,1)S(1)} collective-permute-done((bf16[4,128,128]{2,1,0:T(8,128)(2,1)S(1)}, bf16[4,128,128]{2,1,0:T(8,128)(2,1)S(1)}, u32[]{:S(2)}, u32[]{:S(2)}) %collective-permute-start.7) | collective-permute-done | bytes 131104 | tf_op jit(solution)/shard_map/ppermute | solution.py:44
  14.9 0.8 %edges.1 = (f32[64,128]{1,0:T(8,128)S(1)}, f32[2,512]{1,0:T(2,128)S(1)}, f32[2,512]{1,0:T(2,128)S(1)}) custom-call(f32[64,128]{1,0:T(8,128)S(1)} %pick_near.1.early_ref, bf16[4,128,128]{2,1,0:T(8,128)(2,1)S(1)} %collective-permute-done.6.refs_0_, bf16[4,128,128]{2,1,0:T(8,128)(2,1)S(1)} %collective-permute-done.7.refs_1_, ...), custom_call_target="tpu_custom_call" | custom-call | flops 67108864 | bytes 4194304 | tf_op jit(solution)/shard_map/edges/pallas_call | solution.py:276
  15.6 1.5 %collective-permute-start.8 = (f32[2,512]{1,0:T(2,128)S(1)}, f32[2,512]{1,0:T(2,128)S(1)}, u32[]{:S(2)}, u32[]{:S(2)}) collective-permute-start(f32[2,512]{1,0:T(2,128)S(1)} %get-tuple-element.18), channel_id=1, source_target_pairs={{0,16},{16,0},{1,17},{17,1},{2,18},{18,2},{3,19},{19,3},{4,20},{20... | collective-permute-start | bytes 12296 | tf_op jit(solution)/shard_map/ppermute | solution.py:304
  17.1 0.8 %inner.1 = (f32[32,512]{1,0:T(8,128)S(1)}, f32[32,512]{1,0:T(8,128)S(1)}) custom-call(f32[64,128]{1,0:T(8,128)S(1)} %get-tuple-element.19.picked_ref, s32[128,128]{1,0:T(8,128)S(1)} %prepare.1.refs_2_.meta_ref, bf16[4096,512]{1,0:T(8,128)(2,1)S(1)} %bitcast.8), custom_call_target="tpu_custom_call" | custom-call | flops 268435456 | bytes 4194304 | tf_op jit(solution)/shard_map/inner/pallas_call | solution.py:289
  18.0 0.6 %collective-permute-start.10 = (f32[32,512]{1,0:T(8,128)S(1)}, f32[32,512]{1,0:T(8,128)S(1)}, u32[]{:S(2)}, u32[]{:S(2)}) collective-permute-start(f32[32,512]{1,0:T(8,128)S(1)} %get-tuple-element.21), channel_id=1, source_target_pairs={{0,16},{16,0},{1,17},{17,1},{2,18},{18,2},{3,19},{19,3},{4,20},{20... | collective-permute-start | bytes 196616 | tf_op jit(solution)/shard_map/ppermute | solution.py:304
  18.6 0.7 %collective-permute-done.8.refs_1_ = f32[2,512]{1,0:T(2,128)S(1)} collective-permute-done((f32[2,512]{1,0:T(2,128)S(1)}, f32[2,512]{1,0:T(2,128)S(1)}, u32[]{:S(2)}, u32[]{:S(2)}) %collective-permute-start.8) | collective-permute-done | bytes 4128 | tf_op jit(solution)/shard_map/ppermute | solution.py:304
  19.3 0.0 collective-permute-start.9
  19.3 3.6 %collective-permute-done.9.handed_ref = f32[2,512]{1,0:T(2,128)S(1)} collective-permute-done((f32[2,512]{1,0:T(2,128)S(1)}, f32[2,512]{1,0:T(2,128)S(1)}, u32[]{:S(2)}, u32[]{:S(2)}) %collective-permute-start.9) | collective-permute-done | bytes 4128 | tf_op jit(solution)/shard_map/ppermute | solution.py:323
  22.9 0.6 %finish.1 = (f32[16,512]{1,0:T(8,128)}, f32[16,512]{1,0:T(8,128)}) custom-call(f32[2,512]{1,0:T(2,128)S(1)} %collective-permute-done.9.handed_ref, f32[32,512]{1,0:T(8,128)S(1)} %get-tuple-element.20.refs_0_, f32[32,512]{1,0:T(8,128)S(1)} %collective-permute-done.10.refs_1_), custom_call_target="tpu_custom_call" | custom-call | tf_op jit(solution)/shard_map/finish/pallas_call | solution.py:324
  (9 shorter events, 0.0 us)
Async XLA Ops:
  0.6 1.6 %collective-permute-start = (f32[64,128]{1,0:T(8,128)}, f32[64,128]{1,0:T(8,128)S(1)}, u32[]{:S(2)}, u32[]{:S(2)}) collective-permute-start(f32[64,128]{1,0:T(8,128)} %bitcast.10), channel_id=1, source_target_pairs={{0,1},{1,0},{2,3},{3,2},{4,5},{5,4},{6,7},{7,6},{8,9},{9,8},{10,11... | collective-permute-start | bytes 98312 | tf_op jit(solution)/shard_map/ppermute | solution.py:44
  1.1 1.4 %collective-permute-start.1 = (f32[64,128]{1,0:T(8,128)}, f32[64,128]{1,0:T(8,128)S(1)}, u32[]{:S(2)}, u32[]{:S(2)}) collective-permute-start(f32[64,128]{1,0:T(8,128)} %bitcast.12), channel_id=1, source_target_pairs={{0,1},{1,0},{2,3},{3,2},{4,5},{5,4},{6,7},{7,6},{8,9},{9,8},{10,11... | collective-permute-start | bytes 98312 | tf_op jit(solution)/shard_map/ppermute | solution.py:44
  2.6 5.0 %collective-permute-start.2 = (bf16[2,128,128]{2,1,0:T(8,128)(2,1)S(1)}, bf16[2,128,128]{2,1,0:T(8,128)(2,1)S(1)}, u32[]{:S(2)}, u32[]{:S(2)}) collective-permute-start(bf16[2,128,128]{2,1,0:T(8,128)(2,1)S(1)} %pair_rows.1.refs_2_), channel_id=1, source_target_pairs={{0,4},{1,9},{2,6},{3,11},{4,0},{5,13},{6,2},{7,15},{8,12},{9,1},{1... | collective-permute-start | bytes 196616 | tf_op jit(solution)/shard_map/ppermute | solution.py:44
  5.3 4.9 %collective-permute-start.3 = (bf16[2,128,128]{2,1,0:T(8,128)(2,1)S(1)}, bf16[2,128,128]{2,1,0:T(8,128)(2,1)S(1)}, u32[]{:S(2)}, u32[]{:S(2)}) collective-permute-start(bf16[2,128,128]{2,1,0:T(8,128)(2,1)S(1)} %pair_rows.1.refs_2_), channel_id=1, source_target_pairs={{0,2},{1,15},{2,0},{3,13},{4,6},{5,11},{6,4},{7,9},{8,10},{9,7},{1... | collective-permute-start | bytes 196616 | tf_op jit(solution)/shard_map/ppermute | solution.py:44
  6.9 5.7 %collective-permute-start.4 = (bf16[2,128,128]{2,1,0:T(8,128)(2,1)S(1)}, bf16[2,128,128]{2,1,0:T(8,128)(2,1)S(1)}, u32[]{:S(2)}, u32[]{:S(2)}) collective-permute-start(bf16[2,128,128]{2,1,0:T(8,128)(2,1)S(1)} %pair_rows.1.refs_2_), channel_id=1, source_target_pairs={{0,4},{1,13},{2,6},{3,15},{4,0},{5,9},{6,2},{7,11},{8,12},{9,5},{1... | collective-permute-start | bytes 196616 | tf_op jit(solution)/shard_map/ppermute | solution.py:44
  7.6 5.6 %collective-permute-start.5 = (bf16[2,128,128]{2,1,0:T(8,128)(2,1)S(1)}, bf16[2,128,128]{2,1,0:T(8,128)(2,1)S(1)}, u32[]{:S(2)}, u32[]{:S(2)}) collective-permute-start(bf16[2,128,128]{2,1,0:T(8,128)(2,1)S(1)} %collective-permute-done.2.refs_0_), channel_id=1, source_target_pairs={{0,2},{1,3},{2,0},{3,1},{4,6},{5,7},{6,4},{7,5},{8,10},{9,11},{10,... | collective-permute-start | bytes 196616 | tf_op jit(solution)/shard_map/ppermute | solution.py:44
  10.3 3.6 %copy-start.1 = (s32[4,1,8]{2,1,0:T(1,128)S(1)}, s32[4,1,8]{2,1,0:T(1,128)}, u32[]{:S(2)}) copy-start(s32[4,1,8]{2,1,0:T(1,128)} %param.11) | copy-start | bytes 388
  10.3 3.6 %copy-start.2 = (s32[4,1,8]{2,1,0:T(1,128)S(1)}, s32[4,1,8]{2,1,0:T(1,128)}, u32[]{:S(2)}) copy-start(s32[4,1,8]{2,1,0:T(1,128)} %param.10) | copy-start | bytes 388
  10.3 3.6 %copy-start.3 = (s32[4,1]{0,1:T(1,128)S(1)}, s32[4,1]{0,1:T(1,128)}, u32[]{:S(2)}) copy-start(s32[4,1]{0,1:T(1,128)} %param.9) | copy-start | bytes 52
  10.3 4.6 %copy-start = (bf16[4,1,8,128,512]{4,3,2,1,0:T(8,128)(2,1)S(1)}, bf16[4,1,8,128,512]{4,3,2,1,0:T(8,128)(2,1)}, u32[]{:S(2)}) copy-start(bf16[4,1,8,128,512]{4,3,2,1,0:T(8,128)(2,1)} %param.8) | copy-start | bytes 12582916
  10.3 4.1 %collective-permute-start.6 = (bf16[4,128,128]{2,1,0:T(8,128)(2,1)S(1)}, bf16[4,128,128]{2,1,0:T(8,128)(2,1)S(1)}, u32[]{:S(2)}, u32[]{:S(2)}) collective-permute-start(bf16[4,128,128]{2,1,0:T(8,128)(2,1)S(1)} %join_rows.2.refs_0_), channel_id=1, source_target_pairs={{0,1},{1,0},{2,3},{3,2},{4,5},{5,4},{6,7},{7,6},{8,9},{9,8},{10,11... | collective-permute-start | bytes 393224 | tf_op jit(solution)/shard_map/ppermute | solution.py:44
  13.2 1.7 %collective-permute-start.7 = (bf16[4,128,128]{2,1,0:T(8,128)(2,1)S(1)}, bf16[4,128,128]{2,1,0:T(8,128)(2,1)S(1)}, u32[]{:S(2)}, u32[]{:S(2)}) collective-permute-start(bf16[4,128,128]{2,1,0:T(8,128)(2,1)S(1)} %join_rows.3.refs_1_), channel_id=1, source_target_pairs={{0,1},{1,0},{2,3},{3,2},{4,5},{5,4},{6,7},{7,6},{8,9},{9,8},{10,11... | collective-permute-start | bytes 393224 | tf_op jit(solution)/shard_map/ppermute | solution.py:44
  15.6 3.6 %collective-permute-start.8 = (f32[2,512]{1,0:T(2,128)S(1)}, f32[2,512]{1,0:T(2,128)S(1)}, u32[]{:S(2)}, u32[]{:S(2)}) collective-permute-start(f32[2,512]{1,0:T(2,128)S(1)} %get-tuple-element.18), channel_id=1, source_target_pairs={{0,16},{16,0},{1,17},{17,1},{2,18},{18,2},{3,19},{19,3},{4,20},{20... | collective-permute-start | bytes 12296 | tf_op jit(solution)/shard_map/ppermute | solution.py:304
  18.0 4.9 %collective-permute-start.10 = (f32[32,512]{1,0:T(8,128)S(1)}, f32[32,512]{1,0:T(8,128)S(1)}, u32[]{:S(2)}, u32[]{:S(2)}) collective-permute-start(f32[32,512]{1,0:T(8,128)S(1)} %get-tuple-element.21), channel_id=1, source_target_pairs={{0,16},{16,0},{1,17},{17,1},{2,18},{18,2},{3,19},{19,3},{4,20},{20... | collective-permute-start | bytes 196616 | tf_op jit(solution)/shard_map/ppermute | solution.py:304
  19.3 3.6 %collective-permute-start.9 = (f32[2,512]{1,0:T(2,128)S(1)}, f32[2,512]{1,0:T(2,128)S(1)}, u32[]{:S(2)}, u32[]{:S(2)}) collective-permute-start(f32[2,512]{1,0:T(2,128)S(1)} %sum_edges.1), channel_id=1, source_target_pairs={{0,1},{16,0},{1,2},{17,16},{2,3},{18,17},{3,4},{19,18},{4,5},{20,1... | collective-permute-start | bytes 12296 | tf_op jit(solution)/shard_map/ppermute | solution.py:323
